TPU v7x, 256 devices: a whole 4x4x8 slice. The times are simulated.
256 devices in a mesh: seq: 64 (over z_hi, x, y), grp: 4 (over z_lo, core).
Axes of the slice: x: 4, y: 4, z: 8 (z_hi: 4, z_lo: 2; z = z_hi * 2 + z_lo), core: 2. Of those that a mesh axis runs over, the one named last changes fastest.
Arguments:
- block_query_rows: bfloat16 [4096, 8192], P(('seq', 'grp')), may hold values from -400 to 400
- block_key_rows: bfloat16 [4096, 1024], P(('seq', 'grp')), may hold values from -6 to 6
- block_value_rows: bfloat16 [4096, 1024], P(('seq', 'grp')), may hold values from -6 to 6
- stretch_pos: int32 [4096], replicated, may hold values from 0 to 4095, each once
- prompt_key_cache: bfloat16 [8192, 1024], P(('seq', 'grp')), may hold values from -6 to 6
- prompt_value_cache: bfloat16 [8192, 1024], P(('seq', 'grp')), may hold values from -6 to 6
- embed_table: bfloat16 [65536, 8192], P('grp', 'seq'), may hold values from -6 to 6
- query_weight: bfloat16 [8192, 8192], P('seq', 'grp'), may hold values from -64 to 64
- key_weight: bfloat16 [8192, 1024], P('seq', 'grp'), may hold values from -0.0625 to 0.0625
- value_weight: bfloat16 [8192, 1024], P('seq', 'grp'), may hold values from -0.0625 to 0.0625
- beam_tokens: int32 [128, 2], replicated, may hold values from 0 to 65535
- parent_beam: int32 [128], replicated, may hold values from 0 to 127
Outputs:
- stretch_attn: bfloat16 [4096, 8192], P('seq', 'grp')
- decode_attn: bfloat16 [128, 2, 8192], P('seq', None, 'grp')
Inputs may be any that keep to these rules, and one draw needn't show every extreme that they name: `stretch_pos`: a permutation of 0 to 4095.
All inputs are finite; a program needn't handle non-finite values.
Results may differ from a plain program's by a relative error of at most 0.01155.
Values may be sent and summed in bfloat16 or wider, within the bound.
No kernel may reach another device: no remote copies, remote signals or barrier semaphores. Data moves between devices by JAX's collectives and lax.ppermute only.
A program may use at most 192 MiB of HBM per device.

v0:
```python
import jax
import jax.numpy as jnp
from jax import lax
from jax.sharding import PartitionSpec as P

QUERY_HEADS = 64
KEY_VALUE_HEADS = 8
HEAD_SIZE = 128


def softmax_absorb(carry, query_rows, keys, values, allowed):
    top, total, acc = carry
    scores = jnp.einsum(
        "tkgd,nkd->tkgn", query_rows, keys, preferred_element_type=jnp.float32
    ) * query_rows.shape[-1] ** (-0.5)
    scores = jnp.where(allowed[:, None, None, :], scores, -1e30)
    peak = jnp.maximum(top, jnp.max(scores, axis=-1))
    weights = jnp.exp(scores - peak[..., None])
    total = jnp.sum(weights, axis=-1)
    acc = jnp.einsum(
        "tkgn,nkd->tkgd", weights.astype(jnp.bfloat16), values, preferred_element_type=jnp.float32
    )
    return (peak, total, acc)


def shards(
    block_query_rows,
    block_key_rows,
    block_value_rows,
    stretch_pos,
    prompt_key_cache,
    prompt_value_cache,
    embed_table,
    query_weight,
    key_weight,
    value_weight,
    beam_tokens,
    parent_beam,
):
    query_rows, keys_new, values_new, keys_old, values_old = (
        lax.all_to_all(block_query_rows, "grp", split_axis=1, concat_axis=0, tiled=True),
        lax.all_to_all(block_key_rows, "grp", split_axis=1, concat_axis=0, tiled=True),
        lax.all_to_all(block_value_rows, "grp", split_axis=1, concat_axis=0, tiled=True),
        lax.all_to_all(prompt_key_cache, "grp", split_axis=1, concat_axis=0, tiled=True),
        lax.all_to_all(prompt_value_cache, "grp", split_axis=1, concat_axis=0, tiled=True),
    )
    row_count = query_rows.shape[0]
    kv_local = keys_new.shape[1] // HEAD_SIZE
    query_group = QUERY_HEADS // KEY_VALUE_HEADS
    context_keys = jnp.concatenate([keys_old, keys_new], 0)
    context_values = jnp.concatenate([values_old, values_new], 0)
    span = context_keys.shape[0]
    prefix_rows = keys_old.shape[0]
    shard = lax.axis_index("seq")
    query_pos = lax.dynamic_slice_in_dim(stretch_pos, shard * row_count, row_count, 0)
    grouped = query_rows.reshape(row_count, kv_local, query_group, HEAD_SIZE)
    last_pos = stretch_pos.shape[0] - 1
    start_top = jnp.full((row_count, kv_local, query_group), -1e30, jnp.float32)
    start_total = jnp.zeros((row_count, kv_local, query_group), jnp.float32)
    start_acc = jnp.zeros((row_count, kv_local, query_group, HEAD_SIZE), jnp.float32)
    piece_keys = lax.all_gather(context_keys, "seq", axis=0, tiled=True)
    piece_values = lax.all_gather(context_values, "seq", axis=0, tiled=True)
    count = piece_keys.shape[0]
    index = jnp.arange(count, dtype=jnp.int32)
    owner = index // span
    offset = index % span
    late = offset >= prefix_rows
    where_pos = jnp.clip(owner * row_count + offset - prefix_rows, 0, last_pos)
    key_pos = jnp.take(stretch_pos, where_pos)
    allowed = jnp.logical_or(jnp.logical_not(late)[None, :], key_pos[None, :] <= query_pos[:, None])
    top, total, acc = softmax_absorb(
        (start_top, start_total, start_acc),
        grouped,
        piece_keys.reshape(count, kv_local, HEAD_SIZE),
        piece_values.reshape(count, kv_local, HEAD_SIZE),
        allowed,
    )
    stretch_attn = (
        (acc / total[..., None])
        .reshape(row_count, kv_local * query_group * HEAD_SIZE)
        .astype(jnp.bfloat16)
    )
    vocab_rows = embed_table.shape[0]
    local_ids = beam_tokens - lax.axis_index("grp") * vocab_rows
    inside = jnp.logical_and(local_ids >= 0, local_ids < vocab_rows)
    looked = jnp.take(embed_table, jnp.clip(local_ids, 0, vocab_rows - 1), axis=0)
    partial_rows = jnp.where(inside[..., None], looked.astype(jnp.float32), 0.0)
    hidden_state = lax.psum(partial_rows.astype(jnp.bfloat16), "grp")
    weights = jnp.concatenate([query_weight, key_weight, value_weight], 1)
    beams = hidden_state.shape[0]
    share = beams // lax.axis_size("seq")
    mine = lax.psum_scatter(
        jnp.einsum("bsd,dc->bsc", hidden_state, weights, preferred_element_type=jnp.float32),
        "seq",
        scatter_dimension=0,
        tiled=True,
    ).astype(jnp.bfloat16)
    allrows = lax.all_gather(mine, "seq", axis=0, tiled=True)
    qwidth = query_weight.shape[1]
    kwidth = key_weight.shape[1]
    scale = HEAD_SIZE ** (-0.5)
    beam_query_rows = allrows[..., :qwidth].reshape(beams, 2, kv_local, query_group, HEAD_SIZE)
    scores = (
        jnp.einsum(
            "bskgd,nkd->bskgn",
            beam_query_rows,
            context_keys.reshape(span, kv_local, HEAD_SIZE),
            preferred_element_type=jnp.float32,
        )
        * scale
    )
    local_top = jnp.max(scores, axis=-1)
    local_weights = jnp.exp(scores - local_top[..., None])
    local_total = jnp.sum(local_weights, axis=-1)
    local_acc = jnp.einsum(
        "bskgn,nkd->bskgd",
        local_weights.astype(jnp.bfloat16),
        context_values.reshape(span, kv_local, HEAD_SIZE),
        preferred_element_type=jnp.float32,
    )
    begin = shard * share
    peak = lax.pmax(local_top, "seq")
    factor = jnp.exp(local_top - peak)
    acc_sum, total_sum = (
        lax.psum_scatter(local_acc * factor[..., None], "seq", scatter_dimension=0, tiled=True),
        lax.psum_scatter(local_total * factor, "seq", scatter_dimension=0, tiled=True),
    )
    own_peak = lax.dynamic_slice_in_dim(peak, begin, share, 0)
    own = lax.dynamic_slice_in_dim(allrows, begin, share, 0)
    own_query = own[..., :qwidth].reshape(share, 2, kv_local, query_group, HEAD_SIZE)
    new_keys = own[..., qwidth : qwidth + kwidth]
    new_values = own[..., qwidth + kwidth :]
    parents = lax.dynamic_slice_in_dim(parent_beam, begin, share, 0)
    parent_key = jnp.take(allrows[:, 0, qwidth : qwidth + kwidth], parents, axis=0)
    parent_value = jnp.take(allrows[:, 0, qwidth + kwidth :], parents, axis=0)
    first_keys = jnp.stack([new_keys[:, 0], parent_key], 1)
    first_values = jnp.stack([new_values[:, 0], parent_value], 1)
    extra_keys = jnp.stack([first_keys, new_keys], 2).reshape(share, 2, 2, kv_local, HEAD_SIZE)
    extra_values = jnp.stack([first_values, new_values], 2).reshape(
        share, 2, 2, kv_local, HEAD_SIZE
    )
    valid = jnp.arange(2)[:, None] >= jnp.arange(2)[None, :]
    own_scores = (
        jnp.einsum("bskgd,bsjkd->bskgj", own_query, extra_keys, preferred_element_type=jnp.float32)
        * scale
    )
    own_scores = jnp.where(valid[None, :, None, None, :], own_scores, -1e30)
    high = jnp.maximum(own_peak, jnp.max(own_scores, axis=-1))
    keep = jnp.exp(own_peak - high)
    own_weights = jnp.exp(own_scores - high[..., None])
    final_total = total_sum * keep + jnp.sum(own_weights, axis=-1)
    final_acc = acc_sum * keep[..., None] + jnp.einsum(
        "bskgj,bsjkd->bskgd",
        own_weights.astype(jnp.bfloat16),
        extra_values,
        preferred_element_type=jnp.float32,
    )
    decode_attn = (
        (final_acc / final_total[..., None])
        .reshape(share, 2, kv_local * query_group * HEAD_SIZE)
        .astype(jnp.bfloat16)
    )
    return (stretch_attn, decode_attn)


def solution(mesh):
    return jax.shard_map(
        shards,
        mesh=mesh,
        in_specs=(
            P(("seq", "grp"), None),
            P(("seq", "grp"), None),
            P(("seq", "grp"), None),
            P(),
            P(("seq", "grp"), None),
            P(("seq", "grp"), None),
            P("grp", "seq"),
            P("seq", "grp"),
            P("seq", "grp"),
            P("seq", "grp"),
            P(),
            P(),
        ),
        out_specs=(P("seq", "grp"), P("seq", None, "grp")),
        check_vma=False,
    )
```

profile of v0, /device:TPU:1, one launch (start us, length us, event | category | flops | bytes accessed | tf_op | source)
XLA Modules:
  0.0 1545.6 jit_solution(8929892708554026243)
XLA Ops:
  7.2 0.7 compare_and_fusion.1
  8.2 3.5 gather_fusion.1
  11.7 0.8 select_convert_fusion
  12.5 1.3 dynamic-slice
  14.5 42.4 %all-reduce.5.cloned.1.call-done = bf16[128,2,128]{2,0,1:T(8,128)(2,1)} async-done(((bf16[128,2,128]{2,0,1:T(8,128)(2,1)}), bf16[128,2,128]{2,0,1:T(8,128)(2,1)}) %all-reduce.5.cloned.1.call-update) | async-done | bytes 65552 | tf_op jit(solution)/shard_map/psum | solution.py:88
  56.9 1.6 fusion.26
  58.6 358.6 %all-reduce.6 = bf16[128,2,2560]{2,0,1:T(8,128)(2,1)} all-reduce(f32[128,2,2560]{2,0,1:T(8,128)S(1)} %fusion.26), channel_id=2, replica_groups=mesh['seq'=64,'grp'=4] {'seq'}, use_global_device_ids=true, to_apply=%region_3.4.clone | all-reduce | flops 655360 | bytes 3932160
  417.1 0.9 dynamic-slice_convert_fusion
  418.0 0.6 copy.149
  418.7 0.6 copy.211
  419.3 59.0 %all-to-all-start.3 = ((bf16[16,4,256]{2,0,1:T(8,128)(2,1)}), bf16[16,4,256]{2,0,1:T(8,128)(2,1)S(1)}, u32[]{:S(2)}, u32[]{:S(2)}) async-start(bf16[16,4,256]{2,0,1:T(8,128)(2,1)} %bitcast.116), calls=%async_computation.3 | async-start | bytes 65536 | tf_op jit(solution)/shard_map/all_to_all | solution.py:42
  478.3 0.6 copy.212
  478.9 2.6 all-to-all-done.3
  481.5 4.0 all-to-all-start.1
  485.5 0.6 copy.209
  486.1 2.9 all-to-all-done.1
  489.0 3.7 all-to-all-start.2
  492.7 0.6 copy.210
  493.3 3.0 all-to-all-done.2
  496.4 3.7 all-to-all-start
  500.2 3.1 all-to-all-done
  503.4 40.0 %all-gather.8.cloned.1.call-done = bf16[128,2,2560]{2,1,0:T(2,128)(2,1)} async-done(((bf16[2,2,2560]{2,1,0:T(2,128)(2,1)}), bf16[128,2,2560]{2,1,0:T(2,128)(2,1)}) %all-gather.8.cloned.1.call-update) | async-done | bytes 1310736 | tf_op jit(solution)/shard_map/all_gather | solution.py:98
  543.4 1.9 slice.42
  545.3 2.1 copy.178
  547.4 1.8 bitcast_reduce_fusion
  549.2 320.6 %pmax.7 = f32[128,2,2,8]{0,3,1,2:T(8,128)S(1)} all-reduce(f32[128,2,2,8]{0,3,1,2:T(8,128)S(1)} %get-tuple-element.22), channel_id=1, replica_groups=mesh['seq'=64,'grp'=4] {'seq'}, use_global_device_ids=true, to_apply=%region_5.6 | all-reduce | flops 4096 | bytes 32768 | tf_op jit(solution)/shard_map/pmax | solution.py:122
  870.4 2.1 bitcast_multiply_fusion
  872.6 3.1 copy.152
  875.8 0.6 pad_maximum_fusion.1
  876.4 0.7 copy.208
  877.2 60.0 %all-to-all-start.4 = ((bf16[16,4,2048]{2,0,1:T(8,128)(2,1)}), bf16[16,4,2048]{2,0,1:T(8,128)(2,1)S(1)}, u32[]{:S(2)}, u32[]{:S(2)}) async-start(bf16[16,4,2048]{2,0,1:T(8,128)(2,1)} %bitcast.113), calls=%async_computation.4 | async-start | bytes 524288 | tf_op jit(solution)/shard_map/all_to_all | solution.py:41
  937.6 68.0 %gather_fusion = s32[12288]{0:T(1024)S(1)} fusion(s32[4096]{0:T(1024)S(1)} %copy-done, s32[12288]{0:T(1024)S(1)} %broadcast_clamp_fusion), kind=kCustom, calls=%fused_computation.2 | custom fusion | bytes 147456 | tf_op jit(solution)/shard_map/jit(_take)/gather | solution.py:69
  1005.7 0.6 pad_maximum_fusion
  1007.2 1.2 fusion.75
  1009.6 0.7 constant_dynamic-slice_fusion.2
  1010.3 0.7 constant_dynamic-slice_fusion.1
  1011.0 0.7 dynamic-slice_bitcast_fusion
  1012.5 319.5 %all-reduce.1 = f32[128,2,2,8]{3,2,1,0:T(2,128)S(1)} all-reduce(f32[128,2,2,8]{3,2,1,0:T(2,128)S(1)} %copy.162), channel_id=4, replica_groups=mesh['seq'=64,'grp'=4] {'seq'}, use_global_device_ids=true, to_apply=%region_9.11.clone | all-reduce | flops 4096 | bytes 32768
  1332.5 1.0 fusion.22
  1333.4 0.6 convert_element_type.39
  1334.0 72.1 %all-gather.6.cloned.1.call-done = bf16[12288,256]{1,0:T(8,128)(2,1)} async-done(((bf16[192,256]{1,0:T(8,128)(2,1)}), bf16[12288,256]{1,0:T(8,128)(2,1)}) %all-gather.6.cloned.1.call-update) | async-done | bytes 6291472 | tf_op jit(solution)/shard_map/all_gather | solution.py:61
  1406.1 8.6 copy.137
  1414.7 21.5 %fusion.2 = (f32[64,2,8]{0,2,1:T(8,128)S(1)}, f32[2,12288,64,8]{1,2,3,0:T(8,128)}) fusion(pred[64,12288]{1,0:T(8,128)(4,1)S(1)} %compare_or_fusion, bf16[12288,2,128,1]{0,2,3,1:T(8,128)(2,1)} %bitcast.119, bf16[64,2,8,128]{3,2,1,0:T(8,128)(2,1)S(1)} %bitcast.133), kind=kOutput, calls=%fused_computation.8 | convolution fusion | flops 3258973184 | bytes 57675776 | tf_op jit(solution)/shard_map/tkgd,nkd->tkgn/dot_general | solution.py:13
  1436.2 22.5 %fusion = f32[64,2,8]{0,2,1:T(8,128)S(1)} fusion(f32[2,12288,64,8]{1,2,3,0:T(8,128)} %get-tuple-element.21, f32[64,2,8]{0,2,1:T(8,128)S(1)} %broadcast_maximum_fusion, pred[64,12288]{1,0:T(8,128)(4,1)S(1)} %compare_or_fusion), kind=kLoop, calls=%fused_computation.6 | loop fusion | flops 50330624 | bytes 51126272 | tf_op jit(solution)/shard_map/reduce_sum | solution.py:19
  1458.8 49.6 %all-gather.4.cloned.1.call-done = bf16[12288,256]{1,0:T(8,128)(2,1)} async-done(((bf16[192,256]{1,0:T(8,128)(2,1)}), bf16[12288,256]{1,0:T(8,128)(2,1)}) %all-gather.4.cloned.1.call-update) | async-done | bytes 6291472 | tf_op jit(solution)/shard_map/all_gather | solution.py:62
  1508.4 8.6 copy.134
  1517.0 21.1 %fusion.18 = bf16[64,2,8,128]{3,0,2,1:T(8,128)(2,1)S(1)} fusion(bf16[12288,2,128,1]{0,2,3,1:T(8,128)(2,1)} %bitcast.118, f32[2,12288,64,8]{1,2,3,0:T(8,128)} %get-tuple-element.21, f32[64,2,8]{0,2,1:T(8,128)S(1)} %broadcast_maximum_fusion, pred[64,12288]{1,0:T(8,128)(4,1)S(1)} %compare_or_fusion, f32[64,2,8]{0,2,1:T(8,128)S(1)} %fusion), kind=kOutput, calls=%fused_computation.22 | convolution fusion | flops 3271819264 | bytes 57679872 | tf_op jit(solution)/shard_map/tkgn,nkd->tkgd/dot_general | solution.py:20
  1538.3 0.8 copy.207
  (72 shorter events, 5.0 us)
Async XLA Ops:
  7.2 49.7 %all-reduce.5.cloned.1.call-start = ((), (), s32[]{:S(2)}) async-start(), calls=%async_computation.8 | async-start | bytes 131072 | tf_op jit(solution)/shard_map/psum | solution.py:88
  7.9 410.8 %copy-start.4 = (bf16[16,1024]{1,0:T(8,128)(2,1)S(1)}, bf16[16,1024]{1,0:T(8,128)(2,1)}, u32[]{:S(2)}) copy-start(bf16[16,1024]{1,0:T(8,128)(2,1)} %param.15) | copy-start | bytes 98308
  8.2 470.1 %copy-start.5 = (bf16[16,1024]{1,0:T(8,128)(2,1)S(1)}, bf16[16,1024]{1,0:T(8,128)(2,1)}, u32[]{:S(2)}) copy-start(bf16[16,1024]{1,0:T(8,128)(2,1)} %param.16) | copy-start | bytes 98308
  8.2 477.3 %copy-start.2 = (bf16[32,1024]{1,0:T(8,128)(2,1)S(1)}, bf16[32,1024]{1,0:T(8,128)(2,1)}, u32[]{:S(2)}) copy-start(bf16[32,1024]{1,0:T(8,128)(2,1)} %param.18) | copy-start | bytes 196612
  11.7 481.0 %copy-start.3 = (bf16[32,1024]{1,0:T(8,128)(2,1)S(1)}, bf16[32,1024]{1,0:T(8,128)(2,1)}, u32[]{:S(2)}) copy-start(bf16[32,1024]{1,0:T(8,128)(2,1)} %param.19) | copy-start | bytes 196612
  12.5 530.9 %all-gather.8.cloned.1.call-start = ((), (), s32[]{:S(2)}) async-start(), calls=%async_computation.9 | async-start | bytes 1331200 | tf_op jit(solution)/shard_map/all_gather | solution.py:98
  419.3 62.2 %all-to-all-start.3 = ((bf16[16,4,256]{2,0,1:T(8,128)(2,1)}), bf16[16,4,256]{2,0,1:T(8,128)(2,1)S(1)}, u32[]{:S(2)}, u32[]{:S(2)}) async-start(bf16[16,4,256]{2,0,1:T(8,128)(2,1)} %bitcast.116), calls=%async_computation.3 | async-start | bytes 65536 | tf_op jit(solution)/shard_map/all_to_all | solution.py:42
  481.5 7.5 all-to-all-start.1
  489.0 7.3 all-to-all-start.2
  496.4 7.0 all-to-all-start
  500.1 832.4 %reduce-scatter.3.cloned.1.call-start = ((), (), s32[]{:S(2)}) async-start(), calls=%async_computation.10 | async-start | bytes 2129920 | tf_op jit(solution)/shard_map/reduce_scatter | solution.py:125
  872.5 3.9 copy-start.1
  872.6 64.7 %copy-start = (s32[4096]{0:T(1024)S(1)}, s32[4096]{0:T(1024)}, u32[]{:S(2)}) copy-start(s32[4096]{0:T(1024)} %param.17) | copy-start | bytes 49156
  875.7 530.4 %all-gather.6.cloned.1.call-start = ((), (), s32[]{:S(2)}) async-start(), calls=%async_computation.7 | async-start | bytes 6389760 | tf_op jit(solution)/shard_map/all_gather | solution.py:61
  877.2 129.9 %all-to-all-start.4 = ((bf16[16,4,2048]{2,0,1:T(8,128)(2,1)}), bf16[16,4,2048]{2,0,1:T(8,128)(2,1)S(1)}, u32[]{:S(2)}, u32[]{:S(2)}) async-start(bf16[16,4,2048]{2,0,1:T(8,128)(2,1)} %bitcast.113), calls=%async_computation.4 | async-start | bytes 524288 | tf_op jit(solution)/shard_map/all_to_all | solution.py:41
  937.2 571.2 %all-gather.4.cloned.1.call-start = ((), (), s32[]{:S(2)}) async-start(), calls=%async_computation.6 | async-start | bytes 6389760 | tf_op jit(solution)/shard_map/all_gather | solution.py:62
  937.6 69.4 %copy-start.6 = (s32[128]{0:T(128)S(1)}, s32[128]{0:T(128)}, u32[]{:S(2)}) copy-start(s32[128]{0:T(128)} %param.25) | copy-start | bytes 1540
Sparse Core Ops, SparseCore 0:
  12.6 44.2 all-reduce.4
  418.8 124.5 all-gather.7
  875.8 384.5 reduce-scatter.2
  1263.5 142.5 all-gather.5
  1409.1 99.2 all-gather.3
where the time goes:
time: 1550 us
  blocking collectives  999 us (64%)
  waiting for transfers between devices  216 us (14%)
  starting transfers between devices  131 us (8%)
  local copies, waits for them, and re-layouts  109 us (7%)
  matrix products  49.2 us (3%)
  other arithmetic  27.2 us (2%)
    unnamed x2, blocking collectives  678 us
    pmax x1, blocking collectives, shards(): peak = lax.pmax(local_top, 'seq')  321 us
    all_gather x1, waiting for transfers between devices, shards(): piece_keys = lax.all_gather(context_keys, 'seq', axis=0, tiled=True)  72.1 us
    gather x1, local copies, waits for them, and re-layouts, shards(): key_pos = jnp.take(stretch_pos, where_pos)  68 us
    all_to_all x1, starting transfers between devices, shards(): lax.all_to_all(block_query_rows, 'grp', split_axis=1, concat_axis=0, tile...  60 us
    all_to_all x1, starting transfers between devices, shards(): lax.all_to_all(block_key_rows, 'grp', split_axis=1, concat_axis=0, tiled=...  59 us
    all_gather x1, waiting for transfers between devices, shards(): piece_values = lax.all_gather(context_values, 'seq', axis=0, tiled=True)  49.6 us
    psum x1, waiting for transfers between devices, shards(): hidden_state = lax.psum(partial_rows.astype(jnp.bfloat16), 'grp')  42.4 us
  transfers between devices with their start and end apart: 10, of which 8 were waited for; matrix products, arithmetic and copies ran while one was open for 9% of the time, Pallas kernels for 0%

commit v1 on v0

v1 whole, which is shorter than its diff:
```python
import jax
import jax.numpy as jnp
import numpy as np
from jax import lax
from jax.experimental import pallas as pl
from jax.experimental.pallas import tpu as pltpu
from jax.sharding import Mesh, PartitionSpec as P

HEAD = 128
GROUP = 8
WIDTH = GROUP * HEAD
EXP2_SCALE = HEAD ** (-0.5) * 1.4426950408889634
HIDE = -1e30
ALL = ("zh", "x", "y", "zl", "c")
SEQ = ("zh", "x", "y")
GRP = ("zl", "c")
DEPTH = ("zh", "zl")
OLD, NEW = 32, 16
BOTH = OLD + NEW
TOKENS = 8 * NEW
BEAMS = 8
TILES = 11 * BEAMS
ACC = WIDTH + TOKENS
STATE = ACC + 32
MESSAGE = 48
VMEM = pltpu.CompilerParams(vmem_limit_bytes=56 * 1024 * 1024)
SMEM_SPEC = pl.BlockSpec(memory_space=pltpu.SMEM)
VMEM_SPEC = pl.BlockSpec(memory_space=pltpu.VMEM)
BF16, F32 = jnp.bfloat16, jnp.float32


def dot_nt(a, b):
    return lax.dot_general(a, b, (((1,), (1,)), ((), ())), preferred_element_type=F32)


def dot_nn(a, b):
    return lax.dot_general(a, b, (((1,), (0,)), ((), ())), preferred_element_type=F32)


def call(kernel, out_shape, scalars, args, name, cost=None, scratch=()):
    return pl.pallas_call(
        kernel,
        out_shape=out_shape,
        in_specs=[SMEM_SPEC] * len(scalars) + [VMEM_SPEC] * len(args),
        out_specs=jax.tree.map(lambda _: VMEM_SPEC, out_shape),
        scratch_shapes=list(scratch),
        cost_estimate=cost,
        compiler_params=VMEM,
        name=name,
    )(*scalars, *args)


def head_of(plane):
    return 4 * (plane & 1) + 2 * ((plane >> 1) & 1) + (plane >> 2)


def pack_kv_kernel(old_k, old_v, new_k, new_v, out):
    for plane in range(8):
        cols = slice(head_of(plane) * HEAD, (head_of(plane) + 1) * HEAD)
        out[plane, :OLD, :HEAD] = old_k[:, cols]
        out[plane, :OLD, HEAD:] = old_v[:, cols]
        out[plane, OLD:, :HEAD] = new_k[:, cols]
        out[plane, OLD:, HEAD:] = new_v[:, cols]


def pack_q_kernel(q, out):
    for plane in range(8):
        for pair in range(4):
            at = head_of(plane) * WIDTH + pair * 2 * HEAD
            out[plane, pair * NEW : (pair + 1) * NEW, :] = q[:, at : at + 2 * HEAD]


def hidden_kernel(owner, parent, beam_id, looked, out):
    rows = jnp.zeros((looked.shape[1], HEAD), F32)
    for part in range(4):
        rows = rows + jnp.where(owner[...] == part, looked[part].astype(F32), 0.0)
    rows = rows.astype(BF16)
    half = rows.shape[0] // 2
    pick = jnp.where(parent[...] == beam_id[...], 1.0, 0.0).astype(BF16)
    extra = dot_nn(pick, rows[:half]).astype(BF16)
    for part in range(4):
        out[part, : 2 * half, :] = rows
        out[part, 2 * half :, :] = extra


def project_kernel(first, hidden, *refs):
    weights, (out, total) = refs[:4], refs[4:]
    acc = None
    for k in range(4):
        part = dot_nn(hidden[first[0] ^ k], weights[k][...])
        acc = part if acc is None else acc + part
    total[...] = acc
    count = total.shape[0] // 3
    for chip in range(16):
        y, x = chip // 4, chip % 4
        for step in range(3):
            rows = slice(step * count + chip * BEAMS, step * count + (chip + 1) * BEAMS)
            if step < 2:
                for head in range(4):
                    at = (step * 4 + head) * BEAMS
                    out[y, x, at : at + BEAMS, :] = total[rows, head * HEAD : (head + 1) * HEAD]
            at = (8 + step) * BEAMS
            out[y, x, at : at + BEAMS, :] = total[rows, 4 * HEAD :]


def sum_kernel(parts, out):
    out[...] = (parts[0] + parts[1]) + (parts[2] + parts[3])


def attend_kernel(core, pos, kv, q_own, q_other, mine, theirs, keep, send):
    me = core[0]
    per_step = 4
    steps = kv.shape[0] // per_step
    place = core[1]

    def column(which):
        row = pos[pl.ds(which * 16 + place, 1), :].astype(F32)
        return jnp.transpose(jnp.broadcast_to(row, (TOKENS, HEAD)))[:, :1]

    qpos = (column(me), column(1 - me))
    halves = [jnp.where(me == 0, mine[...], theirs[...]), jnp.where(me == 0, theirs[...], mine[...])]
    queries = jnp.concatenate([h[: 8 * BEAMS] for h in halves], 0).astype(BF16)

    def query(block):
        if block == 2 * GROUP:
            return queries
        source = q_own if block < GROUP else q_other
        head = block % GROUP
        rows = slice((head // 2) * NEW, (head // 2 + 1) * NEW)
        lanes = slice((head % 2) * HEAD, (head % 2 + 1) * HEAD)
        return source[:, rows, lanes].reshape(TOKENS, HEAD)

    tiles = {}

    def load(step):
        part = slice(step * per_step, (step + 1) * per_step)
        wide = []
        for low, high in ((0, OLD), (OLD, BOTH)):
            count = per_step * 8 * (high - low)
            k = kv[part, :, low:high, :HEAD].reshape(count, HEAD)
            v = kv[part, :, low:high, HEAD:].reshape(count, HEAD)
            wide.append((k, jnp.concatenate([v, jnp.ones_like(v)], 1)))
        rows = [pos[pl.ds(me * 16 + step * per_step + i, 1), :] for i in range(per_step)]
        kpos = jnp.concatenate(rows, 1).astype(F32)
        bias = [jnp.where(kpos <= p, 0.0, HIDE) for p in qpos]
        tiles[step] = (wide, bias)

    def scores(step, block):
        if step not in tiles:
            load(step)
        wide, bias = tiles[step]
        q = query(block)
        s_old = dot_nt(q, wide[0][0])
        s_new = dot_nt(q, wide[1][0])
        if block < 2 * GROUP:
            s_new = s_new + bias[block // GROUP]
        return s_old, s_new

    def places(block):
        if block < GROUP:
            return keep, block
        if block < 2 * GROUP:
            return send, block - GROUP
        return keep, GROUP

    def absorb(step, block, pair):
        ref, slot = places(block)
        rows = slice(slot * TOKENS, (slot + 1) * TOKENS)
        peak = jnp.maximum(
            jnp.max(pair[0], axis=-1, keepdims=True), jnp.max(pair[1], axis=-1, keepdims=True)
        )
        if step > 0:
            top, total, acc = state[block]
            peak = jnp.maximum(top, peak)
            alpha = jnp.exp2((top - peak) * EXP2_SCALE)
        else:
            peak = jnp.broadcast_to(peak, (TOKENS, HEAD))
        mixed = 0.0
        for s, (_, v) in zip(pair, tiles[step][0]):
            w = jnp.exp2((s - peak[:, :1]) * EXP2_SCALE).astype(BF16)
            mixed = mixed + dot_nn(w, v)
        acc_new, total_new = mixed[:, :HEAD], mixed[:, HEAD:]
        if step > 0:
            acc_new = acc_new + acc[...] * alpha
            total_new = total_new + total[...] * alpha
        return peak, total_new, acc_new

    state = {}
    order = [(step, block) for step in range(steps) for block in range(2 * GROUP + 1)]
    ahead = scores(*order[0])
    for i, (step, block) in enumerate(order):
        now = ahead
        if i + 1 < len(order):
            ahead = scores(*order[i + 1])
        state[block] = absorb(step, block, now)

    top, total, acc = state[2 * GROUP]
    count = 4 * BEAMS
    pad = jnp.zeros((count - 3 * BEAMS, HEAD), F32)
    own_k = jnp.concatenate([halves[0][8 * BEAMS :], pad], 0).astype(BF16)
    own_v = jnp.concatenate([halves[1][8 * BEAMS :], pad], 0).astype(BF16)
    row = lax.broadcasted_iota(jnp.int32, (TOKENS, count), 0)
    key = lax.broadcasted_iota(jnp.int32, (TOKENS, count), 1)
    step = (row // (4 * BEAMS)) % 2
    beam = row % BEAMS
    slot = key // BEAMS
    first = jnp.logical_and(step == 0, slot == 0)
    second = jnp.logical_and(step == 1, jnp.logical_or(slot == 1, slot == 2))
    seen = jnp.logical_and(beam == key % BEAMS, jnp.logical_or(first, second))
    seen = jnp.logical_and(seen, beam // 4 == me)
    own = jnp.where(seen, dot_nt(queries, own_k), HIDE)
    peak = jnp.maximum(top, jnp.max(own, axis=-1, keepdims=True))
    alpha = jnp.exp2((top - peak) * EXP2_SCALE)
    w = jnp.exp2((own - peak[:, :1]) * EXP2_SCALE)
    total = total * alpha + jnp.sum(w, axis=-1, keepdims=True)
    acc = acc * alpha + dot_nn(w.astype(BF16), own_v)
    state[2 * GROUP] = (peak, total, acc)

    for block in range(2 * GROUP + 1):
        ref, slot = places(block)
        top, total, acc = state[block]
        rows = slice(slot * TOKENS, (slot + 1) * TOKENS)
        top, total = jnp.transpose(top)[:1], jnp.transpose(total)[:1]
        for target in (keep, send) if block == 2 * GROUP else (ref,):
            target[rows, :] = acc
            target[ACC + slot : ACC + slot + 1, :] = top
            target[ACC + 16 + slot : ACC + 17 + slot, :] = total


def merge_kernel(core, keep, got, out, message):
    me, first = core[0], core[2]
    message[...] = jnp.zeros_like(message)

    def spread(ref, row):
        return jnp.transpose(jnp.broadcast_to(ref[row : row + 1, :], (TOKENS, HEAD)))

    for slot in range(GROUP + 1):
        rows = slice(slot * TOKENS, (slot + 1) * TOKENS)
        top_a, top_b = spread(keep, ACC + slot), spread(got, ACC + slot)
        peak = jnp.maximum(top_a, top_b)
        a, b = jnp.exp2((top_a - peak) * EXP2_SCALE), jnp.exp2((top_b - peak) * EXP2_SCALE)
        total = spread(keep, ACC + 16 + slot) * a + spread(got, ACC + 16 + slot) * b
        mixed = (keep[rows, :] * a + got[rows, :] * b) / total
        if slot < GROUP:
            lanes = slice(slot * HEAD, (slot + 1) * HEAD)
            for zh in range(4):
                message[zh, : 2 * NEW, lanes] = mixed[zh * 2 * NEW : (zh + 1) * 2 * NEW]
        else:
            for block in range(16):
                half, step, head = block // 8, (block // 4) % 2, block % 4
                lanes = slice((half * 4 + head) * HEAD, (half * 4 + head + 1) * HEAD)
                tile = mixed[block * BEAMS : (block + 1) * BEAMS]
                tile = jnp.where(me == 0, tile[:4], tile[4:])
                for zh in range(4):
                    message[zh, 2 * NEW + step : 2 * NEW + step + 1, lanes] = tile[zh : zh + 1]
    for k in range(4):
        out[k] = message[(first + k) % 4].astype(BF16)


def place_kernel(core, *refs):
    got, (stretch, decode) = refs[:4], refs[4:]
    zh = core[3]
    few = [jnp.zeros((2, WIDTH), F32)] * 4
    for k in range(4):
        origin = (zh - k + 4) % 4
        lane = pl.multiple_of((origin // 2) * WIDTH, WIDTH)
        for low in range(2):
            row = pl.multiple_of(low * 2 * NEW + (origin % 2) * NEW, NEW)
            stretch[pl.ds(row, NEW), pl.ds(lane, WIDTH)] = got[k][low * NEW : (low + 1) * NEW, :]
        tail = got[k][2 * NEW :, :].astype(F32)[:2]
        few = [jnp.where(origin == i, tail, f) for i, f in enumerate(few)]
    for i in range(4):
        head, parity = i // 2, i % 2
        decode[parity, :, head * WIDTH : (head + 1) * WIDTH] = few[i].astype(BF16)


def shards(
    block_query_rows,
    block_key_rows,
    block_value_rows,
    stretch_pos,
    prompt_key_cache,
    prompt_value_cache,
    embed_table,
    query_weight,
    key_weight,
    value_weight,
    beam_tokens,
    parent_beam,
):
    zh, xi, yi, ci = (lax.axis_index(a) for a in ("zh", "x", "y", "c"))
    core = jnp.stack([ci, xi * 4 + yi, 2 * (zh // 2) + ci, zh]).astype(jnp.int32)

    kv = call(
        pack_kv_kernel,
        jax.ShapeDtypeStruct((8, BOTH, 2 * HEAD), BF16),
        (),
        (prompt_key_cache, prompt_value_cache, block_key_rows, block_value_rows),
        "pack_kv",
    )
    kv = lax.all_to_all(kv, DEPTH, split_axis=0, concat_axis=0, tiled=True)
    kv = lax.all_gather(kv.reshape(8 * BOTH, 2 * HEAD), ("x", "y"), axis=0, tiled=True)
    kv = kv.reshape(16, 8, BOTH, 2 * HEAD)
    q = call(
        pack_q_kernel,
        jax.ShapeDtypeStruct((8, 4 * NEW, 2 * HEAD), BF16),
        (),
        (block_query_rows,),
        "pack_q",
    )
    q = lax.all_to_all(q, DEPTH, split_axis=0, concat_axis=0, tiled=True)
    q_other = lax.ppermute(q, "c", [(0, 1), (1, 0)])

    pos = jnp.transpose(stretch_pos.reshape(4, 4, 4, 2, 2, NEW), (4, 1, 2, 0, 3, 5))
    pos = pos.reshape(32, TOKENS)

    vocab_rows = embed_table.shape[0]
    beams = beam_tokens.shape[0]
    ids = jnp.transpose(beam_tokens.reshape(4, 4, 4, 2, 2), (4, 2, 1, 3, 0)).reshape(-1)
    looked = embed_table.at[ids % vocab_rows].get(mode="promise_in_bounds")
    looked = lax.all_to_all(
        jnp.broadcast_to(looked, (4,) + looked.shape), GRP, split_axis=0, concat_axis=0, tiled=True
    )
    beam_id = np.arange(beams, dtype=np.int32).reshape(4, 4, 4, 2).transpose(2, 1, 3, 0)
    parent = jnp.transpose(parent_beam.reshape(4, 4, 4, 2), (2, 1, 3, 0))
    hidden = call(
        hidden_kernel,
        jax.ShapeDtypeStruct((4, 3 * beams, HEAD), BF16),
        (),
        ((ids // vocab_rows)[:, None], parent.reshape(-1, 1), beam_id.reshape(1, -1), looked),
        "hidden",
    )
    hidden = lax.all_to_all(hidden, "zh", split_axis=0, concat_axis=0, tiled=True)

    depth = query_weight.shape[0]
    q_cols = query_weight.shape[1] // 4
    parts = jnp.concatenate(
        [
            query_weight.reshape(depth, 2, 2, q_cols),
            jnp.stack([key_weight.reshape(depth, 2, HEAD), value_weight.reshape(depth, 2, HEAD)], 2),
        ],
        -1,
    )
    parts = jnp.transpose(parts, (1, 2, 0, 3)).reshape(4, depth, q_cols + HEAD)
    weights = []
    for k in range(4):
        pairs = []
        for at in range(8):
            h, c = at // 2, at % 2
            to = h ^ k
            pairs.append((at, (2 * (to // 2) + c) * 2 + to % 2))
        mine = lax.dynamic_index_in_dim(parts, zh ^ k, 0, keepdims=False)
        weights.append(lax.ppermute(mine, ("zh", "c"), pairs))
    part = call(
        project_kernel,
        jax.ShapeDtypeStruct((4, 4, TILES, HEAD), F32),
        (core[2:3],),
        (hidden, *weights),
        "project",
        scratch=[pltpu.VMEM((3 * beams, q_cols + HEAD), F32)],
    )
    part = lax.all_to_all(part, "y", split_axis=0, concat_axis=0, tiled=True)
    part = call(sum_kernel, jax.ShapeDtypeStruct((4, TILES, HEAD), F32), (), (part,), "sum_y")
    part = lax.all_to_all(part, "x", split_axis=0, concat_axis=0, tiled=True)
    mine = call(sum_kernel, jax.ShapeDtypeStruct((TILES, HEAD), F32), (), (part,), "sum_x")
    theirs = lax.ppermute(mine, "c", [(0, 1), (1, 0)])

    rows = (2 * GROUP + 1) * TOKENS
    keys = 16 * 8 * BOTH
    state = jax.ShapeDtypeStruct((STATE, HEAD), F32)
    keep, send = call(
        attend_kernel,
        (state, state),
        (core,),
        (pos, kv, q, q_other, mine, theirs),
        "attend",
        cost=pl.CostEstimate(
            flops=8 * rows * keys * HEAD, bytes_accessed=keys * 512, transcendentals=rows * keys
        ),
    )
    got = lax.ppermute(send, "c", [(0, 1), (1, 0)])
    messages = call(
        merge_kernel,
        jax.ShapeDtypeStruct((4, MESSAGE, WIDTH), BF16),
        (core,),
        (keep, got),
        "merge",
        scratch=[pltpu.VMEM((4, MESSAGE, WIDTH), F32)],
    )

    got = []
    for k in range(4):
        pairs = []
        for at in range(16):
            h1, h0, l, c = (at >> 3) & 1, (at >> 2) & 1, (at >> 1) & 1, at & 1
            pairs.append((at, (((2 * h1 + c + k) % 4) * 2 + l) * 2 + h0))
        got.append(lax.ppermute(messages[k], ("zh", "zl", "c"), pairs))
    return call(
        place_kernel,
        (
            jax.ShapeDtypeStruct((4 * NEW, 2 * WIDTH), BF16),
            jax.ShapeDtypeStruct((2, 2, 2 * WIDTH), BF16),
        ),
        (core,),
        got,
        "place",
    )


def solution(mesh):
    fine = Mesh(mesh.devices.reshape(4, 4, 4, 2, 2), ALL)
    return jax.shard_map(
        shards,
        mesh=fine,
        in_specs=(
            P(ALL, None),
            P(ALL, None),
            P(ALL, None),
            P(),
            P(ALL, None),
            P(ALL, None),
            P(GRP, SEQ),
            P(SEQ, GRP),
            P(SEQ, GRP),
            P(SEQ, GRP),
            P(),
            P(),
        ),
        out_specs=(P(SEQ, GRP), P(SEQ, None, GRP)),
        check_vma=False,
    )
```

time: 1550 us -> 185 us (0.12)
  blocking collectives: 999 us -> 17.9 us
  waiting for transfers between devices: 216 us -> 50.6 us
  local copies, waits for them, and re-layouts: 109 us -> 15.1 us
  starting transfers between devices: 131 us -> 47.4 us
  matrix products: 49.2 us -> 0 us
  Pallas kernels: 0 us -> 36.1 us
  other arithmetic: 27.2 us -> 2.26 us
    unnamed x2 -> x0, blocking collectives: 678 us -> none
    pmax x1 -> x0, blocking collectives: 321 us -> none  [shards(): peak = lax.pmax(local_top, 'seq')]
    all_gather x3 -> x1, waiting for transfers between devices: 162 us -> 0.02 us  [shards(): lax.all_gather(kv.reshape(8 * BOTH, 2 * HEAD), ('x', 'y'), axis=0, tiled=...]
    all_to_all x5, starting transfers between devices: 130 us -> 23 us  [the longest x1 5.99 us: shards(): lax.all_to_all(jnp.broadcast_to(looked, (4,) + looked.shape), GRP, split_...]
    gather x4 -> x1, local copies, waits for them, and re-layouts: 72.7 us -> 3.45 us  [shards(): looked = embed_table.at[ids % vocab_rows].get(mode='promise_in_bounds')]
    dot_general x7 -> x0, matrix products: 49.2 us -> none  [the longest x1 21.5 us: softmax_absorb(): jnp.einsum('tkgd,nkd->tkgn', query_rows, keys, preferred_element_type=jnp...]
    psum x1 -> x0, waiting for transfers between devices: 42.4 us -> none  [shards(): hidden_state = lax.psum(partial_rows.astype(jnp.bfloat16), 'grp')]
    pallas_call x0 -> x9, Pallas kernels: none -> 36.1 us  [call(): pl.pallas_call(kernel, out_shape=out_shape, in_specs=[SMEM_SPEC] * len(sc...]
  transfers between devices with their start and end apart: 10 -> 17, of which waited for: 8 -> 11; matrix products, arithmetic and copies ran while one was open for 9% -> 6% of each run, Pallas kernels for 0% -> 5%
where the time goes in v1:
time: 185 us; the launch traced here: 184 us
  waiting for transfers between devices  50.6 us (27%)
  starting transfers between devices  47.4 us (26%)
  Pallas kernels  36.1 us (20%)
  blocking collectives  17.9 us (10%)
  local copies, waits for them, and re-layouts  15.1 us (8%)
  between operations  14.3 us (8%)
  other arithmetic  2.26 us (1%)
    pallas_call x9, Pallas kernels, call(): pl.pallas_call(kernel, out_shape=out_shape, in_specs=[SMEM_SPEC] * len(sc...  36.1 us
    all_to_all x1, blocking collectives, shards(): kv = lax.all_to_all(kv, DEPTH, split_axis=0, concat_axis=0, tiled=True)  17.9 us
    ppermute x4, waiting for transfers between devices, shards(): weights.append(lax.ppermute(mine, ('zh', 'c'), pairs))  13.7 us
    all_to_all x1, waiting for transfers between devices, shards(): lax.all_to_all(hidden, 'zh', split_axis=0, concat_axis=0, tiled=True)  9.51 us
    ppermute x4, waiting for transfers between devices, shards(): got.append(lax.ppermute(messages[k], ('zh', 'zl', 'c'), pairs))  9.22 us
    ppermute x4, starting transfers between devices, shards(): weights.append(lax.ppermute(mine, ('zh', 'c'), pairs))  8.9 us
    ppermute x4, starting transfers between devices, shards(): got.append(lax.ppermute(messages[k], ('zh', 'zl', 'c'), pairs))  8.85 us
    all_to_all x1, waiting for transfers between devices, shards(): part = lax.all_to_all(part, 'y', split_axis=0, concat_axis=0, tiled=True)  7.37 us
  transfers between devices with their start and end apart: 17, of which 11 were waited for; matrix products, arithmetic and copies ran while one was open for 6% of the time, Pallas kernels for 5%

profile of v1, /device:TPU:1, one launch (start us, length us, event | category | flops | bytes accessed | tf_op | source)
XLA Modules:
  0.0 183.8 jit_solution(8408417739094698247)
XLA Ops:
  7.2 1.7 pack_kv.1
  8.9 17.9 %all_to_all.30 = bf16[8,48,256]{2,1,0:T(8,128)(2,1)} all-to-all(bf16[8,48,256]{2,1,0:T(8,128)(2,1)} %pack_kv.1), channel_id=1, replica_groups=mesh['zh'=4,'x'=4,'y'=4,'zl'=2,'c'=2] {'zh','zl'}, dimensions={0} | all-to-all | bytes 393216 | tf_op jit(solution)/shard_map/all_to_all | solution.py:301
  26.8 0.8 reshape.149
  28.1 0.8 fusion
  28.9 3.5 %gather_fusion = bf16[256,128]{1,0:T(8,128)(2,1)S(1)} fusion(bf16[16384,128]{1,0:T(8,128)(2,1)} %param.19, s32[1024]{0:T(1024)S(1)} %pad_clamp_fusion), kind=kCustom, calls=%fused_computation | custom fusion | bytes 132096 | tf_op jit(solution)/shard_map/gather | solution.py:320
  32.4 0.7 broadcast_in_dim.2
  33.1 6.0 %all-to-all-start.2 = ((bf16[4,256,128]{2,1,0:T(8,128)(2,1)}), bf16[4,256,128]{2,1,0:T(8,128)(2,1)S(1)}, u32[]{:S(2)}, u32[]{:S(2)}) async-start(bf16[4,256,128]{2,1,0:T(8,128)(2,1)} %broadcast_in_dim.2), calls=%async_computation.2 | async-start | bytes 524288 | tf_op jit(solution)/shard_map/all_to_all | solution.py:321
  39.1 0.8 reshape.151
  40.1 0.7 reshape.164.parent
  40.8 3.4 %all-to-all-done.2.looked = bf16[4,256,128]{2,1,0:T(8,128)(2,1)S(1)} async-done(((bf16[4,256,128]{2,1,0:T(8,128)(2,1)}), bf16[4,256,128]{2,1,0:T(8,128)(2,1)S(1)}, u32[]{:S(2)}, u32[]{:S(2)}) %all-to-all-start.2) | async-done | bytes 262176 | tf_op jit(solution)/shard_map/all_to_all | solution.py:321
  44.3 0.7 copy-done.2
  45.0 2.1 %hidden.1 = bf16[4,384,128]{2,1,0:T(8,128)(2,1)} custom-call(s32[256,1]{1,0:T(8,128)} %get-tuple-element.15.owner, s32[128,1]{1,0:T(8,128)} %reshape.164.parent, s32[1,128]{1,0:T(1,128)} %constant.76.clone.beam_id, bf16[4,256,128]{2,1,0:T(8,128)(2,1)} %copy-done.2), custom_call_target="tpu_custom_call" | custom-call | tf_op jit(solution)/shard_map/hidden/pallas_call | solution.py:41
  47.1 3.5 %all-to-all-start.3 = ((bf16[4,384,128]{2,1,0:T(8,128)(2,1)}), bf16[4,384,128]{2,1,0:T(8,128)(2,1)S(1)}, u32[]{:S(2)}, u32[]{:S(2)}) async-start(bf16[4,384,128]{2,1,0:T(8,128)(2,1)} %hidden.1), calls=%async_computation.3 | async-start | bytes 786432 | tf_op jit(solution)/shard_map/all_to_all | solution.py:333
  50.6 1.7 pack_q.1
  52.3 9.5 %all-to-all-done.3.hidden = bf16[4,384,128]{2,1,0:T(8,128)(2,1)S(1)} async-done(((bf16[4,384,128]{2,1,0:T(8,128)(2,1)}), bf16[4,384,128]{2,1,0:T(8,128)(2,1)S(1)}, u32[]{:S(2)}, u32[]{:S(2)}) %all-to-all-start.3) | async-done | bytes 393248 | tf_op jit(solution)/shard_map/all_to_all | solution.py:333
  61.8 5.2 %all-to-all-start.1 = ((bf16[8,64,256]{2,1,0:T(8,128)(2,1)}), bf16[8,64,256]{2,1,0:T(8,128)(2,1)S(1)}, u32[]{:S(2)}, u32[]{:S(2)}) async-start(bf16[8,64,256]{2,1,0:T(8,128)(2,1)} %pack_q.1), calls=%async_computation.1 | async-start | bytes 524288 | tf_op jit(solution)/shard_map/all_to_all | solution.py:311
  68.7 5.4 %collective-permute-start.1 = (bf16[128,640]{1,0:T(8,128)(2,1)S(1)}, bf16[128,640]{1,0:T(8,128)(2,1)S(1)}, u32[]{:S(2)}, u32[]{:S(2)}) collective-permute-start(bf16[128,640]{1,0:T(8,128)(2,1)S(1)} %get-tuple-element.9), channel_id=1, source_target_pairs={{0,0},{1,64},{64,1},{65,65},{128,128},{129,192},{192,129},{193,193... | collective-permute-start | bytes 491528 | tf_op jit(solution)/shard_map/ppermute | solution.py:353
  74.2 2.5 %collective-permute-start.3 = (bf16[128,640]{1,0:T(8,128)(2,1)S(1)}, bf16[128,640]{1,0:T(8,128)(2,1)S(1)}, u32[]{:S(2)}, u32[]{:S(2)}) collective-permute-start(bf16[128,640]{1,0:T(8,128)(2,1)S(1)} %get-tuple-element.7), channel_id=1, source_target_pairs={{0,128},{1,192},{64,129},{65,193},{128,0},{129,64},{192,1},{193,65... | collective-permute-start | bytes 491528 | tf_op jit(solution)/shard_map/ppermute | solution.py:353
  76.7 0.9 collective-permute-start.4
  77.6 4.6 %collective-permute-done.1.refs_0_ = bf16[128,640]{1,0:T(8,128)(2,1)S(1)} collective-permute-done((bf16[128,640]{1,0:T(8,128)(2,1)S(1)}, bf16[128,640]{1,0:T(8,128)(2,1)S(1)}, u32[]{:S(2)}, u32[]{:S(2)}) %collective-permute-start.1) | collective-permute-done | bytes 163872 | tf_op jit(solution)/shard_map/ppermute | solution.py:353
  82.2 4.1 %collective-permute-done.3.refs_2_ = bf16[128,640]{1,0:T(8,128)(2,1)S(1)} collective-permute-done((bf16[128,640]{1,0:T(8,128)(2,1)S(1)}, bf16[128,640]{1,0:T(8,128)(2,1)S(1)}, u32[]{:S(2)}, u32[]{:S(2)}) %collective-permute-start.3) | collective-permute-done | bytes 163872 | tf_op jit(solution)/shard_map/ppermute | solution.py:353
  86.3 5.0 %collective-permute-done.4.refs_3_ = bf16[128,640]{1,0:T(8,128)(2,1)S(1)} collective-permute-done((bf16[128,640]{1,0:T(8,128)(2,1)S(1)}, bf16[128,640]{1,0:T(8,128)(2,1)S(1)}, u32[]{:S(2)}, u32[]{:S(2)}) %collective-permute-start.4) | collective-permute-done | bytes 163872 | tf_op jit(solution)/shard_map/ppermute | solution.py:353
  91.3 0.6 copy-done.10
  91.9 2.8 %project.1 = f32[4,4,88,128]{3,2,1,0:T(8,128)} custom-call(s32[1]{0:T(128)} %bitcast.2.first, bf16[4,384,128]{2,1,0:T(8,128)(2,1)} %copy-done.1, bf16[128,640]{1,0:T(8,128)(2,1)} %copy-done.7, bf16[128,640]{1,0:T(8,128)(2,1)} %copy-done.8, bf16[128,640]{1,0:T(8,128)(2,1)} %copy-done.9, bf16[128,640]{1,0:T(8,128)(2,1)} %copy-done.10), custom_call_target="tpu_custom_call" | custom-call | tf_op jit(solution)/shard_map/project/pallas_call | solution.py:41
  94.7 4.2 %all-to-all-start.4 = ((f32[4,4,88,128]{3,2,1,0:T(8,128)}), f32[4,4,88,128]{3,2,1,0:T(8,128)S(1)}, u32[]{:S(2)}, u32[]{:S(2)}) async-start(f32[4,4,88,128]{3,2,1,0:T(8,128)} %project.1), calls=%async_computation.4 | async-start | bytes 1441792 | tf_op jit(solution)/shard_map/all_to_all | solution.py:362
  98.9 2.0 %collective-permute-start = (bf16[8,64,256]{2,1,0:T(8,128)(2,1)S(1)}, bf16[8,64,256]{2,1,0:T(8,128)(2,1)S(1)}, u32[]{:S(2)}, u32[]{:S(2)}) collective-permute-start(bf16[8,64,256]{2,1,0:T(8,128)(2,1)S(1)} %all-to-all-done.1.q_own), channel_id=1, source_target_pairs={{0,1},{1,0},{2,3},{3,2},{4,5},{5,4},{6,7},{7,6},{8,9},{9,8},{10,11... | collective-permute-start | bytes 786440 | tf_op jit(solution)/shard_map/ppermute | solution.py:312
  100.9 7.4 %all-to-all-done.4.parts = f32[4,4,88,128]{3,2,1,0:T(8,128)S(1)} async-done(((f32[4,4,88,128]{3,2,1,0:T(8,128)}), f32[4,4,88,128]{3,2,1,0:T(8,128)S(1)}, u32[]{:S(2)}, u32[]{:S(2)}) %all-to-all-start.4) | async-done | bytes 720928 | tf_op jit(solution)/shard_map/all_to_all | solution.py:362
  108.3 0.8 copy-done
  109.1 1.8 sum_y.1
  110.9 4.1 %all-to-all-start.5 = ((f32[4,88,128]{2,1,0:T(8,128)}), f32[4,88,128]{2,1,0:T(8,128)S(1)}, u32[]{:S(2)}, u32[]{:S(2)}) async-start(f32[4,88,128]{2,1,0:T(8,128)} %sum_y.1), calls=%async_computation.5 | async-start | bytes 360448 | tf_op jit(solution)/shard_map/all_to_all | solution.py:364
  115.1 5.1 %all-to-all-done.5.parts = f32[4,88,128]{2,1,0:T(8,128)S(1)} async-done(((f32[4,88,128]{2,1,0:T(8,128)}), f32[4,88,128]{2,1,0:T(8,128)S(1)}, u32[]{:S(2)}, u32[]{:S(2)}) %all-to-all-start.5) | async-done | bytes 180256 | tf_op jit(solution)/shard_map/all_to_all | solution.py:364
  120.2 0.7 copy-done.3
  120.8 1.5 sum_x.1.mine
  122.4 4.6 %collective-permute-start.5 = (f32[88,128]{1,0:T(8,128)}, f32[88,128]{1,0:T(8,128)S(1)}, u32[]{:S(2)}, u32[]{:S(2)}) collective-permute-start(f32[88,128]{1,0:T(8,128)} %sum_x.1.mine), channel_id=1, source_target_pairs={{0,1},{1,0},{2,3},{3,2},{4,5},{5,4},{6,7},{7,6},{8,9},{9,8},{10,11... | collective-permute-start | bytes 135176 | tf_op jit(solution)/shard_map/ppermute | solution.py:366
  127.0 0.7 pad_add_fusion.core
  127.9 0.8 reshape.146.pos
  128.8 0.6 copy-done.18
  129.5 20.0 %attend.1 = (f32[1184,128]{1,0:T(8,128)}, f32[1184,128]{1,0:T(8,128)}) custom-call(s32[4]{0:T(128)} %pad_add_fusion.core, s32[32,128]{1,0:T(8,128)} %reshape.146.pos, bf16[16,8,48,256]{3,2,1,0:T(8,128)(2,1)} %bitcast.35, bf16[8,64,256]{2,1,0:T(8,128)(2,1)} %copy-done.6, bf16[8,64,256]{2,1,0:T(8,128)(2,1)} %copy-done.18, f32[88,128]{1,0:T(8,128)} %sum_x.1.mine, ...), custom_call_target="tpu_custom_call" | custom-call | flops 13690208256 | bytes 3145728 | tf_op jit(solution)/shard_map/attend/pallas_call | solution.py:41
  149.4 2.2 %collective-permute-done.6.got = f32[1184,128]{1,0:T(8,128)S(1)} collective-permute-done((f32[1184,128]{1,0:T(8,128)}, f32[1184,128]{1,0:T(8,128)S(1)}, u32[]{:S(2)}, u32[]{:S(2)}) %collective-permute-start.6) | collective-permute-done | bytes 606240 | tf_op jit(solution)/shard_map/ppermute | solution.py:381
  151.7 0.8 copy-done.4
  152.5 2.8 %merge.1 = bf16[4,48,1024]{2,1,0:T(8,128)(2,1)} custom-call(s32[4]{0:T(128)} %pad_add_fusion.core, f32[1184,128]{1,0:T(8,128)} %get-tuple-element.4.keep, f32[1184,128]{1,0:T(8,128)} %copy-done.4), custom_call_target="tpu_custom_call" | custom-call | tf_op jit(solution)/shard_map/merge/pallas_call | solution.py:41
  155.3 1.1 slice_bitcast_fusion
  156.5 8.4 %collective-permute-start.7 = (bf16[48,1024]{1,0:T(8,128)(2,1)S(1)}, bf16[48,1024]{1,0:T(8,128)(2,1)S(1)}, u32[]{:S(2)}, u32[]{:S(2)}) collective-permute-start(bf16[48,1024]{1,0:T(8,128)(2,1)S(1)} %get-tuple-element.13), channel_id=1, source_target_pairs={{0,0},{1,64},{2,2},{3,66},{64,1},{65,65},{66,3},{67,67},{128,128},... | collective-permute-start | bytes 294920 | tf_op jit(solution)/shard_map/ppermute | solution.py:397
  165.2 4.0 %collective-permute-done.7.refs_0_ = bf16[48,1024]{1,0:T(8,128)(2,1)S(1)} collective-permute-done((bf16[48,1024]{1,0:T(8,128)(2,1)S(1)}, bf16[48,1024]{1,0:T(8,128)(2,1)S(1)}, u32[]{:S(2)}, u32[]{:S(2)}) %collective-permute-start.7) | collective-permute-done | bytes 98336 | tf_op jit(solution)/shard_map/ppermute | solution.py:397
  169.2 2.2 %collective-permute-done.8.refs_1_ = bf16[48,1024]{1,0:T(8,128)(2,1)S(1)} collective-permute-done((bf16[48,1024]{1,0:T(8,128)(2,1)S(1)}, bf16[48,1024]{1,0:T(8,128)(2,1)S(1)}, u32[]{:S(2)}, u32[]{:S(2)}) %collective-permute-start.8) | collective-permute-done | bytes 98336 | tf_op jit(solution)/shard_map/ppermute | solution.py:397
  171.4 3.1 %collective-permute-done.9.refs_2_ = bf16[48,1024]{1,0:T(8,128)(2,1)S(1)} collective-permute-done((bf16[48,1024]{1,0:T(8,128)(2,1)S(1)}, bf16[48,1024]{1,0:T(8,128)(2,1)S(1)}, u32[]{:S(2)}, u32[]{:S(2)}) %collective-permute-start.9) | collective-permute-done | bytes 98336 | tf_op jit(solution)/shard_map/ppermute | solution.py:397
  174.5 0.6 copy-done.14
  175.1 1.8 place.1
  (60 shorter events, 3.2 us)
Async XLA Ops:
  7.2 43.4 %copy-start.15 = (bf16[128,256]{1,0:T(8,128)(2,1)S(1)}, bf16[128,256]{1,0:T(8,128)(2,1)}, u32[]{:S(2)}) copy-start(bf16[128,256]{1,0:T(8,128)(2,1)} %param.21) | copy-start | bytes 196612
  7.2 43.4 %copy-start.16 = (bf16[128,256]{1,0:T(8,128)(2,1)S(1)}, bf16[128,256]{1,0:T(8,128)(2,1)}, u32[]{:S(2)}) copy-start(bf16[128,256]{1,0:T(8,128)(2,1)} %param.22) | copy-start | bytes 196612
  7.2 60.1 %copy-start.5 = (bf16[128,2048]{1,0:T(8,128)(2,1)S(1)}, bf16[128,2048]{1,0:T(8,128)(2,1)}, u32[]{:S(2)}) copy-start(bf16[128,2048]{1,0:T(8,128)(2,1)} %param.20) | copy-start | bytes 1572868
  7.2 121.6 %all-gather.2.cloned.1.call-start = ((), (), s32[]{:S(2)}) async-start(), calls=%async_computation.6 | async-start | bytes 3342336 | tf_op jit(solution)/shard_map/all_gather | solution.py:302
  33.1 11.2 %all-to-all-start.2 = ((bf16[4,256,128]{2,1,0:T(8,128)(2,1)}), bf16[4,256,128]{2,1,0:T(8,128)(2,1)S(1)}, u32[]{:S(2)}, u32[]{:S(2)}) async-start(bf16[4,256,128]{2,1,0:T(8,128)(2,1)} %broadcast_in_dim.2), calls=%async_computation.2 | async-start | bytes 524288 | tf_op jit(solution)/shard_map/all_to_all | solution.py:321
  44.3 0.7 copy-start.2
  47.1 14.7 %all-to-all-start.3 = ((bf16[4,384,128]{2,1,0:T(8,128)(2,1)}), bf16[4,384,128]{2,1,0:T(8,128)(2,1)S(1)}, u32[]{:S(2)}, u32[]{:S(2)}) async-start(bf16[4,384,128]{2,1,0:T(8,128)(2,1)} %hidden.1), calls=%async_computation.3 | async-start | bytes 786432 | tf_op jit(solution)/shard_map/all_to_all | solution.py:333
  61.8 29.5 %copy-start.1 = (bf16[4,384,128]{2,1,0:T(8,128)(2,1)}, bf16[4,384,128]{2,1,0:T(8,128)(2,1)S(1)}, u32[]{:S(2)}) copy-start(bf16[4,384,128]{2,1,0:T(8,128)(2,1)S(1)} %all-to-all-done.3.hidden) | copy-start | bytes 1179652
  61.8 32.9 %all-to-all-start.1 = ((bf16[8,64,256]{2,1,0:T(8,128)(2,1)}), bf16[8,64,256]{2,1,0:T(8,128)(2,1)S(1)}, u32[]{:S(2)}, u32[]{:S(2)}) async-start(bf16[8,64,256]{2,1,0:T(8,128)(2,1)} %pack_q.1), calls=%async_computation.1 | async-start | bytes 524288 | tf_op jit(solution)/shard_map/all_to_all | solution.py:311
  68.6 59.1 %copy-start.17 = (s32[4096]{0:T(1024)S(1)}, s32[4096]{0:T(1024)}, u32[]{:S(2)}) copy-start(s32[4096]{0:T(1024)} %param.16) | copy-start | bytes 49156
  68.7 13.5 %collective-permute-start.1 = (bf16[128,640]{1,0:T(8,128)(2,1)S(1)}, bf16[128,640]{1,0:T(8,128)(2,1)S(1)}, u32[]{:S(2)}, u32[]{:S(2)}) collective-permute-start(bf16[128,640]{1,0:T(8,128)(2,1)S(1)} %get-tuple-element.9), channel_id=1, source_target_pairs={{0,0},{1,64},{64,1},{65,65},{128,128},{129,192},{192,129},{193,193... | collective-permute-start | bytes 491528 | tf_op jit(solution)/shard_map/ppermute | solution.py:353
  74.1 8.1 %collective-permute-start.2 = (bf16[128,640]{1,0:T(8,128)(2,1)S(1)}, bf16[128,640]{1,0:T(8,128)(2,1)S(1)}, u32[]{:S(2)}, u32[]{:S(2)}) collective-permute-start(bf16[128,640]{1,0:T(8,128)(2,1)S(1)} %get-tuple-element.8), channel_id=1, source_target_pairs={{0,1},{1,65},{64,0},{65,64},{128,129},{129,193},{192,128},{193,192... | collective-permute-start | bytes 491528 | tf_op jit(solution)/shard_map/ppermute | solution.py:353
  74.2 12.1 %collective-permute-start.3 = (bf16[128,640]{1,0:T(8,128)(2,1)S(1)}, bf16[128,640]{1,0:T(8,128)(2,1)S(1)}, u32[]{:S(2)}, u32[]{:S(2)}) collective-permute-start(bf16[128,640]{1,0:T(8,128)(2,1)S(1)} %get-tuple-element.7), channel_id=1, source_target_pairs={{0,128},{1,192},{64,129},{65,193},{128,0},{129,64},{192,1},{193,65... | collective-permute-start | bytes 491528 | tf_op jit(solution)/shard_map/ppermute | solution.py:353
  76.7 14.6 %collective-permute-start.4 = (bf16[128,640]{1,0:T(8,128)(2,1)S(1)}, bf16[128,640]{1,0:T(8,128)(2,1)S(1)}, u32[]{:S(2)}, u32[]{:S(2)}) collective-permute-start(bf16[128,640]{1,0:T(8,128)(2,1)S(1)} %get-tuple-element.6), channel_id=1, source_target_pairs={{0,129},{1,193},{64,128},{65,192},{128,1},{129,65},{192,0},{193,64... | collective-permute-start | bytes 491528 | tf_op jit(solution)/shard_map/ppermute | solution.py:353
  82.2 9.1 %copy-start.7 = (bf16[128,640]{1,0:T(8,128)(2,1)}, bf16[128,640]{1,0:T(8,128)(2,1)S(1)}, u32[]{:S(2)}) copy-start(bf16[128,640]{1,0:T(8,128)(2,1)S(1)} %collective-permute-done.1.refs_0_) | copy-start | bytes 491524
  82.2 9.1 %copy-start.8 = (bf16[128,640]{1,0:T(8,128)(2,1)}, bf16[128,640]{1,0:T(8,128)(2,1)S(1)}, u32[]{:S(2)}) copy-start(bf16[128,640]{1,0:T(8,128)(2,1)S(1)} %collective-permute-done.2.refs_1_) | copy-start | bytes 491524
  86.3 5.0 %copy-start.9 = (bf16[128,640]{1,0:T(8,128)(2,1)}, bf16[128,640]{1,0:T(8,128)(2,1)S(1)}, u32[]{:S(2)}) copy-start(bf16[128,640]{1,0:T(8,128)(2,1)S(1)} %collective-permute-done.3.refs_2_) | copy-start | bytes 491524
  91.3 0.7 copy-start.10
  94.7 34.1 %copy-start.6 = (bf16[8,64,256]{2,1,0:T(8,128)(2,1)}, bf16[8,64,256]{2,1,0:T(8,128)(2,1)S(1)}, u32[]{:S(2)}) copy-start(bf16[8,64,256]{2,1,0:T(8,128)(2,1)S(1)} %all-to-all-done.1.q_own) | copy-start | bytes 786436
  94.7 13.6 %all-to-all-start.4 = ((f32[4,4,88,128]{3,2,1,0:T(8,128)}), f32[4,4,88,128]{3,2,1,0:T(8,128)S(1)}, u32[]{:S(2)}, u32[]{:S(2)}) async-start(f32[4,4,88,128]{3,2,1,0:T(8,128)} %project.1), calls=%async_computation.4 | async-start | bytes 1441792 | tf_op jit(solution)/shard_map/all_to_all | solution.py:362
  98.9 29.8 %collective-permute-start = (bf16[8,64,256]{2,1,0:T(8,128)(2,1)S(1)}, bf16[8,64,256]{2,1,0:T(8,128)(2,1)S(1)}, u32[]{:S(2)}, u32[]{:S(2)}) collective-permute-start(bf16[8,64,256]{2,1,0:T(8,128)(2,1)S(1)} %all-to-all-done.1.q_own), channel_id=1, source_target_pairs={{0,1},{1,0},{2,3},{3,2},{4,5},{5,4},{6,7},{7,6},{8,9},{9,8},{10,11... | collective-permute-start | bytes 786440 | tf_op jit(solution)/shard_map/ppermute | solution.py:312
  108.3 0.8 copy-start
  110.9 9.2 %all-to-all-start.5 = ((f32[4,88,128]{2,1,0:T(8,128)}), f32[4,88,128]{2,1,0:T(8,128)S(1)}, u32[]{:S(2)}, u32[]{:S(2)}) async-start(f32[4,88,128]{2,1,0:T(8,128)} %sum_y.1), calls=%async_computation.5 | async-start | bytes 360448 | tf_op jit(solution)/shard_map/all_to_all | solution.py:364
  120.2 0.7 copy-start.3
  122.4 6.4 %collective-permute-start.5 = (f32[88,128]{1,0:T(8,128)}, f32[88,128]{1,0:T(8,128)S(1)}, u32[]{:S(2)}, u32[]{:S(2)}) collective-permute-start(f32[88,128]{1,0:T(8,128)} %sum_x.1.mine), channel_id=1, source_target_pairs={{0,1},{1,0},{2,3},{3,2},{4,5},{5,4},{6,7},{7,6},{8,9},{9,8},{10,11... | collective-permute-start | bytes 135176 | tf_op jit(solution)/shard_map/ppermute | solution.py:366
  128.7 0.7 copy-start.18
  128.7 0.7 copy-start.19
  149.4 2.2 %collective-permute-start.6 = (f32[1184,128]{1,0:T(8,128)}, f32[1184,128]{1,0:T(8,128)S(1)}, u32[]{:S(2)}, u32[]{:S(2)}) collective-permute-start(f32[1184,128]{1,0:T(8,128)} %get-tuple-element.5), channel_id=1, source_target_pairs={{0,1},{1,0},{2,3},{3,2},{4,5},{5,4},{6,7},{7,6},{8,9},{9,8},{10,11... | collective-permute-start | bytes 1818632 | tf_op jit(solution)/shard_map/ppermute | solution.py:381
  151.7 0.8 copy-start.4
  156.3 8.9 %collective-permute-start.10 = (bf16[48,1024]{1,0:T(8,128)(2,1)S(1)}, bf16[48,1024]{1,0:T(8,128)(2,1)S(1)}, u32[]{:S(2)}, u32[]{:S(2)}) collective-permute-start(bf16[48,1024]{1,0:T(8,128)(2,1)S(1)} %get-tuple-element.10), channel_id=1, source_target_pairs={{0,192},{1,0},{2,194},{3,2},{64,193},{65,1},{66,195},{67,3},{128,6... | collective-permute-start | bytes 294920 | tf_op jit(solution)/shard_map/ppermute | solution.py:397
  156.5 12.6 %collective-permute-start.7 = (bf16[48,1024]{1,0:T(8,128)(2,1)S(1)}, bf16[48,1024]{1,0:T(8,128)(2,1)S(1)}, u32[]{:S(2)}, u32[]{:S(2)}) collective-permute-start(bf16[48,1024]{1,0:T(8,128)(2,1)S(1)} %get-tuple-element.13), channel_id=1, source_target_pairs={{0,0},{1,64},{2,2},{3,66},{64,1},{65,65},{66,3},{67,67},{128,128},... | collective-permute-start | bytes 294920 | tf_op jit(solution)/shard_map/ppermute | solution.py:397
  165.0 6.4 %collective-permute-start.8 = (bf16[48,1024]{1,0:T(8,128)(2,1)S(1)}, bf16[48,1024]{1,0:T(8,128)(2,1)S(1)}, u32[]{:S(2)}, u32[]{:S(2)}) collective-permute-start(bf16[48,1024]{1,0:T(8,128)(2,1)S(1)} %get-tuple-element.12), channel_id=1, source_target_pairs={{0,64},{1,128},{2,66},{3,130},{64,65},{65,129},{66,67},{67,131},{1... | collective-permute-start | bytes 294920 | tf_op jit(solution)/shard_map/ppermute | solution.py:397
  165.1 9.3 %collective-permute-start.9 = (bf16[48,1024]{1,0:T(8,128)(2,1)S(1)}, bf16[48,1024]{1,0:T(8,128)(2,1)S(1)}, u32[]{:S(2)}, u32[]{:S(2)}) collective-permute-start(bf16[48,1024]{1,0:T(8,128)(2,1)S(1)} %get-tuple-element.11), channel_id=1, source_target_pairs={{0,128},{1,192},{2,130},{3,194},{64,129},{65,193},{66,131},{67,195... | collective-permute-start | bytes 294920 | tf_op jit(solution)/shard_map/ppermute | solution.py:397
  165.2 9.2 %copy-start.11 = (bf16[48,1024]{1,0:T(8,128)(2,1)}, bf16[48,1024]{1,0:T(8,128)(2,1)S(1)}, u32[]{:S(2)}) copy-start(bf16[48,1024]{1,0:T(8,128)(2,1)S(1)} %collective-permute-done.10.refs_3_) | copy-start | bytes 294916
  169.2 5.3 %copy-start.12 = (bf16[48,1024]{1,0:T(8,128)(2,1)}, bf16[48,1024]{1,0:T(8,128)(2,1)S(1)}, u32[]{:S(2)}) copy-start(bf16[48,1024]{1,0:T(8,128)(2,1)S(1)} %collective-permute-done.7.refs_0_) | copy-start | bytes 294916
  171.4 3.1 %copy-start.13 = (bf16[48,1024]{1,0:T(8,128)(2,1)}, bf16[48,1024]{1,0:T(8,128)(2,1)S(1)}, u32[]{:S(2)}) copy-start(bf16[48,1024]{1,0:T(8,128)(2,1)S(1)} %collective-permute-done.8.refs_1_) | copy-start | bytes 294916
  174.5 0.7 copy-start.14
Sparse Core Ops, SparseCore 0:
  27.0 50.9 all-gather.1

commit v2 on v1

--- a/solution.py
+++ b/solution.py
@@ -22,7 +22,7 @@
 TILES = 11 * BEAMS
 ACC = WIDTH + TOKENS
 STATE = ACC + 32
-MESSAGE = 48
+MESSAGE = WIDTH + HEAD
 VMEM = pltpu.CompilerParams(vmem_limit_bytes=56 * 1024 * 1024)
 SMEM_SPEC = pl.BlockSpec(memory_space=pltpu.SMEM)
 VMEM_SPEC = pl.BlockSpec(memory_space=pltpu.VMEM)
@@ -70,41 +70,43 @@
             out[plane, pair * NEW : (pair + 1) * NEW, :] = q[:, at : at + 2 * HEAD]
 
 
-def hidden_kernel(owner, parent, beam_id, looked, out):
+def hidden_kernel(owner, looked, out):
     rows = jnp.zeros((looked.shape[1], HEAD), F32)
     for part in range(4):
         rows = rows + jnp.where(owner[...] == part, looked[part].astype(F32), 0.0)
     rows = rows.astype(BF16)
-    half = rows.shape[0] // 2
+    for part in range(4):
+        out[part] = rows
+
+
+def project_kernel(first, parent, beam_id, hidden, *refs):
+    weights, (out, total, extra) = refs[:4], refs[4:]
+    beams = extra.shape[0]
     pick = jnp.where(parent[...] == beam_id[...], 1.0, 0.0).astype(BF16)
-    extra = dot_nn(pick, rows[:half]).astype(BF16)
-    for part in range(4):
-        out[part, : 2 * half, :] = rows
-        out[part, 2 * half :, :] = extra
-
-
-def project_kernel(first, hidden, *refs):
-    weights, (out, total) = refs[:4], refs[4:]
-    acc = None
+    acc = acc_extra = 0.0
     for k in range(4):
-        part = dot_nn(hidden[first[0] ^ k], weights[k][...])
-        acc = part if acc is None else acc + part
+        rows = hidden[first[0] ^ k]
+        acc = acc + dot_nn(rows, weights[k][...])
+        chosen = dot_nn(pick, rows[:beams]).astype(BF16)
+        acc_extra = acc_extra + dot_nn(chosen, weights[k][:, 4 * HEAD :])
     total[...] = acc
-    count = total.shape[0] // 3
+    extra[...] = acc_extra
     for chip in range(16):
-        y, x = chip // 4, chip % 4
-        for step in range(3):
-            rows = slice(step * count + chip * BEAMS, step * count + (chip + 1) * BEAMS)
-            if step < 2:
-                for head in range(4):
-                    at = (step * 4 + head) * BEAMS
-                    out[y, x, at : at + BEAMS, :] = total[rows, head * HEAD : (head + 1) * HEAD]
+        for step in range(2):
+            rows = slice(step * beams + chip * BEAMS, step * beams + (chip + 1) * BEAMS)
+            for head in range(4):
+                at = (step * 4 + head) * BEAMS
+                out[chip, at : at + BEAMS, :] = total[rows, head * HEAD : (head + 1) * HEAD]
             at = (8 + step) * BEAMS
-            out[y, x, at : at + BEAMS, :] = total[rows, 4 * HEAD :]
+            out[chip, at : at + BEAMS, :] = total[rows, 4 * HEAD :]
+        out[chip, 10 * BEAMS :, :] = extra[chip * BEAMS : (chip + 1) * BEAMS, :]
 
 
 def sum_kernel(parts, out):
-    out[...] = (parts[0] + parts[1]) + (parts[2] + parts[3])
+    terms = [parts[i] for i in range(parts.shape[0])]
+    while len(terms) > 1:
+        terms = [a + b for a, b in zip(terms[::2], terms[1::2])]
+    out[...] = terms[0]
 
 
 def attend_kernel(core, pos, kv, q_own, q_other, mine, theirs, keep, send):
@@ -227,9 +229,11 @@
             target[ACC + 16 + slot : ACC + 17 + slot, :] = total
 
 
-def merge_kernel(core, keep, got, out, message):
+def merge_kernel(core, keep, got, *refs):
+    out, message = refs[:4], refs[4]
     me, first = core[0], core[2]
-    message[...] = jnp.zeros_like(message)
+    for zh in range(4):
+        message[zh, NEW:, WIDTH:] = jnp.zeros((NEW, HEAD), F32)
 
     def spread(ref, row):
         return jnp.transpose(jnp.broadcast_to(ref[row : row + 1, :], (TOKENS, HEAD)))
@@ -244,34 +248,40 @@
         if slot < GROUP:
             lanes = slice(slot * HEAD, (slot + 1) * HEAD)
             for zh in range(4):
-                message[zh, : 2 * NEW, lanes] = mixed[zh * 2 * NEW : (zh + 1) * 2 * NEW]
+                message[zh, :, lanes] = mixed[zh * 2 * NEW : (zh + 1) * 2 * NEW]
         else:
             for block in range(16):
                 half, step, head = block // 8, (block // 4) % 2, block % 4
-                lanes = slice((half * 4 + head) * HEAD, (half * 4 + head + 1) * HEAD)
+                at = step * GROUP + half * 4 + head
                 tile = mixed[block * BEAMS : (block + 1) * BEAMS]
                 tile = jnp.where(me == 0, tile[:4], tile[4:])
                 for zh in range(4):
-                    message[zh, 2 * NEW + step : 2 * NEW + step + 1, lanes] = tile[zh : zh + 1]
+                    message[zh, at : at + 1, WIDTH:] = tile[zh : zh + 1]
     for k in range(4):
-        out[k] = message[(first + k) % 4].astype(BF16)
+        out[k][...] = message[(first + k) % 4].astype(BF16)
 
 
 def place_kernel(core, *refs):
     got, (stretch, decode) = refs[:4], refs[4:]
     zh = core[3]
-    few = [jnp.zeros((2, WIDTH), F32)] * 4
+    few = [jnp.zeros((NEW, HEAD), F32)] * 4
     for k in range(4):
         origin = (zh - k + 4) % 4
         lane = pl.multiple_of((origin // 2) * WIDTH, WIDTH)
         for low in range(2):
             row = pl.multiple_of(low * 2 * NEW + (origin % 2) * NEW, NEW)
-            stretch[pl.ds(row, NEW), pl.ds(lane, WIDTH)] = got[k][low * NEW : (low + 1) * NEW, :]
-        tail = got[k][2 * NEW :, :].astype(F32)[:2]
+            stretch[pl.ds(row, NEW), pl.ds(lane, WIDTH)] = got[k][
+                low * NEW : (low + 1) * NEW, :WIDTH
+            ]
+        tail = got[k][:NEW, WIDTH:].astype(F32)
         few = [jnp.where(origin == i, tail, f) for i, f in enumerate(few)]
     for i in range(4):
         head, parity = i // 2, i % 2
-        decode[parity, :, head * WIDTH : (head + 1) * WIDTH] = few[i].astype(BF16)
+        steps = [
+            jnp.concatenate([few[i][s * GROUP + g : s * GROUP + g + 1] for g in range(GROUP)], 1)
+            for s in range(2)
+        ]
+        decode[parity, :, head * WIDTH : (head + 1) * WIDTH] = jnp.concatenate(steps, 0).astype(BF16)
 
 
 def shards(
@@ -299,38 +309,6 @@
         "pack_kv",
     )
     kv = lax.all_to_all(kv, DEPTH, split_axis=0, concat_axis=0, tiled=True)
-    kv = lax.all_gather(kv.reshape(8 * BOTH, 2 * HEAD), ("x", "y"), axis=0, tiled=True)
-    kv = kv.reshape(16, 8, BOTH, 2 * HEAD)
-    q = call(
-        pack_q_kernel,
-        jax.ShapeDtypeStruct((8, 4 * NEW, 2 * HEAD), BF16),
-        (),
-        (block_query_rows,),
-        "pack_q",
-    )
-    q = lax.all_to_all(q, DEPTH, split_axis=0, concat_axis=0, tiled=True)
-    q_other = lax.ppermute(q, "c", [(0, 1), (1, 0)])
-
-    pos = jnp.transpose(stretch_pos.reshape(4, 4, 4, 2, 2, NEW), (4, 1, 2, 0, 3, 5))
-    pos = pos.reshape(32, TOKENS)
-
-    vocab_rows = embed_table.shape[0]
-    beams = beam_tokens.shape[0]
-    ids = jnp.transpose(beam_tokens.reshape(4, 4, 4, 2, 2), (4, 2, 1, 3, 0)).reshape(-1)
-    looked = embed_table.at[ids % vocab_rows].get(mode="promise_in_bounds")
-    looked = lax.all_to_all(
-        jnp.broadcast_to(looked, (4,) + looked.shape), GRP, split_axis=0, concat_axis=0, tiled=True
-    )
-    beam_id = np.arange(beams, dtype=np.int32).reshape(4, 4, 4, 2).transpose(2, 1, 3, 0)
-    parent = jnp.transpose(parent_beam.reshape(4, 4, 4, 2), (2, 1, 3, 0))
-    hidden = call(
-        hidden_kernel,
-        jax.ShapeDtypeStruct((4, 3 * beams, HEAD), BF16),
-        (),
-        ((ids // vocab_rows)[:, None], parent.reshape(-1, 1), beam_id.reshape(1, -1), looked),
-        "hidden",
-    )
-    hidden = lax.all_to_all(hidden, "zh", split_axis=0, concat_axis=0, tiled=True)
 
     depth = query_weight.shape[0]
     q_cols = query_weight.shape[1] // 4
@@ -342,6 +320,8 @@
         -1,
     )
     parts = jnp.transpose(parts, (1, 2, 0, 3)).reshape(4, depth, q_cols + HEAD)
+    mine = [lax.dynamic_index_in_dim(parts, zh ^ k, 0, keepdims=False) for k in range(4)]
+    kv, mine = lax.optimization_barrier((kv, mine))
     weights = []
     for k in range(4):
         pairs = []
@@ -349,20 +329,57 @@
             h, c = at // 2, at % 2
             to = h ^ k
             pairs.append((at, (2 * (to // 2) + c) * 2 + to % 2))
-        mine = lax.dynamic_index_in_dim(parts, zh ^ k, 0, keepdims=False)
-        weights.append(lax.ppermute(mine, ("zh", "c"), pairs))
+        weights.append(lax.ppermute(mine[k], ("zh", "c"), pairs))
+
+    kv = lax.all_gather(kv.reshape(8 * BOTH, 2 * HEAD), ("x", "y"), axis=0, tiled=True)
+    kv = kv.reshape(16, 8, BOTH, 2 * HEAD)
+
+    pos = jnp.transpose(stretch_pos.reshape(4, 4, 4, 2, 2, NEW), (4, 1, 2, 0, 3, 5))
+    pos = pos.reshape(32, TOKENS)
+
+    vocab_rows = embed_table.shape[0]
+    beams = beam_tokens.shape[0]
+    ids = jnp.transpose(beam_tokens.reshape(4, 4, 4, 2, 2), (4, 2, 1, 3, 0)).reshape(-1)
+    looked = embed_table.at[ids % vocab_rows].get(mode="promise_in_bounds")
+    looked = lax.all_to_all(
+        jnp.broadcast_to(looked, (4,) + looked.shape), GRP, split_axis=0, concat_axis=0, tiled=True
+    )
+    looked, weights = lax.optimization_barrier((looked, weights))
+    hidden = call(
+        hidden_kernel,
+        jax.ShapeDtypeStruct((4, 2 * beams, HEAD), BF16),
+        (),
+        ((ids // vocab_rows)[:, None], looked),
+        "hidden",
+    )
+    hidden = lax.all_to_all(hidden, "zh", split_axis=0, concat_axis=0, tiled=True)
+
+    q = call(
+        pack_q_kernel,
+        jax.ShapeDtypeStruct((8, 4 * NEW, 2 * HEAD), BF16),
+        (),
+        (block_query_rows,),
+        "pack_q",
+    )
+    hidden, q = lax.optimization_barrier((hidden, q))
+    q = lax.all_to_all(q, DEPTH, split_axis=0, concat_axis=0, tiled=True)
+    q_other = lax.ppermute(q, "c", [(0, 1), (1, 0)])
+
+    beam_id = np.arange(beams, dtype=np.int32).reshape(4, 4, 4, 2).transpose(2, 1, 3, 0)
+    parent = jnp.transpose(parent_beam.reshape(4, 4, 4, 2), (2, 1, 3, 0))
     part = call(
         project_kernel,
-        jax.ShapeDtypeStruct((4, 4, TILES, HEAD), F32),
+        jax.ShapeDtypeStruct((16, TILES, HEAD), F32),
         (core[2:3],),
-        (hidden, *weights),
+        (parent.reshape(-1, 1), beam_id.reshape(1, -1), hidden, *weights),
         "project",
-        scratch=[pltpu.VMEM((3 * beams, q_cols + HEAD), F32)],
-    )
-    part = lax.all_to_all(part, "y", split_axis=0, concat_axis=0, tiled=True)
-    part = call(sum_kernel, jax.ShapeDtypeStruct((4, TILES, HEAD), F32), (), (part,), "sum_y")
-    part = lax.all_to_all(part, "x", split_axis=0, concat_axis=0, tiled=True)
-    mine = call(sum_kernel, jax.ShapeDtypeStruct((TILES, HEAD), F32), (), (part,), "sum_x")
+        scratch=[
+            pltpu.VMEM((2 * beams, q_cols + HEAD), F32),
+            pltpu.VMEM((beams, HEAD), F32),
+        ],
+    )
+    part = lax.all_to_all(part, ("y", "x"), split_axis=0, concat_axis=0, tiled=True)
+    mine = call(sum_kernel, jax.ShapeDtypeStruct((TILES, HEAD), F32), (), (part,), "sum")
     theirs = lax.ppermute(mine, "c", [(0, 1), (1, 0)])
 
     rows = (2 * GROUP + 1) * TOKENS
@@ -381,11 +398,11 @@
     got = lax.ppermute(send, "c", [(0, 1), (1, 0)])
     messages = call(
         merge_kernel,
-        jax.ShapeDtypeStruct((4, MESSAGE, WIDTH), BF16),
+        [jax.ShapeDtypeStruct((2 * NEW, MESSAGE), BF16)] * 4,
         (core,),
         (keep, got),
         "merge",
-        scratch=[pltpu.VMEM((4, MESSAGE, WIDTH), F32)],
+        scratch=[pltpu.VMEM((4, 2 * NEW, MESSAGE), F32)],
     )
 
     got = []

time: 185 us -> 166 us (0.90)
  blocking collectives: 17.9 us -> 0 us
  starting transfers between devices: 47.4 us -> 58.2 us
  waiting for transfers between devices: 50.6 us -> 41.5 us
    all_to_all x1 -> x0, blocking collectives: 17.9 us -> none  [shards(): kv = lax.all_to_all(kv, DEPTH, split_axis=0, concat_axis=0, tiled=True)]
    all_to_all x2, starting transfers between devices: 8.35 us -> 15.9 us  [the longest x1 9.15 us: shards(): kv = lax.all_to_all(kv, DEPTH, split_axis=0, concat_axis=0, tiled=True)]
    ppermute x4, waiting for transfers between devices: 13.7 us -> 7.39 us  [shards(): weights.append(lax.ppermute(mine[k], ('zh', 'c'), pairs))]
    all_to_all x1, starting transfers between devices: 3.46 us -> 9.35 us  [shards(): lax.all_to_all(hidden, 'zh', split_axis=0, concat_axis=0, tiled=True)]
    all_to_all x1, waiting for transfers between devices: 0.01 us -> 5.29 us  [shards(): q = lax.all_to_all(q, DEPTH, split_axis=0, concat_axis=0, tiled=True)]
    all_to_all x1, waiting for transfers between devices: 3.44 us -> 0.01 us  [shards(): lax.all_to_all(jnp.broadcast_to(looked, (4,) + looked.shape), GRP, split_...]
    ppermute x4, starting transfers between devices: 8.85 us -> 5.61 us  [shards(): got.append(lax.ppermute(messages[k], ('zh', 'zl', 'c'), pairs))]
    all_to_all x1, waiting for transfers between devices: 9.51 us -> 6.94 us  [shards(): lax.all_to_all(hidden, 'zh', split_axis=0, concat_axis=0, tiled=True)]
  transfers between devices with their start and end apart: 17 -> 17, of which waited for: 11 -> 11; matrix products, arithmetic and copies ran while one was open for 6% -> 8% of each run, Pallas kernels for 5% -> 5%
where the time goes in v2:
time: 166 us; the launch traced here: 165 us
  starting transfers between devices  58.2 us (35%)
  waiting for transfers between devices  41.5 us (25%)
  Pallas kernels  34.4 us (21%)
  between operations  14.3 us (9%)
  local copies, waits for them, and re-layouts  14.2 us (9%)
  other arithmetic  2.22 us (1%)
    pallas_call x8, Pallas kernels, call(): pl.pallas_call(kernel, out_shape=out_shape, in_specs=[SMEM_SPEC] * len(sc...  34.4 us
    all_to_all x1, starting transfers between devices, shards(): lax.all_to_all(hidden, 'zh', split_axis=0, concat_axis=0, tiled=True)  9.35 us
    all_to_all x1, starting transfers between devices, shards(): kv = lax.all_to_all(kv, DEPTH, split_axis=0, concat_axis=0, tiled=True)  9.15 us
    ppermute x4, waiting for transfers between devices, shards(): got.append(lax.ppermute(messages[k], ('zh', 'zl', 'c'), pairs))  8.97 us
    ppermute x4, starting transfers between devices, shards(): weights.append(lax.ppermute(mine[k], ('zh', 'c'), pairs))  8.03 us
    ppermute x4, waiting for transfers between devices, shards(): weights.append(lax.ppermute(mine[k], ('zh', 'c'), pairs))  7.39 us
    all_to_all x1, waiting for transfers between devices, shards(): lax.all_to_all(hidden, 'zh', split_axis=0, concat_axis=0, tiled=True)  6.94 us
    all_to_all x1, starting transfers between devices, shards(): lax.all_to_all(part, ('y', 'x'), split_axis=0, concat_axis=0, tiled=True)  6.76 us
  transfers between devices with their start and end apart: 17, of which 11 were waited for; matrix products, arithmetic and copies ran while one was open for 8% of the time, Pallas kernels for 5%

profile of v2, /device:TPU:1, one launch (start us, length us, event | category | flops | bytes accessed | tf_op | source)
XLA Modules:
  0.0 164.8 jit_solution(11455851533133283363)
XLA Ops:
  7.2 1.6 pack_kv.1
  8.8 9.1 %all-to-all-start = ((bf16[8,48,256]{2,1,0:T(8,128)(2,1)}), bf16[8,48,256]{2,1,0:T(8,128)(2,1)S(1)}, u32[]{:S(2)}, u32[]{:S(2)}) async-start(bf16[8,48,256]{2,1,0:T(8,128)(2,1)} %pack_kv.1), calls=%async_computation | async-start | bytes 393216 | tf_op jit(solution)/shard_map/all_to_all | solution.py:311
  18.0 1.4 reshape.147
  19.4 0.9 stack_reshape.6
  20.3 0.9 stack_reshape.7
  21.5 0.6 maximum_bitcast_fusion
  22.3 4.4 %all-to-all-done = bf16[8,48,256]{2,1,0:T(8,128)(2,1)S(1)} async-done(((bf16[8,48,256]{2,1,0:T(8,128)(2,1)}), bf16[8,48,256]{2,1,0:T(8,128)(2,1)S(1)}, u32[]{:S(2)}, u32[]{:S(2)}) %all-to-all-start) | async-done | bytes 196640 | tf_op jit(solution)/shard_map/all_to_all | solution.py:311
  26.7 0.7 copy-done.3
  27.6 0.3 copy.23
  28.1 0.8 fusion
  28.8 3.5 %gather_fusion = bf16[256,128]{1,0:T(8,128)(2,1)S(1)} fusion(bf16[16384,128]{1,0:T(8,128)(2,1)} %param.19, s32[1024]{0:T(1024)S(1)} %pad_clamp_fusion), kind=kCustom, calls=%fused_computation | custom fusion | bytes 132096 | tf_op jit(solution)/shard_map/gather | solution.py:343
  32.3 0.7 broadcast_in_dim.2
  33.0 6.0 %all-to-all-start.1 = ((bf16[4,256,128]{2,1,0:T(8,128)(2,1)}), bf16[4,256,128]{2,1,0:T(8,128)(2,1)S(1)}, u32[]{:S(2)}, u32[]{:S(2)}) async-start(bf16[4,256,128]{2,1,0:T(8,128)(2,1)} %broadcast_in_dim.2), calls=%async_computation.1 | async-start | bytes 524288 | tf_op jit(solution)/shard_map/all_to_all | solution.py:344
  39.0 1.9 %collective-permute-start = (bf16[128,640]{1,0:T(8,128)(2,1)S(1)}, bf16[128,640]{1,0:T(8,128)(2,1)S(1)}, u32[]{:S(2)}, u32[]{:S(2)}) collective-permute-start(bf16[128,640]{1,0:T(8,128)(2,1)S(1)} %get-tuple-element.21), channel_id=1, source_target_pairs={{0,0},{1,64},{64,1},{65,65},{128,128},{129,192},{192,129},{193,193... | collective-permute-start | bytes 491528 | tf_op jit(solution)/shard_map/ppermute | solution.py:332
  41.0 0.9 collective-permute-start.2
  42.0 5.1 %collective-permute-start.3 = (bf16[128,640]{1,0:T(8,128)(2,1)S(1)}, bf16[128,640]{1,0:T(8,128)(2,1)S(1)}, u32[]{:S(2)}, u32[]{:S(2)}) collective-permute-start(bf16[128,640]{1,0:T(8,128)(2,1)S(1)} %get-tuple-element.24), channel_id=1, source_target_pairs={{0,129},{1,193},{64,128},{65,192},{128,1},{129,65},{192,0},{193,64... | collective-permute-start | bytes 491528 | tf_op jit(solution)/shard_map/ppermute | solution.py:332
  47.1 2.0 %collective-permute-done.refs_0_ = bf16[128,640]{1,0:T(8,128)(2,1)S(1)} collective-permute-done((bf16[128,640]{1,0:T(8,128)(2,1)S(1)}, bf16[128,640]{1,0:T(8,128)(2,1)S(1)}, u32[]{:S(2)}, u32[]{:S(2)}) %collective-permute-start) | collective-permute-done | bytes 163872 | tf_op jit(solution)/shard_map/ppermute | solution.py:332
  49.0 1.1 collective-permute-done.2.refs_2_
  50.1 4.4 %collective-permute-done.3.refs_3_ = bf16[128,640]{1,0:T(8,128)(2,1)S(1)} collective-permute-done((bf16[128,640]{1,0:T(8,128)(2,1)S(1)}, bf16[128,640]{1,0:T(8,128)(2,1)S(1)}, u32[]{:S(2)}, u32[]{:S(2)}) %collective-permute-start.3) | collective-permute-done | bytes 163872 | tf_op jit(solution)/shard_map/ppermute | solution.py:332
  54.5 2.0 %hidden.1 = bf16[4,256,128]{2,1,0:T(8,128)(2,1)} custom-call(s32[256,1]{1,0:T(8,128)} %get-tuple-element.43.owner, bf16[4,256,128]{2,1,0:T(8,128)(2,1)} %copy-done.1), custom_call_target="tpu_custom_call" | custom-call | tf_op jit(solution)/shard_map/hidden/pallas_call | solution.py:41
  56.5 9.3 %all-to-all-start.2 = ((bf16[4,256,128]{2,1,0:T(8,128)(2,1)}), bf16[4,256,128]{2,1,0:T(8,128)(2,1)S(1)}, u32[]{:S(2)}, u32[]{:S(2)}) async-start(bf16[4,256,128]{2,1,0:T(8,128)(2,1)} %hidden.1), calls=%async_computation.2 | async-start | bytes 524288 | tf_op jit(solution)/shard_map/all_to_all | solution.py:355
  65.8 1.7 %pack_q.1 = bf16[8,64,256]{2,1,0:T(8,128)(2,1)} custom-call(bf16[16,8192]{1,0:T(8,128)(2,1)} %q.1), custom_call_target="tpu_custom_call" | custom-call | tf_op jit(solution)/shard_map/pack_q/pallas_call | solution.py:41
  67.5 6.9 %all-to-all-done.2.hidden = bf16[4,256,128]{2,1,0:T(8,128)(2,1)S(1)} async-done(((bf16[4,256,128]{2,1,0:T(8,128)(2,1)}), bf16[4,256,128]{2,1,0:T(8,128)(2,1)S(1)}, u32[]{:S(2)}, u32[]{:S(2)}) %all-to-all-start.2) | async-done | bytes 262176 | tf_op jit(solution)/shard_map/all_to_all | solution.py:355
  74.5 4.7 %all-to-all-start.3 = ((bf16[8,64,256]{2,1,0:T(8,128)(2,1)}), bf16[8,64,256]{2,1,0:T(8,128)(2,1)S(1)}, u32[]{:S(2)}, u32[]{:S(2)}) async-start(bf16[8,64,256]{2,1,0:T(8,128)(2,1)} %pack_q.1), calls=%async_computation.3 | async-start | bytes 524288 | tf_op jit(solution)/shard_map/all_to_all | solution.py:365
  79.5 0.7 reshape.164.parent
  80.3 3.0 %project.1 = f32[16,88,128]{2,1,0:T(8,128)} custom-call(s32[1]{0:T(128)} %bitcast.2.first, s32[128,1]{1,0:T(8,128)} %reshape.164.parent, s32[1,128]{1,0:T(1,128)} %constant.76.clone.beam_id, bf16[4,256,128]{2,1,0:T(8,128)(2,1)} %copy-done.2, bf16[128,640]{1,0:T(8,128)(2,1)} %copy-done.6, bf16[128,640]{1,0:T(8,128)(2,1)} %copy-done.7, ...), custom_call_target="tpu_custom_call" | custom-call | tf_op jit(solution)/shard_map/project/pallas_call | solution.py:41
  83.3 5.3 %all-to-all-done.3.q_own = bf16[8,64,256]{2,1,0:T(8,128)(2,1)S(1)} async-done(((bf16[8,64,256]{2,1,0:T(8,128)(2,1)}), bf16[8,64,256]{2,1,0:T(8,128)(2,1)S(1)}, u32[]{:S(2)}, u32[]{:S(2)}) %all-to-all-start.3) | async-done | bytes 262176 | tf_op jit(solution)/shard_map/all_to_all | solution.py:365
  88.6 6.8 %all-to-all-start.4 = ((f32[16,88,128]{2,1,0:T(8,128)}), f32[16,88,128]{2,1,0:T(8,128)S(1)}, u32[]{:S(2)}, u32[]{:S(2)}) async-start(f32[16,88,128]{2,1,0:T(8,128)} %project.1), calls=%async_computation.4 | async-start | bytes 1441792 | tf_op jit(solution)/shard_map/all_to_all | solution.py:381
  95.3 3.8 %collective-permute-start.4 = (bf16[8,64,256]{2,1,0:T(8,128)(2,1)S(1)}, bf16[8,64,256]{2,1,0:T(8,128)(2,1)S(1)}, u32[]{:S(2)}, u32[]{:S(2)}) collective-permute-start(bf16[8,64,256]{2,1,0:T(8,128)(2,1)S(1)} %all-to-all-done.3.q_own), channel_id=1, source_target_pairs={{0,1},{1,0},{2,3},{3,2},{4,5},{5,4},{6,7},{7,6},{8,9},{9,8},{10,11... | collective-permute-start | bytes 786440 | tf_op jit(solution)/shard_map/ppermute | solution.py:366
  99.1 6.3 %all-to-all-done.4.parts = f32[16,88,128]{2,1,0:T(8,128)S(1)} async-done(((f32[16,88,128]{2,1,0:T(8,128)}), f32[16,88,128]{2,1,0:T(8,128)S(1)}, u32[]{:S(2)}, u32[]{:S(2)}) %all-to-all-start.4) | async-done | bytes 720928 | tf_op jit(solution)/shard_map/all_to_all | solution.py:381
  105.4 0.9 copy-done
  106.2 1.8 %sum.1.mine = f32[88,128]{1,0:T(8,128)} custom-call(f32[16,88,128]{2,1,0:T(8,128)} %copy-done), custom_call_target="tpu_custom_call" | custom-call | tf_op jit(solution)/shard_map/sum/pallas_call | solution.py:41
  108.0 4.8 %collective-permute-start.5 = (f32[88,128]{1,0:T(8,128)}, f32[88,128]{1,0:T(8,128)S(1)}, u32[]{:S(2)}, u32[]{:S(2)}) collective-permute-start(f32[88,128]{1,0:T(8,128)} %sum.1.mine), channel_id=1, source_target_pairs={{0,1},{1,0},{2,3},{3,2},{4,5},{5,4},{6,7},{7,6},{8,9},{9,8},{10,11... | collective-permute-start | bytes 135176 | tf_op jit(solution)/shard_map/ppermute | solution.py:383
  112.8 0.6 pad_add_fusion.core
  113.4 0.2 reshape.145
  113.7 0.8 reshape.146.pos
  114.5 0.7 copy-done.17
  115.2 19.9 %attend.1 = (f32[1184,128]{1,0:T(8,128)}, f32[1184,128]{1,0:T(8,128)}) custom-call(s32[4]{0:T(128)} %pad_add_fusion.core, s32[32,128]{1,0:T(8,128)} %reshape.146.pos, bf16[16,8,48,256]{3,2,1,0:T(8,128)(2,1)} %bitcast.27, bf16[8,64,256]{2,1,0:T(8,128)(2,1)} %copy-done.5, bf16[8,64,256]{2,1,0:T(8,128)(2,1)} %copy-done.17, f32[88,128]{1,0:T(8,128)} %sum.1.mine, ...), custom_call_target="tpu_custom_call" | custom-call | flops 13690208256 | bytes 3145728 | tf_op jit(solution)/shard_map/attend/pallas_call | solution.py:41
  135.2 2.2 %collective-permute-done.6.got = f32[1184,128]{1,0:T(8,128)S(1)} collective-permute-done((f32[1184,128]{1,0:T(8,128)}, f32[1184,128]{1,0:T(8,128)S(1)}, u32[]{:S(2)}, u32[]{:S(2)}) %collective-permute-start.6) | collective-permute-done | bytes 606240 | tf_op jit(solution)/shard_map/ppermute | solution.py:398
  137.4 0.8 copy-done.4
  138.2 2.6 %merge.1 = (bf16[32,1152]{1,0:T(8,128)(2,1)}, bf16[32,1152]{1,0:T(8,128)(2,1)}, bf16[32,1152]{1,0:T(8,128)(2,1)}, bf16[32,1152]{1,0:T(8,128)(2,1)}) custom-call(s32[4]{0:T(128)} %pad_add_fusion.core, f32[1184,128]{1,0:T(8,128)} %get-tuple-element.32.keep, f32[1184,128]{1,0:T(8,128)} %copy-done.4), custom_call_target="tpu_custom_call" | custom-call | tf_op jit(solution)/shard_map/merge/pallas_call | solution.py:41
  141.0 4.9 %collective-permute-start.7 = (bf16[32,1152]{1,0:T(8,128)(2,1)}, bf16[32,1152]{1,0:T(8,128)(2,1)S(1)}, u32[]{:S(2)}, u32[]{:S(2)}) collective-permute-start(bf16[32,1152]{1,0:T(8,128)(2,1)} %get-tuple-element.34), channel_id=1, source_target_pairs={{0,0},{1,64},{2,2},{3,66},{64,1},{65,65},{66,3},{67,67},{128,128},... | collective-permute-start | bytes 221192 | tf_op jit(solution)/shard_map/ppermute | solution.py:414
  146.1 0.5 collective-permute-start.9
  146.5 2.5 %collective-permute-done.7.refs_0_ = bf16[32,1152]{1,0:T(8,128)(2,1)S(1)} collective-permute-done((bf16[32,1152]{1,0:T(8,128)(2,1)}, bf16[32,1152]{1,0:T(8,128)(2,1)S(1)}, u32[]{:S(2)}, u32[]{:S(2)}) %collective-permute-start.7) | collective-permute-done | bytes 73760 | tf_op jit(solution)/shard_map/ppermute | solution.py:414
  149.1 5.7 %collective-permute-done.8.refs_1_ = bf16[32,1152]{1,0:T(8,128)(2,1)S(1)} collective-permute-done((bf16[32,1152]{1,0:T(8,128)(2,1)}, bf16[32,1152]{1,0:T(8,128)(2,1)S(1)}, u32[]{:S(2)}, u32[]{:S(2)}) %collective-permute-start.8) | collective-permute-done | bytes 73760 | tf_op jit(solution)/shard_map/ppermute | solution.py:414
  154.8 0.7 collective-permute-done.9.refs_2_
  155.5 0.6 copy-done.13
  156.1 1.8 %place.1 = (bf16[64,2048]{1,0:T(8,128)(2,1)}, bf16[2,2,2048]{2,1,0:T(2,128)(2,1)}) custom-call(s32[4]{0:T(128)} %pad_add_fusion.core, bf16[32,1152]{1,0:T(8,128)(2,1)} %copy-done.11, bf16[32,1152]{1,0:T(8,128)(2,1)} %copy-done.12, bf16[32,1152]{1,0:T(8,128)(2,1)} %copy-done.13, bf16[32,1152]{1,0:T(8,128)(2,1)} %copy-done.10), custom_call_target="tpu_custom_call" | custom-call | tf_op jit(solution)/shard_map/place/pallas_call | solution.py:41
  (55 shorter events, 1.7 us)
Async XLA Ops:
  8.8 18.7 %copy-start.15 = (s32[128,2]{0,1:T(2,128)S(1)}, s32[128,2]{0,1:T(2,128)}, u32[]{:S(2)}) copy-start(s32[128,2]{0,1:T(2,128)} %param.23) | copy-start | bytes 3076
  8.8 18.0 %all-to-all-start = ((bf16[8,48,256]{2,1,0:T(8,128)(2,1)}), bf16[8,48,256]{2,1,0:T(8,128)(2,1)S(1)}, u32[]{:S(2)}, u32[]{:S(2)}) async-start(bf16[8,48,256]{2,1,0:T(8,128)(2,1)} %pack_kv.1), calls=%async_computation | async-start | bytes 393216 | tf_op jit(solution)/shard_map/all_to_all | solution.py:311
  17.9 96.6 %all-gather.2.cloned.1.call-start = ((), (), s32[]{:S(2)}) async-start(), calls=%async_computation.5 | async-start | bytes 3342336 | tf_op jit(solution)/shard_map/all_gather | solution.py:334
  22.2 56.9 %copy-start.16 = (s32[128]{0:T(128)S(1)}, s32[128]{0:T(128)}, u32[]{:S(2)}) copy-start(s32[128]{0:T(128)} %param.24) | copy-start | bytes 1540
  26.7 0.7 copy-start.3
  33.0 14.0 %all-to-all-start.1 = ((bf16[4,256,128]{2,1,0:T(8,128)(2,1)}), bf16[4,256,128]{2,1,0:T(8,128)(2,1)S(1)}, u32[]{:S(2)}, u32[]{:S(2)}) async-start(bf16[4,256,128]{2,1,0:T(8,128)(2,1)} %broadcast_in_dim.2), calls=%async_computation.1 | async-start | bytes 524288 | tf_op jit(solution)/shard_map/all_to_all | solution.py:344
  39.0 10.0 %collective-permute-start = (bf16[128,640]{1,0:T(8,128)(2,1)S(1)}, bf16[128,640]{1,0:T(8,128)(2,1)S(1)}, u32[]{:S(2)}, u32[]{:S(2)}) collective-permute-start(bf16[128,640]{1,0:T(8,128)(2,1)S(1)} %get-tuple-element.21), channel_id=1, source_target_pairs={{0,0},{1,64},{64,1},{65,65},{128,128},{129,192},{192,129},{193,193... | collective-permute-start | bytes 491528 | tf_op jit(solution)/shard_map/ppermute | solution.py:332
  40.9 8.1 %collective-permute-start.1 = (bf16[128,640]{1,0:T(8,128)(2,1)S(1)}, bf16[128,640]{1,0:T(8,128)(2,1)S(1)}, u32[]{:S(2)}, u32[]{:S(2)}) collective-permute-start(bf16[128,640]{1,0:T(8,128)(2,1)S(1)} %get-tuple-element.22), channel_id=1, source_target_pairs={{0,1},{1,65},{64,0},{65,64},{128,129},{129,193},{192,128},{193,192... | collective-permute-start | bytes 491528 | tf_op jit(solution)/shard_map/ppermute | solution.py:332
  41.0 9.1 %collective-permute-start.2 = (bf16[128,640]{1,0:T(8,128)(2,1)S(1)}, bf16[128,640]{1,0:T(8,128)(2,1)S(1)}, u32[]{:S(2)}, u32[]{:S(2)}) collective-permute-start(bf16[128,640]{1,0:T(8,128)(2,1)S(1)} %get-tuple-element.23), channel_id=1, source_target_pairs={{0,128},{1,192},{64,129},{65,193},{128,0},{129,64},{192,1},{193,65... | collective-permute-start | bytes 491528 | tf_op jit(solution)/shard_map/ppermute | solution.py:332
  42.0 12.5 %collective-permute-start.3 = (bf16[128,640]{1,0:T(8,128)(2,1)S(1)}, bf16[128,640]{1,0:T(8,128)(2,1)S(1)}, u32[]{:S(2)}, u32[]{:S(2)}) collective-permute-start(bf16[128,640]{1,0:T(8,128)(2,1)S(1)} %get-tuple-element.24), channel_id=1, source_target_pairs={{0,129},{1,193},{64,128},{65,192},{128,1},{129,65},{192,0},{193,64... | collective-permute-start | bytes 491528 | tf_op jit(solution)/shard_map/ppermute | solution.py:332
  47.1 7.4 %copy-start.1 = (bf16[4,256,128]{2,1,0:T(8,128)(2,1)}, bf16[4,256,128]{2,1,0:T(8,128)(2,1)S(1)}, u32[]{:S(2)}) copy-start(bf16[4,256,128]{2,1,0:T(8,128)(2,1)S(1)} %all-to-all-done.1.looked) | copy-start | bytes 786436
  49.0 31.2 %copy-start.6 = (bf16[128,640]{1,0:T(8,128)(2,1)}, bf16[128,640]{1,0:T(8,128)(2,1)S(1)}, u32[]{:S(2)}) copy-start(bf16[128,640]{1,0:T(8,128)(2,1)S(1)} %collective-permute-done.refs_0_) | copy-start | bytes 491524
  49.0 31.2 %copy-start.7 = (bf16[128,640]{1,0:T(8,128)(2,1)}, bf16[128,640]{1,0:T(8,128)(2,1)S(1)}, u32[]{:S(2)}) copy-start(bf16[128,640]{1,0:T(8,128)(2,1)S(1)} %collective-permute-done.1.refs_1_) | copy-start | bytes 491524
  50.1 30.1 %copy-start.8 = (bf16[128,640]{1,0:T(8,128)(2,1)}, bf16[128,640]{1,0:T(8,128)(2,1)S(1)}, u32[]{:S(2)}) copy-start(bf16[128,640]{1,0:T(8,128)(2,1)S(1)} %collective-permute-done.2.refs_2_) | copy-start | bytes 491524
  54.5 25.8 %copy-start.9 = (bf16[128,640]{1,0:T(8,128)(2,1)}, bf16[128,640]{1,0:T(8,128)(2,1)S(1)}, u32[]{:S(2)}) copy-start(bf16[128,640]{1,0:T(8,128)(2,1)S(1)} %collective-permute-done.3.refs_3_) | copy-start | bytes 491524
  54.5 58.9 %copy-start.14 = (s32[4096]{0:T(1024)S(1)}, s32[4096]{0:T(1024)}, u32[]{:S(2)}) copy-start(s32[4096]{0:T(1024)} %param.16) | copy-start | bytes 49156
  56.5 18.0 %all-to-all-start.2 = ((bf16[4,256,128]{2,1,0:T(8,128)(2,1)}), bf16[4,256,128]{2,1,0:T(8,128)(2,1)S(1)}, u32[]{:S(2)}, u32[]{:S(2)}) async-start(bf16[4,256,128]{2,1,0:T(8,128)(2,1)} %hidden.1), calls=%async_computation.2 | async-start | bytes 524288 | tf_op jit(solution)/shard_map/all_to_all | solution.py:355
  74.5 5.8 %copy-start.2 = (bf16[4,256,128]{2,1,0:T(8,128)(2,1)}, bf16[4,256,128]{2,1,0:T(8,128)(2,1)S(1)}, u32[]{:S(2)}) copy-start(bf16[4,256,128]{2,1,0:T(8,128)(2,1)S(1)} %all-to-all-done.2.hidden) | copy-start | bytes 786436
  74.5 14.1 %all-to-all-start.3 = ((bf16[8,64,256]{2,1,0:T(8,128)(2,1)}), bf16[8,64,256]{2,1,0:T(8,128)(2,1)S(1)}, u32[]{:S(2)}, u32[]{:S(2)}) async-start(bf16[8,64,256]{2,1,0:T(8,128)(2,1)} %pack_q.1), calls=%async_computation.3 | async-start | bytes 524288 | tf_op jit(solution)/shard_map/all_to_all | solution.py:365
  88.6 26.0 %copy-start.5 = (bf16[8,64,256]{2,1,0:T(8,128)(2,1)}, bf16[8,64,256]{2,1,0:T(8,128)(2,1)S(1)}, u32[]{:S(2)}) copy-start(bf16[8,64,256]{2,1,0:T(8,128)(2,1)S(1)} %all-to-all-done.3.q_own) | copy-start | bytes 786436
  88.6 16.8 %all-to-all-start.4 = ((f32[16,88,128]{2,1,0:T(8,128)}), f32[16,88,128]{2,1,0:T(8,128)S(1)}, u32[]{:S(2)}, u32[]{:S(2)}) async-start(f32[16,88,128]{2,1,0:T(8,128)} %project.1), calls=%async_computation.4 | async-start | bytes 1441792 | tf_op jit(solution)/shard_map/all_to_all | solution.py:381
  95.3 19.2 %collective-permute-start.4 = (bf16[8,64,256]{2,1,0:T(8,128)(2,1)S(1)}, bf16[8,64,256]{2,1,0:T(8,128)(2,1)S(1)}, u32[]{:S(2)}, u32[]{:S(2)}) collective-permute-start(bf16[8,64,256]{2,1,0:T(8,128)(2,1)S(1)} %all-to-all-done.3.q_own), channel_id=1, source_target_pairs={{0,1},{1,0},{2,3},{3,2},{4,5},{5,4},{6,7},{7,6},{8,9},{9,8},{10,11... | collective-permute-start | bytes 786440 | tf_op jit(solution)/shard_map/ppermute | solution.py:366
  105.4 0.9 copy-start
  108.0 6.5 %collective-permute-start.5 = (f32[88,128]{1,0:T(8,128)}, f32[88,128]{1,0:T(8,128)S(1)}, u32[]{:S(2)}, u32[]{:S(2)}) collective-permute-start(f32[88,128]{1,0:T(8,128)} %sum.1.mine), channel_id=1, source_target_pairs={{0,1},{1,0},{2,3},{3,2},{4,5},{5,4},{6,7},{7,6},{8,9},{9,8},{10,11... | collective-permute-start | bytes 135176 | tf_op jit(solution)/shard_map/ppermute | solution.py:383
  114.5 0.7 copy-start.17
  114.5 0.7 copy-start.18
  135.2 2.2 %collective-permute-start.6 = (f32[1184,128]{1,0:T(8,128)}, f32[1184,128]{1,0:T(8,128)S(1)}, u32[]{:S(2)}, u32[]{:S(2)}) collective-permute-start(f32[1184,128]{1,0:T(8,128)} %get-tuple-element.33), channel_id=1, source_target_pairs={{0,1},{1,0},{2,3},{3,2},{4,5},{5,4},{6,7},{7,6},{8,9},{9,8},{10,11... | collective-permute-start | bytes 1818632 | tf_op jit(solution)/shard_map/ppermute | solution.py:398
  137.4 0.8 copy-start.4
  140.9 5.6 %collective-permute-start.10 = (bf16[32,1152]{1,0:T(8,128)(2,1)}, bf16[32,1152]{1,0:T(8,128)(2,1)S(1)}, u32[]{:S(2)}, u32[]{:S(2)}) collective-permute-start(bf16[32,1152]{1,0:T(8,128)(2,1)} %get-tuple-element.37), channel_id=1, source_target_pairs={{0,192},{1,0},{2,194},{3,2},{64,193},{65,1},{66,195},{67,3},{128,6... | collective-permute-start | bytes 221192 | tf_op jit(solution)/shard_map/ppermute | solution.py:414
  141.0 8.0 %collective-permute-start.7 = (bf16[32,1152]{1,0:T(8,128)(2,1)}, bf16[32,1152]{1,0:T(8,128)(2,1)S(1)}, u32[]{:S(2)}, u32[]{:S(2)}) collective-permute-start(bf16[32,1152]{1,0:T(8,128)(2,1)} %get-tuple-element.34), channel_id=1, source_target_pairs={{0,0},{1,64},{2,2},{3,66},{64,1},{65,65},{66,3},{67,67},{128,128},... | collective-permute-start | bytes 221192 | tf_op jit(solution)/shard_map/ppermute | solution.py:414
  145.9 8.9 %collective-permute-start.8 = (bf16[32,1152]{1,0:T(8,128)(2,1)}, bf16[32,1152]{1,0:T(8,128)(2,1)S(1)}, u32[]{:S(2)}, u32[]{:S(2)}) collective-permute-start(bf16[32,1152]{1,0:T(8,128)(2,1)} %get-tuple-element.35), channel_id=1, source_target_pairs={{0,64},{1,128},{2,66},{3,130},{64,65},{65,129},{66,67},{67,131},{1... | collective-permute-start | bytes 221192 | tf_op jit(solution)/shard_map/ppermute | solution.py:414
  146.1 9.4 %collective-permute-start.9 = (bf16[32,1152]{1,0:T(8,128)(2,1)}, bf16[32,1152]{1,0:T(8,128)(2,1)S(1)}, u32[]{:S(2)}, u32[]{:S(2)}) collective-permute-start(bf16[32,1152]{1,0:T(8,128)(2,1)} %get-tuple-element.36), channel_id=1, source_target_pairs={{0,128},{1,192},{2,130},{3,194},{64,129},{65,193},{66,131},{67,195... | collective-permute-start | bytes 221192 | tf_op jit(solution)/shard_map/ppermute | solution.py:414
  146.5 9.0 %copy-start.10 = (bf16[32,1152]{1,0:T(8,128)(2,1)}, bf16[32,1152]{1,0:T(8,128)(2,1)S(1)}, u32[]{:S(2)}) copy-start(bf16[32,1152]{1,0:T(8,128)(2,1)S(1)} %collective-permute-done.10.refs_3_) | copy-start | bytes 221188
  149.1 6.4 %copy-start.11 = (bf16[32,1152]{1,0:T(8,128)(2,1)}, bf16[32,1152]{1,0:T(8,128)(2,1)S(1)}, u32[]{:S(2)}) copy-start(bf16[32,1152]{1,0:T(8,128)(2,1)S(1)} %collective-permute-done.7.refs_0_) | copy-start | bytes 221188
  154.8 0.7 copy-start.12
  155.5 0.6 copy-start.13
Sparse Core Ops, SparseCore 0:
  27.6 50.9 all-gather.1

commit v3 on v2

--- a/solution.py
+++ b/solution.py
@@ -20,8 +20,7 @@
 TOKENS = 8 * NEW
 BEAMS = 8
 TILES = 11 * BEAMS
-ACC = WIDTH + TOKENS
-STATE = ACC + 32
+SHIFTS = (1, 3, 2)
 MESSAGE = WIDTH + HEAD
 VMEM = pltpu.CompilerParams(vmem_limit_bytes=56 * 1024 * 1024)
 SMEM_SPEC = pl.BlockSpec(memory_space=pltpu.SMEM)
@@ -54,20 +53,17 @@
     return 4 * (plane & 1) + 2 * ((plane >> 1) & 1) + (plane >> 2)
 
 
-def pack_kv_kernel(old_k, old_v, new_k, new_v, out):
+def pack_kernel(old_k, old_v, new_k, new_v, q, out):
     for plane in range(8):
-        cols = slice(head_of(plane) * HEAD, (head_of(plane) + 1) * HEAD)
+        head = head_of(plane)
+        cols = slice(head * HEAD, (head + 1) * HEAD)
         out[plane, :OLD, :HEAD] = old_k[:, cols]
         out[plane, :OLD, HEAD:] = old_v[:, cols]
-        out[plane, OLD:, :HEAD] = new_k[:, cols]
-        out[plane, OLD:, HEAD:] = new_v[:, cols]
-
-
-def pack_q_kernel(q, out):
-    for plane in range(8):
+        out[plane, OLD:BOTH, :HEAD] = new_k[:, cols]
+        out[plane, OLD:BOTH, HEAD:] = new_v[:, cols]
         for pair in range(4):
-            at = head_of(plane) * WIDTH + pair * 2 * HEAD
-            out[plane, pair * NEW : (pair + 1) * NEW, :] = q[:, at : at + 2 * HEAD]
+            at = head * WIDTH + pair * 2 * HEAD
+            out[plane, BOTH + pair * NEW : BOTH + (pair + 1) * NEW, :] = q[:, at : at + 2 * HEAD]
 
 
 def hidden_kernel(owner, looked, out):
@@ -109,94 +105,116 @@
     out[...] = terms[0]
 
 
-def attend_kernel(core, pos, kv, q_own, q_other, mine, theirs, keep, send):
-    me = core[0]
-    per_step = 4
-    steps = kv.shape[0] // per_step
-    place = core[1]
+def spread(ref, row):
+    return jnp.transpose(jnp.broadcast_to(ref[row : row + 1, :], (TOKENS, HEAD)))
+
+
+def load_lines(pair):
+    wide = []
+    for low, high in ((0, OLD), (OLD, BOTH)):
+        count = 16 * (high - low)
+        k = jnp.concatenate([r[:, :, low:high, :HEAD].reshape(count, HEAD) for r in pair], 0)
+        v = jnp.concatenate([r[:, :, low:high, HEAD:].reshape(count, HEAD) for r in pair], 0)
+        wide.append((k, jnp.concatenate([v, jnp.ones_like(v)], 1)))
+    return wide
+
+
+def absorb(state, tiles, wide):
+    peak = jnp.maximum(
+        jnp.max(tiles[0], axis=-1, keepdims=True), jnp.max(tiles[1], axis=-1, keepdims=True)
+    )
+    if state is None:
+        peak = jnp.broadcast_to(peak, (TOKENS, HEAD))
+    else:
+        top, total, acc = state
+        peak = jnp.maximum(top, peak)
+        alpha = jnp.exp2((top - peak) * EXP2_SCALE)
+    mixed = 0.0
+    for s, (_, v) in zip(tiles, wide):
+        w = jnp.exp2((s - peak[:, :1]) * EXP2_SCALE).astype(BF16)
+        mixed = mixed + dot_nn(w, v)
+    if state is None:
+        return peak, mixed[:, HEAD:], mixed[:, :HEAD]
+    return peak, mixed[:, HEAD:] + total * alpha, mixed[:, :HEAD] + acc * alpha
+
+
+def put_state(ref, slot, slots, state):
+    top, total, acc = state
+    ref[slot * TOKENS : (slot + 1) * TOKENS, :] = acc
+    at = slots * TOKENS + slot
+    ref[at : at + 1, :] = jnp.transpose(top)[:1]
+    at = at + slots
+    ref[at : at + 1, :] = jnp.transpose(total)[:1]
+
+
+def get_state(ref, slot, slots):
+    at = slots * TOKENS + slot
+    return spread(ref, at), spread(ref, at + slots), ref[slot * TOKENS : (slot + 1) * TOKENS, :]
+
+
+def attend_kernel(shifts, resumed, core, pos, lines, own, other, *refs):
+    if resumed:
+        states, refs = refs[:2], refs[2:]
+    kv, (keep, send) = refs[:-2], refs[-2:]
+    me, place, xi, yi = core[0], core[1], core[4], core[5]
 
     def column(which):
         row = pos[pl.ds(which * 16 + place, 1), :].astype(F32)
         return jnp.transpose(jnp.broadcast_to(row, (TOKENS, HEAD)))[:, :1]
 
     qpos = (column(me), column(1 - me))
-    halves = [jnp.where(me == 0, mine[...], theirs[...]), jnp.where(me == 0, theirs[...], mine[...])]
-    queries = jnp.concatenate([h[: 8 * BEAMS] for h in halves], 0).astype(BF16)
-
-    def query(block):
-        if block == 2 * GROUP:
-            return queries
-        source = q_own if block < GROUP else q_other
+    loaded = {}
+
+    def scores(step, block):
+        if step not in loaded:
+            back = 4 - shifts[step]
+            a = lines[pl.ds(me * 4 + (yi + back) % 4, 1), :]
+            b = lines[pl.ds(8 + me * 4 + (xi + back) % 4, 1), :]
+            kpos = jnp.concatenate([a, b], 1).astype(F32)
+            bias = [jnp.where(kpos <= p, 0.0, HIDE) for p in qpos]
+            loaded[step] = (load_lines(kv[2 * step : 2 * step + 2]), bias)
+        wide, bias = loaded[step]
         head = block % GROUP
-        rows = slice((head // 2) * NEW, (head // 2 + 1) * NEW)
         lanes = slice((head % 2) * HEAD, (head % 2 + 1) * HEAD)
-        return source[:, rows, lanes].reshape(TOKENS, HEAD)
-
-    tiles = {}
-
-    def load(step):
-        part = slice(step * per_step, (step + 1) * per_step)
-        wide = []
-        for low, high in ((0, OLD), (OLD, BOTH)):
-            count = per_step * 8 * (high - low)
-            k = kv[part, :, low:high, :HEAD].reshape(count, HEAD)
-            v = kv[part, :, low:high, HEAD:].reshape(count, HEAD)
-            wide.append((k, jnp.concatenate([v, jnp.ones_like(v)], 1)))
-        rows = [pos[pl.ds(me * 16 + step * per_step + i, 1), :] for i in range(per_step)]
-        kpos = jnp.concatenate(rows, 1).astype(F32)
-        bias = [jnp.where(kpos <= p, 0.0, HIDE) for p in qpos]
-        tiles[step] = (wide, bias)
-
-    def scores(step, block):
-        if step not in tiles:
-            load(step)
-        wide, bias = tiles[step]
-        q = query(block)
-        s_old = dot_nt(q, wide[0][0])
-        s_new = dot_nt(q, wide[1][0])
-        if block < 2 * GROUP:
-            s_new = s_new + bias[block // GROUP]
-        return s_old, s_new
-
-    def places(block):
         if block < GROUP:
-            return keep, block
-        if block < 2 * GROUP:
-            return send, block - GROUP
-        return keep, GROUP
-
-    def absorb(step, block, pair):
-        ref, slot = places(block)
-        rows = slice(slot * TOKENS, (slot + 1) * TOKENS)
-        peak = jnp.maximum(
-            jnp.max(pair[0], axis=-1, keepdims=True), jnp.max(pair[1], axis=-1, keepdims=True)
-        )
-        if step > 0:
-            top, total, acc = state[block]
-            peak = jnp.maximum(top, peak)
-            alpha = jnp.exp2((top - peak) * EXP2_SCALE)
+            at = BOTH + (head // 2) * NEW
+            q = own[:, at : at + NEW, lanes].reshape(TOKENS, HEAD)
         else:
-            peak = jnp.broadcast_to(peak, (TOKENS, HEAD))
-        mixed = 0.0
-        for s, (_, v) in zip(pair, tiles[step][0]):
-            w = jnp.exp2((s - peak[:, :1]) * EXP2_SCALE).astype(BF16)
-            mixed = mixed + dot_nn(w, v)
-        acc_new, total_new = mixed[:, :HEAD], mixed[:, HEAD:]
-        if step > 0:
-            acc_new = acc_new + acc[...] * alpha
-            total_new = total_new + total[...] * alpha
-        return peak, total_new, acc_new
+            at = (head // 2) * NEW
+            q = other[:, at : at + NEW, lanes].reshape(TOKENS, HEAD)
+        return dot_nt(q, wide[0][0]), dot_nt(q, wide[1][0]) + bias[block // GROUP]
 
     state = {}
-    order = [(step, block) for step in range(steps) for block in range(2 * GROUP + 1)]
+    order = [(step, block) for step in range(len(shifts)) for block in range(2 * GROUP)]
     ahead = scores(*order[0])
     for i, (step, block) in enumerate(order):
         now = ahead
         if i + 1 < len(order):
             ahead = scores(*order[i + 1])
-        state[block] = absorb(step, block, now)
-
-    top, total, acc = state[2 * GROUP]
+        if step == 0:
+            state[block] = get_state(states[block // GROUP], block % GROUP, GROUP) if resumed else None
+        state[block] = absorb(state[block], now, loaded[step][0])
+        if step == len(shifts) - 1:
+            put_state((keep, send)[block // GROUP], block % GROUP, GROUP, state[block])
+
+
+def decode_kernel(core, mine, theirs, *refs):
+    kv, out = refs[:-1], refs[-1]
+    me = core[0]
+    halves = [jnp.where(me == 0, mine[...], theirs[...]), jnp.where(me == 0, theirs[...], mine[...])]
+    queries = jnp.concatenate([h[: 8 * BEAMS] for h in halves], 0).astype(BF16)
+    state = None
+    steps = len(kv) // 2
+    wide = load_lines(kv[:2])
+    ahead = [dot_nt(queries, k) for k, _ in wide]
+    for step in range(steps):
+        now, now_wide = ahead, wide
+        if step + 1 < steps:
+            wide = load_lines(kv[2 * step + 2 : 2 * step + 4])
+            ahead = [dot_nt(queries, k) for k, _ in wide]
+        state = absorb(state, now, now_wide)
+
+    top, total, acc = state
     count = 4 * BEAMS
     pad = jnp.zeros((count - 3 * BEAMS, HEAD), F32)
     own_k = jnp.concatenate([halves[0][8 * BEAMS :], pad], 0).astype(BF16)
@@ -216,35 +234,23 @@
     w = jnp.exp2((own - peak[:, :1]) * EXP2_SCALE)
     total = total * alpha + jnp.sum(w, axis=-1, keepdims=True)
     acc = acc * alpha + dot_nn(w.astype(BF16), own_v)
-    state[2 * GROUP] = (peak, total, acc)
-
-    for block in range(2 * GROUP + 1):
-        ref, slot = places(block)
-        top, total, acc = state[block]
-        rows = slice(slot * TOKENS, (slot + 1) * TOKENS)
-        top, total = jnp.transpose(top)[:1], jnp.transpose(total)[:1]
-        for target in (keep, send) if block == 2 * GROUP else (ref,):
-            target[rows, :] = acc
-            target[ACC + slot : ACC + slot + 1, :] = top
-            target[ACC + 16 + slot : ACC + 17 + slot, :] = total
-
-
-def merge_kernel(core, keep, got, *refs):
+    put_state(out, 0, 1, (peak, total, acc))
+
+
+def merge_kernel(core, keep, got, beams_keep, beams_got, *refs):
     out, message = refs[:4], refs[4]
     me, first = core[0], core[2]
     for zh in range(4):
         message[zh, NEW:, WIDTH:] = jnp.zeros((NEW, HEAD), F32)
-
-    def spread(ref, row):
-        return jnp.transpose(jnp.broadcast_to(ref[row : row + 1, :], (TOKENS, HEAD)))
-
     for slot in range(GROUP + 1):
-        rows = slice(slot * TOKENS, (slot + 1) * TOKENS)
-        top_a, top_b = spread(keep, ACC + slot), spread(got, ACC + slot)
-        peak = jnp.maximum(top_a, top_b)
-        a, b = jnp.exp2((top_a - peak) * EXP2_SCALE), jnp.exp2((top_b - peak) * EXP2_SCALE)
-        total = spread(keep, ACC + 16 + slot) * a + spread(got, ACC + 16 + slot) * b
-        mixed = (keep[rows, :] * a + got[rows, :] * b) / total
+        if slot < GROUP:
+            parts = [get_state(ref, slot, GROUP) for ref in (keep, got)]
+        else:
+            parts = [get_state(ref, 0, 1) for ref in (beams_keep, beams_got)]
+        peak = jnp.maximum(parts[0][0], parts[1][0])
+        a, b = [jnp.exp2((p[0] - peak) * EXP2_SCALE) for p in parts]
+        total = parts[0][1] * a + parts[1][1] * b
+        mixed = (parts[0][2] * a + parts[1][2] * b) / total
         if slot < GROUP:
             lanes = slice(slot * HEAD, (slot + 1) * HEAD)
             for zh in range(4):
@@ -299,16 +305,16 @@
     parent_beam,
 ):
     zh, xi, yi, ci = (lax.axis_index(a) for a in ("zh", "x", "y", "c"))
-    core = jnp.stack([ci, xi * 4 + yi, 2 * (zh // 2) + ci, zh]).astype(jnp.int32)
-
-    kv = call(
-        pack_kv_kernel,
-        jax.ShapeDtypeStruct((8, BOTH, 2 * HEAD), BF16),
+    core = jnp.stack([ci, xi * 4 + yi, 2 * (zh // 2) + ci, zh, xi, yi]).astype(jnp.int32)
+
+    packed = call(
+        pack_kernel,
+        jax.ShapeDtypeStruct((8, BOTH + 4 * NEW, 2 * HEAD), BF16),
         (),
-        (prompt_key_cache, prompt_value_cache, block_key_rows, block_value_rows),
-        "pack_kv",
-    )
-    kv = lax.all_to_all(kv, DEPTH, split_axis=0, concat_axis=0, tiled=True)
+        (prompt_key_cache, prompt_value_cache, block_key_rows, block_value_rows, block_query_rows),
+        "pack",
+    )
+    packed = lax.all_to_all(packed, DEPTH, split_axis=0, concat_axis=0, tiled=True)
 
     depth = query_weight.shape[0]
     q_cols = query_weight.shape[1] // 4
@@ -321,7 +327,7 @@
     )
     parts = jnp.transpose(parts, (1, 2, 0, 3)).reshape(4, depth, q_cols + HEAD)
     mine = [lax.dynamic_index_in_dim(parts, zh ^ k, 0, keepdims=False) for k in range(4)]
-    kv, mine = lax.optimization_barrier((kv, mine))
+    packed, mine = lax.optimization_barrier((packed, mine))
     weights = []
     for k in range(4):
         pairs = []
@@ -331,11 +337,26 @@
             pairs.append((at, (2 * (to // 2) + c) * 2 + to % 2))
         weights.append(lax.ppermute(mine[k], ("zh", "c"), pairs))
 
-    kv = lax.all_gather(kv.reshape(8 * BOTH, 2 * HEAD), ("x", "y"), axis=0, tiled=True)
-    kv = kv.reshape(16, 8, BOTH, 2 * HEAD)
+    line_a = jnp.broadcast_to(packed[:4, :BOTH], (4, 4, BOTH, 2 * HEAD))
+    line_b = jnp.broadcast_to(packed[4:, :BOTH], (4, 4, BOTH, 2 * HEAD))
+    line_a = lax.all_to_all(line_a, "x", split_axis=0, concat_axis=0, tiled=True)
+    line_b = lax.all_to_all(line_b, "y", split_axis=0, concat_axis=0, tiled=True)
+    lines = [line_a, line_b]
+    for k in SHIFTS:
+        pairs = [(i, (i + k) % 4) for i in range(4)]
+        lines.append(lax.ppermute(line_a, "y", pairs))
+        lines.append(lax.ppermute(line_b, "x", pairs))
+    q_other = lax.ppermute(packed[:, BOTH:], "c", [(0, 1), (1, 0)])
 
     pos = jnp.transpose(stretch_pos.reshape(4, 4, 4, 2, 2, NEW), (4, 1, 2, 0, 3, 5))
+    halves = pos.reshape(2, 4, 4, 2, TOKENS // 2)
     pos = pos.reshape(32, TOKENS)
+    line_pos = jnp.stack(
+        [
+            jnp.transpose(halves[:, :, :, 0], (0, 2, 1, 3)).reshape(8, 2 * TOKENS),
+            halves[:, :, :, 1].reshape(8, 2 * TOKENS),
+        ]
+    ).reshape(16, 2 * TOKENS)
 
     vocab_rows = embed_table.shape[0]
     beams = beam_tokens.shape[0]
@@ -353,17 +374,6 @@
         "hidden",
     )
     hidden = lax.all_to_all(hidden, "zh", split_axis=0, concat_axis=0, tiled=True)
-
-    q = call(
-        pack_q_kernel,
-        jax.ShapeDtypeStruct((8, 4 * NEW, 2 * HEAD), BF16),
-        (),
-        (block_query_rows,),
-        "pack_q",
-    )
-    hidden, q = lax.optimization_barrier((hidden, q))
-    q = lax.all_to_all(q, DEPTH, split_axis=0, concat_axis=0, tiled=True)
-    q_other = lax.ppermute(q, "c", [(0, 1), (1, 0)])
 
     beam_id = np.arange(beams, dtype=np.int32).reshape(4, 4, 4, 2).transpose(2, 1, 3, 0)
     parent = jnp.transpose(parent_beam.reshape(4, 4, 4, 2), (2, 1, 3, 0))
@@ -382,25 +392,41 @@
     mine = call(sum_kernel, jax.ShapeDtypeStruct((TILES, HEAD), F32), (), (part,), "sum")
     theirs = lax.ppermute(mine, "c", [(0, 1), (1, 0)])
 
-    rows = (2 * GROUP + 1) * TOKENS
-    keys = 16 * 8 * BOTH
-    state = jax.ShapeDtypeStruct((STATE, HEAD), F32)
-    keep, send = call(
-        attend_kernel,
-        (state, state),
+    def attend(shifts, carry, pieces, name):
+        work = 2 * GROUP * TOKENS * len(shifts) * 32 * BOTH
+        state = jax.ShapeDtypeStruct((GROUP * (TOKENS + 2), HEAD), F32)
+        return call(
+            lambda *refs: attend_kernel(shifts, bool(carry), *refs),
+            (state, state),
+            (core,),
+            (pos, line_pos, packed, q_other, *carry, *pieces),
+            name,
+            cost=pl.CostEstimate(
+                flops=8 * work * HEAD, bytes_accessed=work // 4, transcendentals=work
+            ),
+        )
+
+    carry = attend((0,), (), lines[:2], "attend_near")
+    keep, send = attend(SHIFTS, carry, lines[2:], "attend_far")
+    got = lax.ppermute(send, "c", [(0, 1), (1, 0)])
+    beams_keep = call(
+        decode_kernel,
+        jax.ShapeDtypeStruct((TOKENS + 8, HEAD), F32),
         (core,),
-        (pos, kv, q, q_other, mine, theirs),
-        "attend",
+        (mine, theirs, *lines),
+        "decode",
         cost=pl.CostEstimate(
-            flops=8 * rows * keys * HEAD, bytes_accessed=keys * 512, transcendentals=rows * keys
+            flops=8 * TOKENS * 128 * BOTH * HEAD,
+            bytes_accessed=512 * 128 * BOTH,
+            transcendentals=TOKENS * 128 * BOTH,
         ),
     )
-    got = lax.ppermute(send, "c", [(0, 1), (1, 0)])
+    beams_got = lax.ppermute(beams_keep, "c", [(0, 1), (1, 0)])
     messages = call(
         merge_kernel,
         [jax.ShapeDtypeStruct((2 * NEW, MESSAGE), BF16)] * 4,
         (core,),
-        (keep, got),
+        (keep, got, beams_keep, beams_got),
         "merge",
         scratch=[pltpu.VMEM((4, 2 * NEW, MESSAGE), F32)],
     )

time: 166 us -> 158 us (0.952)
  between operations: 14.3 us -> 1.02 us
  starting transfers between devices: 58.2 us -> 64.3 us
  waiting for transfers between devices: 41.5 us -> 36.2 us
  Pallas kernels: 34.4 us -> 38.5 us
    all_to_all x2 -> x3, waiting for transfers between devices: 9.66 us -> 16.9 us  [the longest x1 14.2 us: shards(): lax.all_to_all(packed, DEPTH, split_axis=0, concat_axis=0, tiled=True)]
    all_to_all x1, waiting for transfers between devices: 6.94 us -> 0.15 us  [shards(): lax.all_to_all(hidden, 'zh', split_axis=0, concat_axis=0, tiled=True)]
    all_to_all x1, waiting for transfers between devices: 6.26 us -> 0.01 us  [shards(): lax.all_to_all(part, ('y', 'x'), split_axis=0, concat_axis=0, tiled=True)]
    ppermute x1 -> x8, starting transfers between devices: 3.78 us -> 9.92 us  [the longest x3 5.83 us: shards(): lines.append(lax.ppermute(line_a, 'y', pairs))]
    ppermute x4, starting transfers between devices: 5.61 us -> 11 us  [shards(): got.append(lax.ppermute(messages[k], ('zh', 'zl', 'c'), pairs))]
    ppermute x1, starting transfers between devices: 4.8 us -> 0.01 us  [shards(): theirs = lax.ppermute(mine, 'c', [(0, 1), (1, 0)])]
    ppermute x4, waiting for transfers between devices: 8.97 us -> 4.56 us  [shards(): got.append(lax.ppermute(messages[k], ('zh', 'zl', 'c'), pairs))]
    pallas_call x8 -> x9, Pallas kernels: 34.4 us -> 38.5 us  [call(): pl.pallas_call(kernel, out_shape=out_shape, in_specs=[SMEM_SPEC] * len(sc...]
  transfers between devices with their start and end apart: 17 -> 24, of which waited for: 11 -> 11; matrix products, arithmetic and copies ran while one was open for 8% -> 7% of each run, Pallas kernels for 5% -> 21%
where the time goes in v3:
time: 158 us; the launch traced here: 157 us
  starting transfers between devices  64.3 us (41%)
  Pallas kernels  38.5 us (24%)
  waiting for transfers between devices  36.2 us (23%)
  local copies, waits for them, and re-layouts  14.6 us (9%)
  other arithmetic  2.25 us (1%)
    pallas_call x9, Pallas kernels, call(): pl.pallas_call(kernel, out_shape=out_shape, in_specs=[SMEM_SPEC] * len(sc...  38.5 us
    all_to_all x1, waiting for transfers between devices, shards(): lax.all_to_all(packed, DEPTH, split_axis=0, concat_axis=0, tiled=True)  14.2 us
    ppermute x4, starting transfers between devices, shards(): got.append(lax.ppermute(messages[k], ('zh', 'zl', 'c'), pairs))  11 us
    ppermute x4, waiting for transfers between devices, shards(): weights.append(lax.ppermute(mine[k], ('zh', 'c'), pairs))  10.4 us
    all_to_all x1, starting transfers between devices, shards(): lax.all_to_all(packed, DEPTH, split_axis=0, concat_axis=0, tiled=True)  9.01 us
    all_to_all x1, starting transfers between devices, shards(): lax.all_to_all(hidden, 'zh', split_axis=0, concat_axis=0, tiled=True)  7.31 us
    all_to_all x1, starting transfers between devices, shards(): lax.all_to_all(part, ('y', 'x'), split_axis=0, concat_axis=0, tiled=True)  6.22 us
    ppermute x3, starting transfers between devices, shards(): lines.append(lax.ppermute(line_a, 'y', pairs))  5.83 us
  transfers between devices with their start and end apart: 24, of which 11 were waited for; matrix products, arithmetic and copies ran while one was open for 7% of the time, Pallas kernels for 21%

profile of v3, /device:TPU:1, one launch (start us, length us, event | category | flops | bytes accessed | tf_op | source)
XLA Modules:
  0.0 156.9 jit_solution(4276104865684741226)
XLA Ops:
  0.7 1.9 %pack.1 = bf16[8,112,256]{2,1,0:T(8,128)(2,1)} custom-call(bf16[32,1024]{1,0:T(8,128)(2,1)} %old_k.1, bf16[32,1024]{1,0:T(8,128)(2,1)} %old_v.1, bf16[16,1024]{1,0:T(8,128)(2,1)} %new_k.1, bf16[16,1024]{1,0:T(8,128)(2,1)} %new_v.1, bf16[16,8192]{1,0:T(8,128)(2,1)} %q.1), custom_call_target="tpu_custom_call" | custom-call | tf_op jit(solution)/shard_map/pack/pallas_call | solution.py:40
  2.6 9.0 %all-to-all-start = ((bf16[8,112,256]{2,1,0:T(8,128)(2,1)}), bf16[8,112,256]{2,1,0:T(8,128)(2,1)S(1)}, u32[]{:S(2)}, u32[]{:S(2)}) async-start(bf16[8,112,256]{2,1,0:T(8,128)(2,1)} %pack.1), calls=%async_computation | async-start | bytes 917504 | tf_op jit(solution)/shard_map/all_to_all | solution.py:317
  13.1 0.6 maximum_bitcast_fusion
  13.9 14.2 %all-to-all-done.refs_3_ = bf16[8,112,256]{2,1,0:T(8,128)(2,1)S(1)} async-done(((bf16[8,112,256]{2,1,0:T(8,128)(2,1)}), bf16[8,112,256]{2,1,0:T(8,128)(2,1)S(1)}, u32[]{:S(2)}, u32[]{:S(2)}) %all-to-all-start) | async-done | bytes 458784 | tf_op jit(solution)/shard_map/all_to_all | solution.py:317
  28.1 0.8 broadcast_in_dim.11
  28.9 4.0 %all-to-all-start.1 = ((bf16[4,4,48,256]{3,2,1,0:T(8,128)(2,1)}), bf16[4,4,48,256]{3,2,1,0:T(8,128)(2,1)S(1)}, u32[]{:S(2)}, u32[]{:S(2)}) async-start(bf16[4,4,48,256]{3,2,1,0:T(8,128)(2,1)} %broadcast_in_dim.11), calls=%async_computation.1 | async-start | bytes 786432 | tf_op jit(solution)/shard_map/all_to_all | solution.py:342
  33.0 0.8 fusion
  33.7 3.5 %gather_fusion = bf16[256,128]{1,0:T(8,128)(2,1)S(1)} fusion(bf16[16384,128]{1,0:T(8,128)(2,1)} %param.19, s32[1024]{0:T(1024)S(1)} %pad_clamp_fusion), kind=kCustom, calls=%fused_computation | custom fusion | bytes 132096 | tf_op jit(solution)/shard_map/gather | solution.py:364
  37.2 2.7 %all-to-all-done.1.refs_5_.refs_0_ = bf16[4,4,48,256]{3,2,1,0:T(8,128)(2,1)S(1)} async-done(((bf16[4,4,48,256]{3,2,1,0:T(8,128)(2,1)}), bf16[4,4,48,256]{3,2,1,0:T(8,128)(2,1)S(1)}, u32[]{:S(2)}, u32[]{:S(2)}) %all-to-all-start.1) | async-done | bytes 393248 | tf_op jit(solution)/shard_map/all_to_all | solution.py:342
  39.9 0.8 broadcast_in_dim.13
  40.7 5.4 %all-to-all-start.3 = ((bf16[4,256,128]{2,1,0:T(8,128)(2,1)}), bf16[4,256,128]{2,1,0:T(8,128)(2,1)S(1)}, u32[]{:S(2)}, u32[]{:S(2)}) async-start(bf16[4,256,128]{2,1,0:T(8,128)(2,1)} %broadcast_in_dim.13), calls=%async_computation.3 | async-start | bytes 524288 | tf_op jit(solution)/shard_map/all_to_all | solution.py:365
  46.2 2.9 %collective-permute-start.5 = (bf16[4,4,48,256]{3,2,1,0:T(8,128)(2,1)S(1)}, bf16[4,4,48,256]{3,2,1,0:T(8,128)(2,1)S(1)}, u32[]{:S(2)}, u32[]{:S(2)}) collective-permute-start(bf16[4,4,48,256]{3,2,1,0:T(8,128)(2,1)S(1)} %all-to-all-done.1.refs_5_.refs_0_), channel_id=1, source_target_pairs={{0,8},{4,12},{8,0},{12,4},{1,9},{5,13},{9,1},{13,5},{2,10},{6,14},... | collective-permute-start | bytes 1179656 | tf_op jit(solution)/shard_map/ppermute | solution.py:347
  49.1 1.9 %collective-permute-start.8 = (bf16[128,640]{1,0:T(8,128)(2,1)S(1)}, bf16[128,640]{1,0:T(8,128)(2,1)S(1)}, u32[]{:S(2)}, u32[]{:S(2)}) collective-permute-start(bf16[128,640]{1,0:T(8,128)(2,1)S(1)} %get-tuple-element.25), channel_id=1, source_target_pairs={{0,0},{1,64},{64,1},{65,65},{128,128},{129,192},{192,129},{193,193... | collective-permute-start | bytes 491528 | tf_op jit(solution)/shard_map/ppermute | solution.py:338
  51.3 0.8 broadcast_in_dim.12
  52.2 4.2 %all-to-all-start.2 = ((bf16[4,4,48,256]{3,2,1,0:T(8,128)(2,1)}), bf16[4,4,48,256]{3,2,1,0:T(8,128)(2,1)S(1)}, u32[]{:S(2)}, u32[]{:S(2)}) async-start(bf16[4,4,48,256]{3,2,1,0:T(8,128)(2,1)} %broadcast_in_dim.12), calls=%async_computation.2 | async-start | bytes 786432 | tf_op jit(solution)/shard_map/all_to_all | solution.py:343
  56.4 1.2 collective-permute-start
  57.9 0.8 reshape.146.refs_1_
  59.3 0.7 reshape.163.parent
  60.6 3.3 %collective-permute-start.11 = (bf16[128,640]{1,0:T(8,128)(2,1)S(1)}, bf16[128,640]{1,0:T(8,128)(2,1)S(1)}, u32[]{:S(2)}, u32[]{:S(2)}) collective-permute-start(bf16[128,640]{1,0:T(8,128)(2,1)S(1)} %get-tuple-element.28), channel_id=1, source_target_pairs={{0,129},{1,193},{64,128},{65,192},{128,1},{129,65},{192,0},{193,64... | collective-permute-start | bytes 491528 | tf_op jit(solution)/shard_map/ppermute | solution.py:338
  64.1 0.6 stack.33.refs_0_.core
  64.8 8.0 %collective-permute-done.10.refs_2_ = bf16[128,640]{1,0:T(8,128)(2,1)S(1)} collective-permute-done((bf16[128,640]{1,0:T(8,128)(2,1)S(1)}, bf16[128,640]{1,0:T(8,128)(2,1)S(1)}, u32[]{:S(2)}, u32[]{:S(2)}) %collective-permute-start.10) | collective-permute-done | bytes 163872 | tf_op jit(solution)/shard_map/ppermute | solution.py:338
  72.8 2.4 %collective-permute-done.11.refs_3_ = bf16[128,640]{1,0:T(8,128)(2,1)S(1)} collective-permute-done((bf16[128,640]{1,0:T(8,128)(2,1)S(1)}, bf16[128,640]{1,0:T(8,128)(2,1)S(1)}, u32[]{:S(2)}, u32[]{:S(2)}) %collective-permute-start.11) | collective-permute-done | bytes 163872 | tf_op jit(solution)/shard_map/ppermute | solution.py:338
  75.1 2.0 %hidden.1 = bf16[4,256,128]{2,1,0:T(8,128)(2,1)} custom-call(s32[256,1]{1,0:T(8,128)} %get-tuple-element.45.owner, bf16[4,256,128]{2,1,0:T(8,128)(2,1)} %copy-done.4), custom_call_target="tpu_custom_call" | custom-call | tf_op jit(solution)/shard_map/hidden/pallas_call | solution.py:40
  77.1 2.9 %collective-permute-start.3 = (bf16[4,4,48,256]{3,2,1,0:T(8,128)(2,1)S(1)}, bf16[4,4,48,256]{3,2,1,0:T(8,128)(2,1)S(1)}, u32[]{:S(2)}, u32[]{:S(2)}) collective-permute-start(bf16[4,4,48,256]{3,2,1,0:T(8,128)(2,1)S(1)} %all-to-all-done.1.refs_5_.refs_0_), channel_id=1, source_target_pairs={{0,12},{4,0},{8,4},{12,8},{1,13},{5,1},{9,5},{13,9},{2,14},{6,2},{... | collective-permute-start | bytes 1179656 | tf_op jit(solution)/shard_map/ppermute | solution.py:347
  80.1 7.3 %all-to-all-start.4 = ((bf16[4,256,128]{2,1,0:T(8,128)(2,1)}), bf16[4,256,128]{2,1,0:T(8,128)(2,1)S(1)}, u32[]{:S(2)}, u32[]{:S(2)}) async-start(bf16[4,256,128]{2,1,0:T(8,128)(2,1)} %hidden.1), calls=%async_computation.4 | async-start | bytes 524288 | tf_op jit(solution)/shard_map/all_to_all | solution.py:376
  87.7 2.4 %collective-permute-start.4 = (bf16[4,4,48,256]{3,2,1,0:T(8,128)(2,1)S(1)}, bf16[4,4,48,256]{3,2,1,0:T(8,128)(2,1)S(1)}, u32[]{:S(2)}, u32[]{:S(2)}) collective-permute-start(bf16[4,4,48,256]{3,2,1,0:T(8,128)(2,1)S(1)} %all-to-all-done.2.refs_6_.refs_1_), channel_id=1, source_target_pairs={{0,48},{16,0},{32,16},{48,32},{1,49},{17,1},{33,17},{49,33},{2,50}... | collective-permute-start | bytes 1179656 | tf_op jit(solution)/shard_map/ppermute | solution.py:348
  90.1 0.7 add_bitcast_fusion.refs_2_
  90.7 6.4 %attend_near.1 = (f32[1040,128]{1,0:T(8,128)}, f32[1040,128]{1,0:T(8,128)}) custom-call(s32[6]{0:T(128)} %stack.33.refs_0_.core, s32[32,128]{1,0:T(8,128)} %reshape.146.refs_1_, s32[16,256]{1,0:T(8,128)} %add_bitcast_fusion.refs_2_, bf16[8,112,256]{2,1,0:T(8,128)(2,1)} %copy-done.1, bf16[8,64,256]{2,1,0:T(8,128)(2,1)} %collective-permute-done.refs_4_, ...), custom_call_target="tpu_custom_call" | custom-call | flops 3221225472 | bytes 786432 | tf_op jit(solution)/shard_map/attend_near/pallas_call | solution.py:40
  97.3 0.7 copy-done.5
  98.0 3.0 %project.1 = f32[16,88,128]{2,1,0:T(8,128)} custom-call(s32[1]{0:T(128)} %bitcast.2.first, s32[128,1]{1,0:T(8,128)} %reshape.163.parent, s32[1,128]{1,0:T(1,128)} %constant.76.clone.beam_id, bf16[4,256,128]{2,1,0:T(8,128)(2,1)} %copy-done.5, bf16[128,640]{1,0:T(8,128)(2,1)} %copy-done.13, bf16[128,640]{1,0:T(8,128)(2,1)} %copy-done.14, ...), custom_call_target="tpu_custom_call" | custom-call | tf_op jit(solution)/shard_map/project/pallas_call | solution.py:40
  101.0 6.2 %all-to-all-start.5 = ((f32[16,88,128]{2,1,0:T(8,128)}), f32[16,88,128]{2,1,0:T(8,128)S(1)}, u32[]{:S(2)}, u32[]{:S(2)}) async-start(f32[16,88,128]{2,1,0:T(8,128)} %project.1), calls=%async_computation.5 | async-start | bytes 1441792 | tf_op jit(solution)/shard_map/all_to_all | solution.py:391
  107.3 1.1 collective-permute-done.2.refs_8_.refs_3_
  108.5 15.1 %attend_far.1 = (f32[1040,128]{1,0:T(8,128)}, f32[1040,128]{1,0:T(8,128)}) custom-call(s32[6]{0:T(128)} %stack.33.refs_0_.core, s32[32,128]{1,0:T(8,128)} %reshape.146.refs_1_, s32[16,256]{1,0:T(8,128)} %add_bitcast_fusion.refs_2_, bf16[8,112,256]{2,1,0:T(8,128)(2,1)} %copy-done.1, bf16[8,64,256]{2,1,0:T(8,128)(2,1)} %collective-permute-done.refs_4_, ...), custom_call_target="tpu_custom_call" | custom-call | flops 9663676416 | bytes 2359296 | tf_op jit(solution)/shard_map/attend_far/pallas_call | solution.py:40
  123.6 1.4 collective-permute-start.7
  125.1 0.9 copy-done
  126.0 1.8 %sum.1.mine = f32[88,128]{1,0:T(8,128)} custom-call(f32[16,88,128]{2,1,0:T(8,128)} %copy-done), custom_call_target="tpu_custom_call" | custom-call | tf_op jit(solution)/shard_map/sum/pallas_call | solution.py:40
  127.7 1.4 collective-permute-done.12.theirs
  129.8 3.9 %decode.1.beams_keep = f32[136,128]{1,0:T(8,128)} custom-call(s32[6]{0:T(128)} %stack.33.refs_0_.core, f32[88,128]{1,0:T(8,128)} %sum.1.mine, f32[88,128]{1,0:T(8,128)} %copy-done.24, bf16[4,4,48,256]{3,2,1,0:T(8,128)(2,1)} %copy-done.2, bf16[4,4,48,256]{3,2,1,0:T(8,128)(2,1)} %copy-done.3, bf16[4,4,48,256]{3,2,1,0:T(8,128)(2,1)} %copy-done.10, ...), custom_call_target="tpu_custom_call" | custom-call | flops 805306368 | bytes 3145728 | tf_op jit(solution)/shard_map/decode/pallas_call | solution.py:40
  133.8 1.3 collective-permute-done.13.beams_got
  135.7 2.6 %merge.1 = (bf16[32,1152]{1,0:T(8,128)(2,1)}, bf16[32,1152]{1,0:T(8,128)(2,1)}, bf16[32,1152]{1,0:T(8,128)(2,1)}, bf16[32,1152]{1,0:T(8,128)(2,1)}) custom-call(s32[6]{0:T(128)} %stack.33.refs_0_.core, f32[1040,128]{1,0:T(8,128)} %get-tuple-element.23.keep, f32[1040,128]{1,0:T(8,128)} %copy-done.6, f32[136,128]{1,0:T(8,128)} %decode.1.beams_keep, ...), custom_call_target="tpu_custom_call" | custom-call | tf_op jit(solution)/shard_map/merge/pallas_call | solution.py:40
  138.4 4.6 %collective-permute-start.14 = (bf16[32,1152]{1,0:T(8,128)(2,1)}, bf16[32,1152]{1,0:T(8,128)(2,1)S(1)}, u32[]{:S(2)}, u32[]{:S(2)}) collective-permute-start(bf16[32,1152]{1,0:T(8,128)(2,1)} %get-tuple-element.34), channel_id=1, source_target_pairs={{0,0},{1,64},{2,2},{3,66},{64,1},{65,65},{66,3},{67,67},{128,128},... | collective-permute-start | bytes 221192 | tf_op jit(solution)/shard_map/ppermute | solution.py:440
  142.9 2.6 %collective-permute-start.15 = (bf16[32,1152]{1,0:T(8,128)(2,1)}, bf16[32,1152]{1,0:T(8,128)(2,1)S(1)}, u32[]{:S(2)}, u32[]{:S(2)}) collective-permute-start(bf16[32,1152]{1,0:T(8,128)(2,1)} %get-tuple-element.35), channel_id=1, source_target_pairs={{0,64},{1,128},{2,66},{3,130},{64,65},{65,129},{66,67},{67,131},{1... | collective-permute-start | bytes 221192 | tf_op jit(solution)/shard_map/ppermute | solution.py:440
  145.6 1.1 collective-permute-start.16
  146.7 2.7 %collective-permute-start.17 = (bf16[32,1152]{1,0:T(8,128)(2,1)}, bf16[32,1152]{1,0:T(8,128)(2,1)S(1)}, u32[]{:S(2)}, u32[]{:S(2)}) collective-permute-start(bf16[32,1152]{1,0:T(8,128)(2,1)} %get-tuple-element.37), channel_id=1, source_target_pairs={{0,192},{1,0},{2,194},{3,2},{64,193},{65,1},{66,195},{67,3},{128,6... | collective-permute-start | bytes 221192 | tf_op jit(solution)/shard_map/ppermute | solution.py:440
  149.3 0.8 collective-permute-done.15.refs_1_
  150.1 3.7 %collective-permute-done.16.refs_2_ = bf16[32,1152]{1,0:T(8,128)(2,1)S(1)} collective-permute-done((bf16[32,1152]{1,0:T(8,128)(2,1)}, bf16[32,1152]{1,0:T(8,128)(2,1)S(1)}, u32[]{:S(2)}, u32[]{:S(2)}) %collective-permute-start.16) | collective-permute-done | bytes 73760 | tf_op jit(solution)/shard_map/ppermute | solution.py:440
  154.5 0.6 copy-done.20
  155.1 1.8 %place.1 = (bf16[64,2048]{1,0:T(8,128)(2,1)}, bf16[2,2,2048]{2,1,0:T(2,128)(2,1)}) custom-call(s32[6]{0:T(128)} %stack.33.refs_0_.core, bf16[32,1152]{1,0:T(8,128)(2,1)} %copy-done.17, bf16[32,1152]{1,0:T(8,128)(2,1)} %copy-done.18, bf16[32,1152]{1,0:T(8,128)(2,1)} %copy-done.19, bf16[32,1152]{1,0:T(8,128)(2,1)} %copy-done.20), custom_call_target="tpu_custom_call" | custom-call | tf_op jit(solution)/shard_map/place/pallas_call | solution.py:40
  (97 shorter events, 6.1 us)
Async XLA Ops:
  0.6 11.0 %copy-start.22 = (bf16[128,256]{1,0:T(8,128)(2,1)S(1)}, bf16[128,256]{1,0:T(8,128)(2,1)}, u32[]{:S(2)}) copy-start(bf16[128,256]{1,0:T(8,128)(2,1)} %param.21) | copy-start | bytes 196612
  0.6 11.0 %copy-start.23 = (bf16[128,256]{1,0:T(8,128)(2,1)S(1)}, bf16[128,256]{1,0:T(8,128)(2,1)}, u32[]{:S(2)}) copy-start(bf16[128,256]{1,0:T(8,128)(2,1)} %param.22) | copy-start | bytes 196612
  0.7 11.4 %copy-start.26 = (s32[128,2]{0,1:T(2,128)S(1)}, s32[128,2]{0,1:T(2,128)}, u32[]{:S(2)}) copy-start(s32[128,2]{0,1:T(2,128)} %param.23) | copy-start | bytes 3076
  0.7 12.0 %copy-start.7 = (bf16[128,2048]{1,0:T(8,128)(2,1)S(1)}, bf16[128,2048]{1,0:T(8,128)(2,1)}, u32[]{:S(2)}) copy-start(bf16[128,2048]{1,0:T(8,128)(2,1)} %param.20) | copy-start | bytes 1572868
  2.6 25.5 %all-to-all-start = ((bf16[8,112,256]{2,1,0:T(8,128)(2,1)}), bf16[8,112,256]{2,1,0:T(8,128)(2,1)S(1)}, u32[]{:S(2)}, u32[]{:S(2)}) async-start(bf16[8,112,256]{2,1,0:T(8,128)(2,1)} %pack.1), calls=%async_computation | async-start | bytes 917504 | tf_op jit(solution)/shard_map/all_to_all | solution.py:317
  28.1 28.3 %copy-start.1 = (bf16[8,112,256]{2,1,0:T(8,128)(2,1)}, bf16[8,112,256]{2,1,0:T(8,128)(2,1)S(1)}, u32[]{:S(2)}) copy-start(bf16[8,112,256]{2,1,0:T(8,128)(2,1)S(1)} %all-to-all-done.refs_3_) | copy-start | bytes 1376260
  28.9 11.0 %all-to-all-start.1 = ((bf16[4,4,48,256]{3,2,1,0:T(8,128)(2,1)}), bf16[4,4,48,256]{3,2,1,0:T(8,128)(2,1)S(1)}, u32[]{:S(2)}, u32[]{:S(2)}) async-start(bf16[4,4,48,256]{3,2,1,0:T(8,128)(2,1)} %broadcast_in_dim.11), calls=%async_computation.1 | async-start | bytes 786432 | tf_op jit(solution)/shard_map/all_to_all | solution.py:342
  37.2 20.4 %copy-start.25 = (s32[4096]{0:T(1024)S(1)}, s32[4096]{0:T(1024)}, u32[]{:S(2)}) copy-start(s32[4096]{0:T(1024)} %param.16) | copy-start | bytes 49156
  39.9 40.1 %copy-start.2 = (bf16[4,4,48,256]{3,2,1,0:T(8,128)(2,1)}, bf16[4,4,48,256]{3,2,1,0:T(8,128)(2,1)S(1)}, u32[]{:S(2)}) copy-start(bf16[4,4,48,256]{3,2,1,0:T(8,128)(2,1)S(1)} %all-to-all-done.1.refs_5_.refs_0_) | copy-start | bytes 1179652
  40.7 10.6 %all-to-all-start.3 = ((bf16[4,256,128]{2,1,0:T(8,128)(2,1)}), bf16[4,256,128]{2,1,0:T(8,128)(2,1)S(1)}, u32[]{:S(2)}, u32[]{:S(2)}) async-start(bf16[4,256,128]{2,1,0:T(8,128)(2,1)} %broadcast_in_dim.13), calls=%async_computation.3 | async-start | bytes 524288 | tf_op jit(solution)/shard_map/all_to_all | solution.py:365
  46.2 12.7 %copy-start.27 = (s32[128]{0:T(128)S(1)}, s32[128]{0:T(128)}, u32[]{:S(2)}) copy-start(s32[128]{0:T(128)} %param.24) | copy-start | bytes 1540
  46.2 43.9 %collective-permute-start.5 = (bf16[4,4,48,256]{3,2,1,0:T(8,128)(2,1)S(1)}, bf16[4,4,48,256]{3,2,1,0:T(8,128)(2,1)S(1)}, u32[]{:S(2)}, u32[]{:S(2)}) collective-permute-start(bf16[4,4,48,256]{3,2,1,0:T(8,128)(2,1)S(1)} %all-to-all-done.1.refs_5_.refs_0_), channel_id=1, source_target_pairs={{0,8},{4,12},{8,0},{12,4},{1,9},{5,13},{9,1},{13,5},{2,10},{6,14},... | collective-permute-start | bytes 1179656 | tf_op jit(solution)/shard_map/ppermute | solution.py:347
  49.1 11.5 %collective-permute-start.8 = (bf16[128,640]{1,0:T(8,128)(2,1)S(1)}, bf16[128,640]{1,0:T(8,128)(2,1)S(1)}, u32[]{:S(2)}, u32[]{:S(2)}) collective-permute-start(bf16[128,640]{1,0:T(8,128)(2,1)S(1)} %get-tuple-element.25), channel_id=1, source_target_pairs={{0,0},{1,64},{64,1},{65,65},{128,128},{129,192},{192,129},{193,193... | collective-permute-start | bytes 491528 | tf_op jit(solution)/shard_map/ppermute | solution.py:338
  51.3 7.9 %copy-start.4 = (bf16[4,256,128]{2,1,0:T(8,128)(2,1)}, bf16[4,256,128]{2,1,0:T(8,128)(2,1)S(1)}, u32[]{:S(2)}) copy-start(bf16[4,256,128]{2,1,0:T(8,128)(2,1)S(1)} %all-to-all-done.3.looked) | copy-start | bytes 786436
  52.2 27.9 %all-to-all-start.2 = ((bf16[4,4,48,256]{3,2,1,0:T(8,128)(2,1)}), bf16[4,4,48,256]{3,2,1,0:T(8,128)(2,1)S(1)}, u32[]{:S(2)}, u32[]{:S(2)}) async-start(bf16[4,4,48,256]{3,2,1,0:T(8,128)(2,1)} %broadcast_in_dim.12), calls=%async_computation.2 | async-start | bytes 786432 | tf_op jit(solution)/shard_map/all_to_all | solution.py:343
  56.4 31.3 %collective-permute-start = (bf16[8,64,256]{2,1,0:T(8,128)(2,1)S(1)}, bf16[8,64,256]{2,1,0:T(8,128)(2,1)}, u32[]{:S(2)}, u32[]{:S(2)}) collective-permute-start(bf16[8,64,256]{2,1,0:T(8,128)(2,1)S(1)} %slice.17), channel_id=1, source_target_pairs={{0,1},{1,0},{2,3},{3,2},{4,5},{5,4},{6,7},{7,6},{8,9},{9,8},{10,11... | collective-permute-start | bytes 786440 | tf_op jit(solution)/shard_map/ppermute | solution.py:349
  60.0 4.8 %collective-permute-start.9 = (bf16[128,640]{1,0:T(8,128)(2,1)S(1)}, bf16[128,640]{1,0:T(8,128)(2,1)S(1)}, u32[]{:S(2)}, u32[]{:S(2)}) collective-permute-start(bf16[128,640]{1,0:T(8,128)(2,1)S(1)} %get-tuple-element.26), channel_id=1, source_target_pairs={{0,1},{1,65},{64,0},{65,64},{128,129},{129,193},{192,128},{193,192... | collective-permute-start | bytes 491528 | tf_op jit(solution)/shard_map/ppermute | solution.py:338
  60.6 12.2 %collective-permute-start.10 = (bf16[128,640]{1,0:T(8,128)(2,1)S(1)}, bf16[128,640]{1,0:T(8,128)(2,1)S(1)}, u32[]{:S(2)}, u32[]{:S(2)}) collective-permute-start(bf16[128,640]{1,0:T(8,128)(2,1)S(1)} %get-tuple-element.27), channel_id=1, source_target_pairs={{0,128},{1,192},{64,129},{65,193},{128,0},{129,64},{192,1},{193,65... | collective-permute-start | bytes 491528 | tf_op jit(solution)/shard_map/ppermute | solution.py:338
  60.6 36.6 %copy-start.13 = (bf16[128,640]{1,0:T(8,128)(2,1)}, bf16[128,640]{1,0:T(8,128)(2,1)S(1)}, u32[]{:S(2)}) copy-start(bf16[128,640]{1,0:T(8,128)(2,1)S(1)} %collective-permute-done.8.refs_0_) | copy-start | bytes 491524
  60.6 14.5 %collective-permute-start.11 = (bf16[128,640]{1,0:T(8,128)(2,1)S(1)}, bf16[128,640]{1,0:T(8,128)(2,1)S(1)}, u32[]{:S(2)}, u32[]{:S(2)}) collective-permute-start(bf16[128,640]{1,0:T(8,128)(2,1)S(1)} %get-tuple-element.28), channel_id=1, source_target_pairs={{0,129},{1,193},{64,128},{65,192},{128,1},{129,65},{192,0},{193,64... | collective-permute-start | bytes 491528 | tf_op jit(solution)/shard_map/ppermute | solution.py:338
  64.8 10.4 %copy-start.14 = (bf16[128,640]{1,0:T(8,128)(2,1)}, bf16[128,640]{1,0:T(8,128)(2,1)S(1)}, u32[]{:S(2)}) copy-start(bf16[128,640]{1,0:T(8,128)(2,1)S(1)} %collective-permute-done.9.refs_1_) | copy-start | bytes 491524
  72.8 2.4 %copy-start.15 = (bf16[128,640]{1,0:T(8,128)(2,1)}, bf16[128,640]{1,0:T(8,128)(2,1)S(1)}, u32[]{:S(2)}) copy-start(bf16[128,640]{1,0:T(8,128)(2,1)S(1)} %collective-permute-done.10.refs_2_) | copy-start | bytes 491524
  75.1 22.0 %copy-start.16 = (bf16[128,640]{1,0:T(8,128)(2,1)}, bf16[128,640]{1,0:T(8,128)(2,1)S(1)}, u32[]{:S(2)}) copy-start(bf16[128,640]{1,0:T(8,128)(2,1)S(1)} %collective-permute-done.11.refs_3_) | copy-start | bytes 491524
  77.1 30.1 %collective-permute-start.3 = (bf16[4,4,48,256]{3,2,1,0:T(8,128)(2,1)S(1)}, bf16[4,4,48,256]{3,2,1,0:T(8,128)(2,1)S(1)}, u32[]{:S(2)}, u32[]{:S(2)}) collective-permute-start(bf16[4,4,48,256]{3,2,1,0:T(8,128)(2,1)S(1)} %all-to-all-done.1.refs_5_.refs_0_), channel_id=1, source_target_pairs={{0,12},{4,0},{8,4},{12,8},{1,13},{5,1},{9,5},{13,9},{2,14},{6,2},{... | collective-permute-start | bytes 1179656 | tf_op jit(solution)/shard_map/ppermute | solution.py:347
  80.0 27.2 %collective-permute-start.1 = (bf16[4,4,48,256]{3,2,1,0:T(8,128)(2,1)S(1)}, bf16[4,4,48,256]{3,2,1,0:T(8,128)(2,1)S(1)}, u32[]{:S(2)}, u32[]{:S(2)}) collective-permute-start(bf16[4,4,48,256]{3,2,1,0:T(8,128)(2,1)S(1)} %all-to-all-done.1.refs_5_.refs_0_), channel_id=1, source_target_pairs={{0,4},{4,8},{8,12},{12,0},{1,5},{5,9},{9,13},{13,1},{2,6},{6,10},{... | collective-permute-start | bytes 1179656 | tf_op jit(solution)/shard_map/ppermute | solution.py:347
  80.1 10.7 %copy-start.3 = (bf16[4,4,48,256]{3,2,1,0:T(8,128)(2,1)}, bf16[4,4,48,256]{3,2,1,0:T(8,128)(2,1)S(1)}, u32[]{:S(2)}) copy-start(bf16[4,4,48,256]{3,2,1,0:T(8,128)(2,1)S(1)} %all-to-all-done.2.refs_6_.refs_1_) | copy-start | bytes 1179652
  80.1 17.2 %all-to-all-start.4 = ((bf16[4,256,128]{2,1,0:T(8,128)(2,1)}), bf16[4,256,128]{2,1,0:T(8,128)(2,1)S(1)}, u32[]{:S(2)}, u32[]{:S(2)}) async-start(bf16[4,256,128]{2,1,0:T(8,128)(2,1)} %hidden.1), calls=%async_computation.4 | async-start | bytes 524288 | tf_op jit(solution)/shard_map/all_to_all | solution.py:376
  87.4 19.9 %collective-permute-start.6 = (bf16[4,4,48,256]{3,2,1,0:T(8,128)(2,1)S(1)}, bf16[4,4,48,256]{3,2,1,0:T(8,128)(2,1)S(1)}, u32[]{:S(2)}, u32[]{:S(2)}) collective-permute-start(bf16[4,4,48,256]{3,2,1,0:T(8,128)(2,1)S(1)} %all-to-all-done.2.refs_6_.refs_1_), channel_id=1, source_target_pairs={{0,32},{16,48},{32,0},{48,16},{1,33},{17,49},{33,1},{49,17},{2,34}... | collective-permute-start | bytes 1179656 | tf_op jit(solution)/shard_map/ppermute | solution.py:348
  87.7 19.6 %collective-permute-start.4 = (bf16[4,4,48,256]{3,2,1,0:T(8,128)(2,1)S(1)}, bf16[4,4,48,256]{3,2,1,0:T(8,128)(2,1)S(1)}, u32[]{:S(2)}, u32[]{:S(2)}) collective-permute-start(bf16[4,4,48,256]{3,2,1,0:T(8,128)(2,1)S(1)} %all-to-all-done.2.refs_6_.refs_1_), channel_id=1, source_target_pairs={{0,48},{16,0},{32,16},{48,32},{1,49},{17,1},{33,17},{49,33},{2,50}... | collective-permute-start | bytes 1179656 | tf_op jit(solution)/shard_map/ppermute | solution.py:348
  90.1 7.1 %copy-start.8 = (bf16[4,4,48,256]{3,2,1,0:T(8,128)(2,1)}, bf16[4,4,48,256]{3,2,1,0:T(8,128)(2,1)S(1)}, u32[]{:S(2)}) copy-start(bf16[4,4,48,256]{3,2,1,0:T(8,128)(2,1)S(1)} %collective-permute-done.5.refs_11_.refs_6_) | copy-start | bytes 1179652
  90.1 18.4 %collective-permute-start.2 = (bf16[4,4,48,256]{3,2,1,0:T(8,128)(2,1)S(1)}, bf16[4,4,48,256]{3,2,1,0:T(8,128)(2,1)}, u32[]{:S(2)}, u32[]{:S(2)}) collective-permute-start(bf16[4,4,48,256]{3,2,1,0:T(8,128)(2,1)S(1)} %all-to-all-done.2.refs_6_.refs_1_), channel_id=1, source_target_pairs={{0,16},{16,32},{32,48},{48,0},{1,17},{17,33},{33,49},{49,1},{2,18}... | collective-permute-start | bytes 1179656 | tf_op jit(solution)/shard_map/ppermute | solution.py:348
  97.3 0.7 copy-start.5
  101.0 24.0 %all-to-all-start.5 = ((f32[16,88,128]{2,1,0:T(8,128)}), f32[16,88,128]{2,1,0:T(8,128)S(1)}, u32[]{:S(2)}, u32[]{:S(2)}) async-start(f32[16,88,128]{2,1,0:T(8,128)} %project.1), calls=%async_computation.5 | async-start | bytes 1441792 | tf_op jit(solution)/shard_map/all_to_all | solution.py:391
  107.3 1.2 copy-start.9
  107.3 1.2 copy-start.10
  107.3 1.2 copy-start.11
  107.3 1.1 copy-start.12
  123.6 10.2 %collective-permute-start.7 = (f32[1040,128]{1,0:T(8,128)}, f32[1040,128]{1,0:T(8,128)S(1)}, u32[]{:S(2)}, u32[]{:S(2)}) collective-permute-start(f32[1040,128]{1,0:T(8,128)} %get-tuple-element.24), channel_id=1, source_target_pairs={{0,1},{1,0},{2,3},{3,2},{4,5},{5,4},{6,7},{7,6},{8,9},{9,8},{10,11... | collective-permute-start | bytes 1597448 | tf_op jit(solution)/shard_map/ppermute | solution.py:411
  125.1 0.9 copy-start
  127.7 1.4 collective-permute-start.12
  133.6 1.5 collective-permute-start.13
  133.8 1.3 copy-start.6
  138.4 11.0 %collective-permute-start.14 = (bf16[32,1152]{1,0:T(8,128)(2,1)}, bf16[32,1152]{1,0:T(8,128)(2,1)S(1)}, u32[]{:S(2)}, u32[]{:S(2)}) collective-permute-start(bf16[32,1152]{1,0:T(8,128)(2,1)} %get-tuple-element.34), channel_id=1, source_target_pairs={{0,0},{1,64},{2,2},{3,66},{64,1},{65,65},{66,3},{67,67},{128,128},... | collective-permute-start | bytes 221192 | tf_op jit(solution)/shard_map/ppermute | solution.py:440
  142.9 7.2 %collective-permute-start.15 = (bf16[32,1152]{1,0:T(8,128)(2,1)}, bf16[32,1152]{1,0:T(8,128)(2,1)S(1)}, u32[]{:S(2)}, u32[]{:S(2)}) collective-permute-start(bf16[32,1152]{1,0:T(8,128)(2,1)} %get-tuple-element.35), channel_id=1, source_target_pairs={{0,64},{1,128},{2,66},{3,130},{64,65},{65,129},{66,67},{67,131},{1... | collective-permute-start | bytes 221192 | tf_op jit(solution)/shard_map/ppermute | solution.py:440
  145.6 8.3 %collective-permute-start.16 = (bf16[32,1152]{1,0:T(8,128)(2,1)}, bf16[32,1152]{1,0:T(8,128)(2,1)S(1)}, u32[]{:S(2)}, u32[]{:S(2)}) collective-permute-start(bf16[32,1152]{1,0:T(8,128)(2,1)} %get-tuple-element.36), channel_id=1, source_target_pairs={{0,128},{1,192},{2,130},{3,194},{64,129},{65,193},{66,131},{67,195... | collective-permute-start | bytes 221192 | tf_op jit(solution)/shard_map/ppermute | solution.py:440
  146.7 7.2 %collective-permute-start.17 = (bf16[32,1152]{1,0:T(8,128)(2,1)}, bf16[32,1152]{1,0:T(8,128)(2,1)S(1)}, u32[]{:S(2)}, u32[]{:S(2)}) collective-permute-start(bf16[32,1152]{1,0:T(8,128)(2,1)} %get-tuple-element.37), channel_id=1, source_target_pairs={{0,192},{1,0},{2,194},{3,2},{64,193},{65,1},{66,195},{67,3},{128,6... | collective-permute-start | bytes 221192 | tf_op jit(solution)/shard_map/ppermute | solution.py:440
  149.3 4.6 %copy-start.17 = (bf16[32,1152]{1,0:T(8,128)(2,1)}, bf16[32,1152]{1,0:T(8,128)(2,1)S(1)}, u32[]{:S(2)}) copy-start(bf16[32,1152]{1,0:T(8,128)(2,1)S(1)} %collective-permute-done.14.refs_0_) | copy-start | bytes 221188
  150.1 3.8 %copy-start.18 = (bf16[32,1152]{1,0:T(8,128)(2,1)}, bf16[32,1152]{1,0:T(8,128)(2,1)S(1)}, u32[]{:S(2)}) copy-start(bf16[32,1152]{1,0:T(8,128)(2,1)S(1)} %collective-permute-done.15.refs_1_) | copy-start | bytes 221188
  (4 other events, 2.5 us)

commit v4 on v3

--- a/solution.py
+++ b/solution.py
@@ -20,7 +20,6 @@
 TOKENS = 8 * NEW
 BEAMS = 8
 TILES = 11 * BEAMS
-SHIFTS = (1, 3, 2)
 MESSAGE = WIDTH + HEAD
 VMEM = pltpu.CompilerParams(vmem_limit_bytes=56 * 1024 * 1024)
 SMEM_SPEC = pl.BlockSpec(memory_space=pltpu.SMEM)
@@ -75,16 +74,15 @@
         out[part] = rows
 
 
-def project_kernel(first, parent, beam_id, hidden, *refs):
-    weights, (out, total, extra) = refs[:4], refs[4:]
+def project_kernel(parent, beam_id, hidden, weights, out, total, extra):
     beams = extra.shape[0]
     pick = jnp.where(parent[...] == beam_id[...], 1.0, 0.0).astype(BF16)
     acc = acc_extra = 0.0
     for k in range(4):
-        rows = hidden[first[0] ^ k]
-        acc = acc + dot_nn(rows, weights[k][...])
+        rows = hidden[k]
+        acc = acc + dot_nn(rows, weights[k])
         chosen = dot_nn(pick, rows[:beams]).astype(BF16)
-        acc_extra = acc_extra + dot_nn(chosen, weights[k][:, 4 * HEAD :])
+        acc_extra = acc_extra + dot_nn(chosen, weights[k, :, 4 * HEAD :])
     total[...] = acc
     extra[...] = acc_extra
     for chip in range(16):
@@ -152,11 +150,11 @@
     return spread(ref, at), spread(ref, at + slots), ref[slot * TOKENS : (slot + 1) * TOKENS, :]
 
 
-def attend_kernel(shifts, resumed, core, pos, lines, own, other, *refs):
+def attend_kernel(starts, resumed, core, pos, lines, own, other, *refs):
     if resumed:
         states, refs = refs[:2], refs[2:]
     kv, (keep, send) = refs[:-2], refs[-2:]
-    me, place, xi, yi = core[0], core[1], core[4], core[5]
+    me, place = core[0], core[1]
 
     def column(which):
         row = pos[pl.ds(which * 16 + place, 1), :].astype(F32)
@@ -167,12 +165,12 @@
 
     def scores(step, block):
         if step not in loaded:
-            back = 4 - shifts[step]
-            a = lines[pl.ds(me * 4 + (yi + back) % 4, 1), :]
-            b = lines[pl.ds(8 + me * 4 + (xi + back) % 4, 1), :]
-            kpos = jnp.concatenate([a, b], 1).astype(F32)
+            first, part, line = starts[step]
+            kpos = jnp.concatenate([lines[line : line + 1], lines[4 + line : 5 + line]], 1)
+            kpos = kpos.astype(F32)
             bias = [jnp.where(kpos <= p, 0.0, HIDE) for p in qpos]
-            loaded[step] = (load_lines(kv[2 * step : 2 * step + 2]), bias)
+            pair = [r.at[4 * part : 4 * part + 4] for r in kv[first : first + 2]]
+            loaded[step] = (load_lines(pair), bias)
         wide, bias = loaded[step]
         head = block % GROUP
         lanes = slice((head % 2) * HEAD, (head % 2 + 1) * HEAD)
@@ -185,7 +183,7 @@
         return dot_nt(q, wide[0][0]), dot_nt(q, wide[1][0]) + bias[block // GROUP]
 
     state = {}
-    order = [(step, block) for step in range(len(shifts)) for block in range(2 * GROUP)]
+    order = [(step, block) for step in range(len(starts)) for block in range(2 * GROUP)]
     ahead = scores(*order[0])
     for i, (step, block) in enumerate(order):
         now = ahead
@@ -194,7 +192,7 @@
         if step == 0:
             state[block] = get_state(states[block // GROUP], block % GROUP, GROUP) if resumed else None
         state[block] = absorb(state[block], now, loaded[step][0])
-        if step == len(shifts) - 1:
+        if step == len(starts) - 1:
             put_state((keep, send)[block // GROUP], block % GROUP, GROUP, state[block])
 
 
@@ -204,13 +202,17 @@
     halves = [jnp.where(me == 0, mine[...], theirs[...]), jnp.where(me == 0, theirs[...], mine[...])]
     queries = jnp.concatenate([h[: 8 * BEAMS] for h in halves], 0).astype(BF16)
     state = None
-    steps = len(kv) // 2
-    wide = load_lines(kv[:2])
+    pairs = []
+    for i in range(0, len(kv), 2):
+        for part in range(kv[i].shape[0] // 4):
+            pairs.append([r.at[4 * part : 4 * part + 4] for r in kv[i : i + 2]])
+    steps = len(pairs)
+    wide = load_lines(pairs[0])
     ahead = [dot_nt(queries, k) for k, _ in wide]
     for step in range(steps):
         now, now_wide = ahead, wide
         if step + 1 < steps:
-            wide = load_lines(kv[2 * step + 2 : 2 * step + 4])
+            wide = load_lines(pairs[step + 1])
             ahead = [dot_nt(queries, k) for k, _ in wide]
         state = absorb(state, now, now_wide)
 
@@ -305,7 +307,7 @@
     parent_beam,
 ):
     zh, xi, yi, ci = (lax.axis_index(a) for a in ("zh", "x", "y", "c"))
-    core = jnp.stack([ci, xi * 4 + yi, 2 * (zh // 2) + ci, zh, xi, yi]).astype(jnp.int32)
+    core = jnp.stack([ci, xi * 4 + yi, 2 * (zh // 2) + ci, zh]).astype(jnp.int32)
 
     packed = call(
         pack_kernel,
@@ -326,46 +328,53 @@
         -1,
     )
     parts = jnp.transpose(parts, (1, 2, 0, 3)).reshape(4, depth, q_cols + HEAD)
-    mine = [lax.dynamic_index_in_dim(parts, zh ^ k, 0, keepdims=False) for k in range(4)]
-    packed, mine = lax.optimization_barrier((packed, mine))
-    weights = []
-    for k in range(4):
+    weights = lax.all_to_all(parts, "x", split_axis=0, concat_axis=0, tiled=True)
+    packed, weights = lax.optimization_barrier((packed, weights))
+
+    def swap(v, axis, turn):
         pairs = []
         for at in range(8):
-            h, c = at // 2, at % 2
-            to = h ^ k
-            pairs.append((at, (2 * (to // 2) + c) * 2 + to % 2))
-        weights.append(lax.ppermute(mine[k], ("zh", "c"), pairs))
-
-    line_a = jnp.broadcast_to(packed[:4, :BOTH], (4, 4, BOTH, 2 * HEAD))
-    line_b = jnp.broadcast_to(packed[4:, :BOTH], (4, 4, BOTH, 2 * HEAD))
-    line_a = lax.all_to_all(line_a, "x", split_axis=0, concat_axis=0, tiled=True)
-    line_b = lax.all_to_all(line_b, "y", split_axis=0, concat_axis=0, tiled=True)
-    lines = [line_a, line_b]
-    for k in SHIFTS:
-        pairs = [(i, (i + k) % 4) for i in range(4)]
-        lines.append(lax.ppermute(line_a, "y", pairs))
-        lines.append(lax.ppermute(line_b, "x", pairs))
+            i, c = at // 2, at % 2
+            pairs.append((at, (i ^ (1 if c == turn else 3)) * 2 + c))
+        return lax.ppermute(v, (axis, "c"), pairs)
+
+    halves = [packed[:4, :BOTH][None], packed[4:, :BOTH][None]]
+    near = []
+    for half, axis in zip(halves, ("x", "y")):
+        half = jnp.concatenate([half, swap(half, axis, 0)], 0)
+        near.append(jnp.concatenate([half, swap(half, axis, 1)], 0))
+    far = [swap(line, axis, 0) for line, axis in zip(near, ("y", "x"))]
+    both = [jnp.concatenate(pair, 0) for pair in zip(near, far)]
+    rest = [swap(line, axis, 1) for line, axis in zip(both, ("y", "x"))]
     q_other = lax.ppermute(packed[:, BOTH:], "c", [(0, 1), (1, 0)])
 
     pos = jnp.transpose(stretch_pos.reshape(4, 4, 4, 2, 2, NEW), (4, 1, 2, 0, 3, 5))
-    halves = pos.reshape(2, 4, 4, 2, TOKENS // 2)
+    halves = lax.dynamic_index_in_dim(pos.reshape(2, 4, 4, 2, TOKENS // 2), ci, 0, keepdims=False)
     pos = pos.reshape(32, TOKENS)
-    line_pos = jnp.stack(
+
+    def met(table, axis, index):
+        table = jnp.moveaxis(table, axis, 0)
+        table = jnp.where(index % 2 == 1, jnp.concatenate([table[1:2], table[:1], table[3:], table[2:3]], 0), table)
+        table = jnp.where(index // 2 == 1, jnp.concatenate([table[2:], table[:2]], 0), table)
+        one, three = jnp.where(ci == 0, table[1], table[3]), jnp.where(ci == 0, table[3], table[1])
+        return jnp.moveaxis(jnp.stack([table[0], one, three, table[2]]), 0, axis)
+
+    halves = met(met(halves, 0, xi), 1, yi)
+    line_pos = jnp.concatenate(
         [
-            jnp.transpose(halves[:, :, :, 0], (0, 2, 1, 3)).reshape(8, 2 * TOKENS),
-            halves[:, :, :, 1].reshape(8, 2 * TOKENS),
-        ]
-    ).reshape(16, 2 * TOKENS)
+            jnp.transpose(halves[:, :, 0], (1, 0, 2)).reshape(4, 2 * TOKENS),
+            halves[:, :, 1].reshape(4, 2 * TOKENS),
+        ],
+        0,
+    )
 
     vocab_rows = embed_table.shape[0]
     beams = beam_tokens.shape[0]
-    ids = jnp.transpose(beam_tokens.reshape(4, 4, 4, 2, 2), (4, 2, 1, 3, 0)).reshape(-1)
+    ids = jnp.transpose(beam_tokens.reshape(4, 4, 4, 2, 2), (4, 1, 2, 3, 0)).reshape(-1)
     looked = embed_table.at[ids % vocab_rows].get(mode="promise_in_bounds")
     looked = lax.all_to_all(
         jnp.broadcast_to(looked, (4,) + looked.shape), GRP, split_axis=0, concat_axis=0, tiled=True
     )
-    looked, weights = lax.optimization_barrier((looked, weights))
     hidden = call(
         hidden_kernel,
         jax.ShapeDtypeStruct((4, 2 * beams, HEAD), BF16),
@@ -373,30 +382,37 @@
         ((ids // vocab_rows)[:, None], looked),
         "hidden",
     )
-    hidden = lax.all_to_all(hidden, "zh", split_axis=0, concat_axis=0, tiled=True)
-
-    beam_id = np.arange(beams, dtype=np.int32).reshape(4, 4, 4, 2).transpose(2, 1, 3, 0)
-    parent = jnp.transpose(parent_beam.reshape(4, 4, 4, 2), (2, 1, 3, 0))
+    hidden = lax.all_to_all(hidden, "x", split_axis=0, concat_axis=0, tiled=True)
+
+    beam_id = np.arange(beams, dtype=np.int32).reshape(4, 4, 4, 2).transpose(1, 2, 3, 0)
+    parent = jnp.transpose(parent_beam.reshape(4, 4, 4, 2), (1, 2, 3, 0))
     part = call(
         project_kernel,
         jax.ShapeDtypeStruct((16, TILES, HEAD), F32),
-        (core[2:3],),
-        (parent.reshape(-1, 1), beam_id.reshape(1, -1), hidden, *weights),
+        (),
+        (parent.reshape(-1, 1), beam_id.reshape(1, -1), hidden, weights),
         "project",
         scratch=[
             pltpu.VMEM((2 * beams, q_cols + HEAD), F32),
             pltpu.VMEM((beams, HEAD), F32),
         ],
     )
-    part = lax.all_to_all(part, ("y", "x"), split_axis=0, concat_axis=0, tiled=True)
-    mine = call(sum_kernel, jax.ShapeDtypeStruct((TILES, HEAD), F32), (), (part,), "sum")
-    theirs = lax.ppermute(mine, "c", [(0, 1), (1, 0)])
-
-    def attend(shifts, carry, pieces, name):
-        work = 2 * GROUP * TOKENS * len(shifts) * 32 * BOTH
+    part = lax.all_to_all(part, ("zh", "y"), split_axis=0, concat_axis=0, tiled=True)
+    part = call(sum_kernel, jax.ShapeDtypeStruct((TILES, HEAD), F32), (), (part,), "sum")
+    sides = []
+    for i in range(2):
+        pairs = []
+        for at in range(64):
+            h, j, p, l, c = at >> 4, (at >> 3) & 1, (at >> 2) & 1, (at >> 1) & 1, at & 1
+            pairs.append((at, (((2 * j + c) * 4 + h) * 2 + l) * 2 + (p ^ i)))
+        sides.append(lax.ppermute(part, ("zh", "x", "zl", "c"), pairs))
+    mine, theirs = sides
+
+    def attend(starts, carry, pieces, name):
+        work = 2 * GROUP * TOKENS * len(starts) * 32 * BOTH
         state = jax.ShapeDtypeStruct((GROUP * (TOKENS + 2), HEAD), F32)
         return call(
-            lambda *refs: attend_kernel(shifts, bool(carry), *refs),
+            lambda *refs: attend_kernel(starts, bool(carry), *refs),
             (state, state),
             (core,),
             (pos, line_pos, packed, q_other, *carry, *pieces),
@@ -406,14 +422,15 @@
             ),
         )
 
-    carry = attend((0,), (), lines[:2], "attend_near")
-    keep, send = attend(SHIFTS, carry, lines[2:], "attend_far")
+    carry = attend(((0, 0, 0),), (), near, "attend_near")
+    carry = attend(((0, 0, 1),), carry, far, "attend_far")
+    keep, send = attend(((0, 0, 2), (0, 1, 3)), carry, rest, "attend_rest")
     got = lax.ppermute(send, "c", [(0, 1), (1, 0)])
     beams_keep = call(
         decode_kernel,
         jax.ShapeDtypeStruct((TOKENS + 8, HEAD), F32),
         (core,),
-        (mine, theirs, *lines),
+        (mine, theirs, *near, *far, *rest),
         "decode",
         cost=pl.CostEstimate(
             flops=8 * TOKENS * 128 * BOTH * HEAD,

time: 158 us -> 160 us (1.013); the launches traced: 157 us -> 157 us
  waiting for transfers between devices: 36.2 us -> 32.8 us
  starting transfers between devices: 64.3 us -> 61 us
  Pallas kernels: 38.5 us -> 41.4 us
  local copies, waits for them, and re-layouts: 14.6 us -> 16.6 us
  other arithmetic: 2.25 us -> 4.23 us
    all_to_all x4 -> x3, starting transfers between devices: 21.7 us -> 12.2 us  [the longest x1 4.97 us: shards(): lax.all_to_all(parts, 'x', split_axis=0, concat_axis=0, tiled=True)]
    ppermute x4, starting transfers between devices: 11 us -> 15.7 us  [shards(): got.append(lax.ppermute(messages[k], ('zh', 'zl', 'c'), pairs))]
    pallas_call x9 -> x10, Pallas kernels: 38.5 us -> 41.4 us  [call(): pl.pallas_call(kernel, out_shape=out_shape, in_specs=[SMEM_SPEC] * len(sc...]
    concatenate x0 -> x8, other arithmetic: none -> 2.74 us  [the longest x2 1.09 us: shards(): both = [jnp.concatenate(pair, 0) for pair in zip(near, far)]]
    unnamed x56 -> x42, local copies, waits for them, and re-layouts: 4.15 us -> 5.87 us
    broadcast_in_dim x2 -> x1, local copies, waits for them, and re-layouts: 1.66 us -> 0.01 us  [shards(): halves = [packed[:4, :BOTH][None], packed[4:, :BOTH][None]]]
    ppermute x11 -> x10, starting transfers between devices: 14.3 us -> 13 us  [the longest x8 8.82 us: swap(): return lax.ppermute(v, (axis, 'c'), pairs)]
    ppermute x11 -> x10, waiting for transfers between devices: 12.9 us -> 11.7 us  [the longest x8 8.15 us: swap(): return lax.ppermute(v, (axis, 'c'), pairs)]
  transfers between devices with their start and end apart: 24 -> 22, of which waited for: 11 -> 8; matrix products, arithmetic and copies ran while one was open for 7% -> 6% of each run, Pallas kernels for 21% -> 24%
where the time goes in v4:
time: 160 us; the launch traced here: 157 us
  starting transfers between devices  61 us (38%)
  Pallas kernels  41.4 us (26%)
  waiting for transfers between devices  32.8 us (20%)
  local copies, waits for them, and re-layouts  16.6 us (10%)
  other arithmetic  4.23 us (3%)
    pallas_call x10, Pallas kernels, call(): pl.pallas_call(kernel, out_shape=out_shape, in_specs=[SMEM_SPEC] * len(sc...  41.4 us
    ppermute x4, starting transfers between devices, shards(): got.append(lax.ppermute(messages[k], ('zh', 'zl', 'c'), pairs))  15.7 us
    all_to_all x1, waiting for transfers between devices, shards(): lax.all_to_all(packed, DEPTH, split_axis=0, concat_axis=0, tiled=True)  13.6 us
    all_to_all x1, starting transfers between devices, shards(): lax.all_to_all(packed, DEPTH, split_axis=0, concat_axis=0, tiled=True)  9.39 us
    ppermute x8, starting transfers between devices, swap(): return lax.ppermute(v, (axis, 'c'), pairs)  8.82 us
    ppermute x8, waiting for transfers between devices, swap(): return lax.ppermute(v, (axis, 'c'), pairs)  8.15 us
    all_to_all x1, starting transfers between devices, shards(): lax.all_to_all(jnp.broadcast_to(looked, (4,) + looked.shape), GRP, split_...  6.77 us
    unnamed x42, local copies, waits for them, and re-layouts  5.87 us
  transfers between devices with their start and end apart: 22, of which 8 were waited for; matrix products, arithmetic and copies ran while one was open for 6% of the time, Pallas kernels for 24%

profile of v4, /device:TPU:1, one launch (start us, length us, event | category | flops | bytes accessed | tf_op | source)
XLA Modules:
  0.0 157.1 jit_solution(1677333316985418611)
XLA Ops:
  0.6 0.9 stack_reshape.6
  1.5 0.9 stack_reshape.7
  2.4 1.4 reshape.153
  3.9 0.9 maximum_maximum_fusion
  4.9 5.0 %all-to-all-start.1 = ((bf16[4,128,640]{2,1,0:T(8,128)(2,1)}), bf16[4,128,640]{2,1,0:T(8,128)(2,1)S(1)}, u32[]{:S(2)}, u32[]{:S(2)}) async-start(bf16[4,128,640]{2,1,0:T(8,128)(2,1)} %bitcast.17), calls=%async_computation.1 | async-start | bytes 1310720 | tf_op jit(solution)/shard_map/all_to_all | solution.py:331
  10.4 0.8 fusion
  11.7 3.5 %gather_fusion = bf16[256,128]{1,0:T(8,128)(2,1)S(1)} fusion(bf16[16384,128]{1,0:T(8,128)(2,1)} %param.19, s32[1024]{0:T(1024)S(1)} %pad_clamp_fusion), kind=kCustom, calls=%fused_computation | custom fusion | bytes 132096 | tf_op jit(solution)/shard_map/gather | solution.py:374
  15.2 1.9 %pack.1 = bf16[8,112,256]{2,1,0:T(8,128)(2,1)} custom-call(bf16[32,1024]{1,0:T(8,128)(2,1)} %old_k.1, bf16[32,1024]{1,0:T(8,128)(2,1)} %old_v.1, bf16[16,1024]{1,0:T(8,128)(2,1)} %new_k.1, bf16[16,1024]{1,0:T(8,128)(2,1)} %new_v.1, bf16[16,8192]{1,0:T(8,128)(2,1)} %q.1), custom_call_target="tpu_custom_call" | custom-call | tf_op jit(solution)/shard_map/pack/pallas_call | solution.py:39
  17.1 1.5 all-to-all-done.1.weights
  18.6 9.4 %all-to-all-start = ((bf16[8,112,256]{2,1,0:T(8,128)(2,1)}), bf16[8,112,256]{2,1,0:T(8,128)(2,1)S(1)}, u32[]{:S(2)}, u32[]{:S(2)}) async-start(bf16[8,112,256]{2,1,0:T(8,128)(2,1)} %pack.1), calls=%async_computation | async-start | bytes 917504 | tf_op jit(solution)/shard_map/all_to_all | solution.py:319
  28.1 13.6 %all-to-all-done.refs_3_ = bf16[8,112,256]{2,1,0:T(8,128)(2,1)S(1)} async-done(((bf16[8,112,256]{2,1,0:T(8,128)(2,1)}), bf16[8,112,256]{2,1,0:T(8,128)(2,1)S(1)}, u32[]{:S(2)}, u32[]{:S(2)}) %all-to-all-start) | async-done | bytes 458784 | tf_op jit(solution)/shard_map/all_to_all | solution.py:319
  41.6 0.8 broadcast_in_dim.13
  42.5 6.8 %all-to-all-start.2 = ((bf16[4,256,128]{2,1,0:T(8,128)(2,1)}), bf16[4,256,128]{2,1,0:T(8,128)(2,1)S(1)}, u32[]{:S(2)}, u32[]{:S(2)}) async-start(bf16[4,256,128]{2,1,0:T(8,128)(2,1)} %broadcast_in_dim.13), calls=%async_computation.2 | async-start | bytes 524288 | tf_op jit(solution)/shard_map/all_to_all | solution.py:375
  49.2 2.8 %collective-permute-start.3 = (bf16[1,4,48,256]{3,2,1,0:T(8,128)(2,1)S(1)}, bf16[1,4,48,256]{3,2,1,0:T(8,128)(2,1)S(1)}, u32[]{:S(2)}, u32[]{:S(2)}) collective-permute-start(bf16[1,4,48,256]{3,2,1,0:T(8,128)(2,1)S(1)} %get-tuple-element.26), channel_id=1, source_target_pairs={{0,4},{1,13},{4,0},{5,9},{8,12},{9,5},{12,8},{13,1},{2,6},{3,15},{... | collective-permute-start | bytes 294920 | tf_op jit(solution)/shard_map/ppermute | solution.py:339
  52.1 1.0 collective-permute-start.1
  53.1 1.0 collective-permute-done.3
  54.5 2.4 %collective-permute-done.1 = bf16[1,4,48,256]{3,2,1,0:T(8,128)(2,1)S(1)} collective-permute-done((bf16[1,4,48,256]{3,2,1,0:T(8,128)(2,1)S(1)}, bf16[1,4,48,256]{3,2,1,0:T(8,128)(2,1)S(1)}, u32[]{:S(2)}, u32[]{:S(2)}) %collective-permute-start.1) | collective-permute-done | bytes 98336 | tf_op jit(solution)/shard_map/ppermute | solution.py:339
  57.0 4.8 %collective-permute-done.2 = bf16[2,4,48,256]{3,2,1,0:T(8,128)(2,1)S(1)} collective-permute-done((bf16[2,4,48,256]{3,2,1,0:T(8,128)(2,1)S(1)}, bf16[2,4,48,256]{3,2,1,0:T(8,128)(2,1)S(1)}, u32[]{:S(2)}, u32[]{:S(2)}) %collective-permute-start.2) | collective-permute-done | bytes 196640 | tf_op jit(solution)/shard_map/ppermute | solution.py:339
  62.0 1.0 collective-permute-start.6
  63.0 0.8 reshape.150.refs_1_
  64.2 0.7 reshape.167.parent
  65.8 1.9 %hidden.1 = bf16[4,256,128]{2,1,0:T(8,128)(2,1)} custom-call(s32[256,1]{1,0:T(8,128)} %get-tuple-element.29.owner, bf16[4,256,128]{2,1,0:T(8,128)(2,1)} %copy-done.8), custom_call_target="tpu_custom_call" | custom-call | tf_op jit(solution)/shard_map/hidden/pallas_call | solution.py:39
  67.7 3.4 %all-to-all-start.3 = ((bf16[4,256,128]{2,1,0:T(8,128)(2,1)}), bf16[4,256,128]{2,1,0:T(8,128)(2,1)S(1)}, u32[]{:S(2)}, u32[]{:S(2)}) async-start(bf16[4,256,128]{2,1,0:T(8,128)(2,1)} %hidden.1), calls=%async_computation.3 | async-start | bytes 524288 | tf_op jit(solution)/shard_map/all_to_all | solution.py:385
  71.2 2.1 %collective-permute-start = (bf16[8,64,256]{2,1,0:T(8,128)(2,1)S(1)}, bf16[8,64,256]{2,1,0:T(8,128)(2,1)}, u32[]{:S(2)}, u32[]{:S(2)}) collective-permute-start(bf16[8,64,256]{2,1,0:T(8,128)(2,1)S(1)} %slice.117), channel_id=1, source_target_pairs={{0,1},{1,0},{2,3},{3,2},{4,5},{5,4},{6,7},{7,6},{8,9},{9,8},{10,11... | collective-permute-start | bytes 786440 | tf_op jit(solution)/shard_map/ppermute | solution.py:349
  73.3 1.0 pad_maximum_fusion
  74.3 1.6 %collective-permute-start.7 = (bf16[8,4,48,256]{3,2,1,0:T(8,128)(2,1)}, bf16[8,4,48,256]{3,2,1,0:T(8,128)(2,1)}, u32[]{:S(2)}, u32[]{:S(2)}) collective-permute-start(bf16[8,4,48,256]{3,2,1,0:T(8,128)(2,1)} %pad_maximum_fusion), channel_id=1, source_target_pairs={{0,12},{1,5},{4,8},{5,1},{8,4},{9,13},{12,0},{13,9},{2,14},{3,7},{... | collective-permute-start | bytes 2359304 | tf_op jit(solution)/shard_map/ppermute | solution.py:339
  76.1 1.8 %collective-permute-start.8 = (bf16[8,4,48,256]{3,2,1,0:T(8,128)(2,1)S(1)}, bf16[8,4,48,256]{3,2,1,0:T(8,128)(2,1)S(1)}, u32[]{:S(2)}, u32[]{:S(2)}) collective-permute-start(bf16[8,4,48,256]{3,2,1,0:T(8,128)(2,1)S(1)} %pad_maximum_fusion.1), channel_id=1, source_target_pairs={{0,48},{1,17},{16,32},{17,1},{32,16},{33,49},{48,0},{49,33},{2,50}... | collective-permute-start | bytes 2359304 | tf_op jit(solution)/shard_map/ppermute | solution.py:339
  79.8 3.0 %project.1 = f32[16,88,128]{2,1,0:T(8,128)} custom-call(s32[128,1]{1,0:T(8,128)} %reshape.167.parent, s32[1,128]{1,0:T(1,128)} %constant.96.clone.beam_id, bf16[4,256,128]{2,1,0:T(8,128)(2,1)} %copy-done.7, bf16[4,128,640]{2,1,0:T(8,128)(2,1)} %copy-done.1), custom_call_target="tpu_custom_call" | custom-call | tf_op jit(solution)/shard_map/project/pallas_call | solution.py:39
  82.8 3.8 %all-to-all-start.4 = ((f32[16,88,128]{2,1,0:T(8,128)}), f32[16,88,128]{2,1,0:T(8,128)S(1)}, u32[]{:S(2)}, u32[]{:S(2)}) async-start(f32[16,88,128]{2,1,0:T(8,128)} %project.1), calls=%async_computation.4 | async-start | bytes 1441792 | tf_op jit(solution)/shard_map/all_to_all | solution.py:400
  86.6 6.4 %attend_near.1 = (f32[1040,128]{1,0:T(8,128)}, f32[1040,128]{1,0:T(8,128)}) custom-call(s32[4]{0:T(128)} %pad_add_fusion.1.refs_0_.core, s32[32,128]{1,0:T(8,128)} %reshape.150.refs_1_, s32[8,256]{1,0:T(8,128)} %pad_add_fusion.refs_2_, bf16[8,112,256]{2,1,0:T(8,128)(2,1)} %copy-done.2, bf16[8,64,256]{2,1,0:T(8,128)(2,1)} %collective-permute-done.refs_4_, ...), custom_call_target="tpu_custom_call" | custom-call | flops 3221225472 | bytes 786432 | tf_op jit(solution)/shard_map/attend_near/pallas_call | solution.py:39
  92.9 7.1 %attend_far.1 = (f32[1040,128]{1,0:T(8,128)}, f32[1040,128]{1,0:T(8,128)}) custom-call(s32[4]{0:T(128)} %pad_add_fusion.1.refs_0_.core, s32[32,128]{1,0:T(8,128)} %reshape.150.refs_1_, s32[8,256]{1,0:T(8,128)} %pad_add_fusion.refs_2_, bf16[8,112,256]{2,1,0:T(8,128)(2,1)} %copy-done.2, bf16[8,64,256]{2,1,0:T(8,128)(2,1)} %collective-permute-done.refs_4_, ...), custom_call_target="tpu_custom_call" | custom-call | flops 3221225472 | bytes 786432 | tf_op jit(solution)/shard_map/attend_far/pallas_call | solution.py:39
  100.0 0.9 copy-done.9
  100.9 11.1 %attend_rest.1 = (f32[1040,128]{1,0:T(8,128)}, f32[1040,128]{1,0:T(8,128)}) custom-call(s32[4]{0:T(128)} %pad_add_fusion.1.refs_0_.core, s32[32,128]{1,0:T(8,128)} %reshape.150.refs_1_, s32[8,256]{1,0:T(8,128)} %pad_add_fusion.refs_2_, bf16[8,112,256]{2,1,0:T(8,128)(2,1)} %copy-done.2, bf16[8,64,256]{2,1,0:T(8,128)(2,1)} %collective-permute-done.refs_4_, ...), custom_call_target="tpu_custom_call" | custom-call | flops 6442450944 | bytes 1572864 | tf_op jit(solution)/shard_map/attend_rest/pallas_call | solution.py:39
  112.0 1.8 %collective-permute-start.9 = (f32[1040,128]{1,0:T(8,128)}, f32[1040,128]{1,0:T(8,128)S(1)}, u32[]{:S(2)}, u32[]{:S(2)}) collective-permute-start(f32[1040,128]{1,0:T(8,128)} %get-tuple-element.20), channel_id=1, source_target_pairs={{0,1},{1,0},{2,3},{3,2},{4,5},{5,4},{6,7},{7,6},{8,9},{9,8},{10,11... | collective-permute-start | bytes 1597448 | tf_op jit(solution)/shard_map/ppermute | solution.py:428
  113.8 0.9 copy-done
  114.7 1.8 %sum.1 = f32[88,128]{1,0:T(8,128)} custom-call(f32[16,88,128]{2,1,0:T(8,128)} %copy-done), custom_call_target="tpu_custom_call" | custom-call | tf_op jit(solution)/shard_map/sum/pallas_call | solution.py:39
  116.5 2.3 %collective-permute-start.11 = (f32[88,128]{1,0:T(8,128)}, f32[88,128]{1,0:T(8,128)S(1)}, u32[]{:S(2)}, u32[]{:S(2)}) collective-permute-start(f32[88,128]{1,0:T(8,128)} %sum.1), channel_id=1, source_target_pairs={{0,1},{1,65},{2,3},{3,67},{16,0},{17,64},{18,2},{19,66},{32,129},{... | collective-permute-start | bytes 135176 | tf_op jit(solution)/shard_map/ppermute | solution.py:408
  118.7 2.0 %collective-permute-start.10 = (f32[88,128]{1,0:T(8,128)}, f32[88,128]{1,0:T(8,128)S(1)}, u32[]{:S(2)}, u32[]{:S(2)}) collective-permute-start(f32[88,128]{1,0:T(8,128)} %sum.1), channel_id=1, source_target_pairs={{0,0},{1,64},{2,2},{3,66},{16,1},{17,65},{18,3},{19,67},{32,128},{... | collective-permute-start | bytes 135176 | tf_op jit(solution)/shard_map/ppermute | solution.py:408
  120.7 3.6 %collective-permute-done.10.mine = f32[88,128]{1,0:T(8,128)S(1)} collective-permute-done((f32[88,128]{1,0:T(8,128)}, f32[88,128]{1,0:T(8,128)S(1)}, u32[]{:S(2)}, u32[]{:S(2)}) %collective-permute-start.10) | collective-permute-done | bytes 45088 | tf_op jit(solution)/shard_map/ppermute | solution.py:408
  124.9 3.9 %decode.1.beams_keep = f32[136,128]{1,0:T(8,128)} custom-call(s32[4]{0:T(128)} %pad_add_fusion.1.refs_0_.core, f32[88,128]{1,0:T(8,128)} %copy-done.17, f32[88,128]{1,0:T(8,128)} %copy-done.16, bf16[4,4,48,256]{3,2,1,0:T(8,128)(2,1)} %copy-done.3, bf16[4,4,48,256]{3,2,1,0:T(8,128)(2,1)} %copy-done.4, bf16[4,4,48,256]{3,2,1,0:T(8,128)(2,1)} %copy-done.5, ...), custom_call_target="tpu_custom_call" | custom-call | flops 805306368 | bytes 3145728 | tf_op jit(solution)/shard_map/decode/pallas_call | solution.py:39
  128.8 1.5 collective-permute-done.12.beams_got
  131.1 2.6 %merge.1 = (bf16[32,1152]{1,0:T(8,128)(2,1)}, bf16[32,1152]{1,0:T(8,128)(2,1)}, bf16[32,1152]{1,0:T(8,128)(2,1)}, bf16[32,1152]{1,0:T(8,128)(2,1)}) custom-call(s32[4]{0:T(128)} %pad_add_fusion.1.refs_0_.core, f32[1040,128]{1,0:T(8,128)} %get-tuple-element.19.keep, f32[1040,128]{1,0:T(8,128)} %copy-done.10, f32[136,128]{1,0:T(8,128)} %decode.1.beams_keep, ...), custom_call_target="tpu_custom_call" | custom-call | tf_op jit(solution)/shard_map/merge/pallas_call | solution.py:39
  133.7 4.0 %collective-permute-start.13 = (bf16[32,1152]{1,0:T(8,128)(2,1)}, bf16[32,1152]{1,0:T(8,128)(2,1)S(1)}, u32[]{:S(2)}, u32[]{:S(2)}) collective-permute-start(bf16[32,1152]{1,0:T(8,128)(2,1)} %get-tuple-element.22), channel_id=1, source_target_pairs={{0,0},{1,64},{2,2},{3,66},{64,1},{65,65},{66,3},{67,67},{128,128},... | collective-permute-start | bytes 221192 | tf_op jit(solution)/shard_map/ppermute | solution.py:457
  137.7 8.2 %collective-permute-start.14 = (bf16[32,1152]{1,0:T(8,128)(2,1)}, bf16[32,1152]{1,0:T(8,128)(2,1)S(1)}, u32[]{:S(2)}, u32[]{:S(2)}) collective-permute-start(bf16[32,1152]{1,0:T(8,128)(2,1)} %get-tuple-element.23), channel_id=1, source_target_pairs={{0,64},{1,128},{2,66},{3,130},{64,65},{65,129},{66,67},{67,131},{1... | collective-permute-start | bytes 221192 | tf_op jit(solution)/shard_map/ppermute | solution.py:457
  145.9 0.9 collective-permute-start.15
  146.8 2.7 %collective-permute-start.16 = (bf16[32,1152]{1,0:T(8,128)(2,1)}, bf16[32,1152]{1,0:T(8,128)(2,1)S(1)}, u32[]{:S(2)}, u32[]{:S(2)}) collective-permute-start(bf16[32,1152]{1,0:T(8,128)(2,1)} %get-tuple-element.25), channel_id=1, source_target_pairs={{0,192},{1,0},{2,194},{3,2},{64,193},{65,1},{66,195},{67,3},{128,6... | collective-permute-start | bytes 221192 | tf_op jit(solution)/shard_map/ppermute | solution.py:457
  149.5 4.6 %collective-permute-done.15.refs_2_ = bf16[32,1152]{1,0:T(8,128)(2,1)S(1)} collective-permute-done((bf16[32,1152]{1,0:T(8,128)(2,1)}, bf16[32,1152]{1,0:T(8,128)(2,1)S(1)}, u32[]{:S(2)}, u32[]{:S(2)}) %collective-permute-start.15) | collective-permute-done | bytes 73760 | tf_op jit(solution)/shard_map/ppermute | solution.py:457
  155.3 1.8 %place.1 = (bf16[64,2048]{1,0:T(8,128)(2,1)}, bf16[2,2,2048]{2,1,0:T(2,128)(2,1)}) custom-call(s32[4]{0:T(128)} %pad_add_fusion.1.refs_0_.core, bf16[32,1152]{1,0:T(8,128)(2,1)} %copy-done.11, bf16[32,1152]{1,0:T(8,128)(2,1)} %copy-done.12, bf16[32,1152]{1,0:T(8,128)(2,1)} %copy-done.13, bf16[32,1152]{1,0:T(8,128)(2,1)} %copy-done.14), custom_call_target="tpu_custom_call" | custom-call | tf_op jit(solution)/shard_map/place/pallas_call | solution.py:39
  (96 shorter events, 8.1 us)
Async XLA Ops:
  3.9 5.9 %copy-start.19 = (s32[128,2]{0,1:T(2,128)S(1)}, s32[128,2]{0,1:T(2,128)}, u32[]{:S(2)}) copy-start(s32[128,2]{0,1:T(2,128)} %param.23) | copy-start | bytes 3076
  4.9 6.4 %copy-start.18 = (s32[4096]{0:T(1024)S(1)}, s32[4096]{0:T(1024)}, u32[]{:S(2)}) copy-start(s32[4096]{0:T(1024)} %param.16) | copy-start | bytes 49156
  4.9 13.7 %all-to-all-start.1 = ((bf16[4,128,640]{2,1,0:T(8,128)(2,1)}), bf16[4,128,640]{2,1,0:T(8,128)(2,1)S(1)}, u32[]{:S(2)}, u32[]{:S(2)}) async-start(bf16[4,128,640]{2,1,0:T(8,128)(2,1)} %bitcast.17), calls=%async_computation.1 | async-start | bytes 1310720 | tf_op jit(solution)/shard_map/all_to_all | solution.py:331
  18.6 35.5 %copy-start.1 = (bf16[4,128,640]{2,1,0:T(8,128)(2,1)}, bf16[4,128,640]{2,1,0:T(8,128)(2,1)S(1)}, u32[]{:S(2)}) copy-start(bf16[4,128,640]{2,1,0:T(8,128)(2,1)S(1)} %all-to-all-done.1.weights) | copy-start | bytes 1966084
  18.6 23.0 %all-to-all-start = ((bf16[8,112,256]{2,1,0:T(8,128)(2,1)}), bf16[8,112,256]{2,1,0:T(8,128)(2,1)S(1)}, u32[]{:S(2)}, u32[]{:S(2)}) async-start(bf16[8,112,256]{2,1,0:T(8,128)(2,1)} %pack.1), calls=%async_computation | async-start | bytes 917504 | tf_op jit(solution)/shard_map/all_to_all | solution.py:319
  41.6 29.5 %copy-start.2 = (bf16[8,112,256]{2,1,0:T(8,128)(2,1)}, bf16[8,112,256]{2,1,0:T(8,128)(2,1)S(1)}, u32[]{:S(2)}) copy-start(bf16[8,112,256]{2,1,0:T(8,128)(2,1)S(1)} %all-to-all-done.refs_3_) | copy-start | bytes 1376260
  42.5 22.7 %all-to-all-start.2 = ((bf16[4,256,128]{2,1,0:T(8,128)(2,1)}), bf16[4,256,128]{2,1,0:T(8,128)(2,1)S(1)}, u32[]{:S(2)}, u32[]{:S(2)}) async-start(bf16[4,256,128]{2,1,0:T(8,128)(2,1)} %broadcast_in_dim.13), calls=%async_computation.2 | async-start | bytes 524288 | tf_op jit(solution)/shard_map/all_to_all | solution.py:375
  49.2 4.8 %collective-permute-start.3 = (bf16[1,4,48,256]{3,2,1,0:T(8,128)(2,1)S(1)}, bf16[1,4,48,256]{3,2,1,0:T(8,128)(2,1)S(1)}, u32[]{:S(2)}, u32[]{:S(2)}) collective-permute-start(bf16[1,4,48,256]{3,2,1,0:T(8,128)(2,1)S(1)} %get-tuple-element.26), channel_id=1, source_target_pairs={{0,4},{1,13},{4,0},{5,9},{8,12},{9,5},{12,8},{13,1},{2,6},{3,15},{... | collective-permute-start | bytes 294920 | tf_op jit(solution)/shard_map/ppermute | solution.py:339
  52.1 11.7 %copy-start.20 = (s32[128]{0:T(128)S(1)}, s32[128]{0:T(128)}, u32[]{:S(2)}) copy-start(s32[128]{0:T(128)} %param.24) | copy-start | bytes 1540
  52.1 4.8 %collective-permute-start.1 = (bf16[1,4,48,256]{3,2,1,0:T(8,128)(2,1)S(1)}, bf16[1,4,48,256]{3,2,1,0:T(8,128)(2,1)S(1)}, u32[]{:S(2)}, u32[]{:S(2)}) collective-permute-start(bf16[1,4,48,256]{3,2,1,0:T(8,128)(2,1)S(1)} %get-tuple-element.27), channel_id=1, source_target_pairs={{0,16},{1,49},{16,0},{17,33},{32,48},{33,17},{48,32},{49,1},{2,18}... | collective-permute-start | bytes 294920 | tf_op jit(solution)/shard_map/ppermute | solution.py:339
  54.1 7.9 %collective-permute-start.4 = (bf16[2,4,48,256]{3,2,1,0:T(8,128)(2,1)S(1)}, bf16[2,4,48,256]{3,2,1,0:T(8,128)(2,1)S(1)}, u32[]{:S(2)}, u32[]{:S(2)}) collective-permute-start(bf16[2,4,48,256]{3,2,1,0:T(8,128)(2,1)S(1)} %pad_maximum_fusion.5), channel_id=1, source_target_pairs={{0,12},{1,5},{4,8},{5,1},{8,4},{9,13},{12,0},{13,9},{2,14},{3,7},{... | collective-permute-start | bytes 589832 | tf_op jit(solution)/shard_map/ppermute | solution.py:339
  56.9 4.9 %collective-permute-start.2 = (bf16[2,4,48,256]{3,2,1,0:T(8,128)(2,1)S(1)}, bf16[2,4,48,256]{3,2,1,0:T(8,128)(2,1)S(1)}, u32[]{:S(2)}, u32[]{:S(2)}) collective-permute-start(bf16[2,4,48,256]{3,2,1,0:T(8,128)(2,1)S(1)} %pad_maximum_fusion.4), channel_id=1, source_target_pairs={{0,48},{1,17},{16,32},{17,1},{32,16},{33,49},{48,0},{49,33},{2,50}... | collective-permute-start | bytes 589832 | tf_op jit(solution)/shard_map/ppermute | solution.py:339
  61.8 9.4 %copy-start.3 = (bf16[4,4,48,256]{3,2,1,0:T(8,128)(2,1)}, bf16[4,4,48,256]{3,2,1,0:T(8,128)(2,1)S(1)}, u32[]{:S(2)}) copy-start(bf16[4,4,48,256]{3,2,1,0:T(8,128)(2,1)S(1)} %pad_maximum_fusion.2.refs_5_.refs_0_) | copy-start | bytes 1179652
  61.8 11.5 %collective-permute-start.5 = (bf16[4,4,48,256]{3,2,1,0:T(8,128)(2,1)S(1)}, bf16[4,4,48,256]{3,2,1,0:T(8,128)(2,1)S(1)}, u32[]{:S(2)}, u32[]{:S(2)}) collective-permute-start(bf16[4,4,48,256]{3,2,1,0:T(8,128)(2,1)S(1)} %pad_maximum_fusion.2.refs_5_.refs_0_), channel_id=1, source_target_pairs={{0,4},{1,13},{4,0},{5,9},{8,12},{9,5},{12,8},{13,1},{2,6},{3,15},{... | collective-permute-start | bytes 1179656 | tf_op jit(solution)/shard_map/ppermute | solution.py:339
  62.0 12.3 %copy-start.4 = (bf16[4,4,48,256]{3,2,1,0:T(8,128)(2,1)}, bf16[4,4,48,256]{3,2,1,0:T(8,128)(2,1)S(1)}, u32[]{:S(2)}) copy-start(bf16[4,4,48,256]{3,2,1,0:T(8,128)(2,1)S(1)} %pad_maximum_fusion.3.refs_6_.refs_1_) | copy-start | bytes 1179652
  62.0 13.9 %collective-permute-start.6 = (bf16[4,4,48,256]{3,2,1,0:T(8,128)(2,1)S(1)}, bf16[4,4,48,256]{3,2,1,0:T(8,128)(2,1)S(1)}, u32[]{:S(2)}, u32[]{:S(2)}) collective-permute-start(bf16[4,4,48,256]{3,2,1,0:T(8,128)(2,1)S(1)} %pad_maximum_fusion.3.refs_6_.refs_1_), channel_id=1, source_target_pairs={{0,16},{1,49},{16,0},{17,33},{32,48},{33,17},{48,32},{49,1},{2,18}... | collective-permute-start | bytes 1179656 | tf_op jit(solution)/shard_map/ppermute | solution.py:339
  65.1 0.7 copy-start.8
  67.7 11.3 %all-to-all-start.3 = ((bf16[4,256,128]{2,1,0:T(8,128)(2,1)}), bf16[4,256,128]{2,1,0:T(8,128)(2,1)S(1)}, u32[]{:S(2)}, u32[]{:S(2)}) async-start(bf16[4,256,128]{2,1,0:T(8,128)(2,1)} %hidden.1), calls=%async_computation.3 | async-start | bytes 524288 | tf_op jit(solution)/shard_map/all_to_all | solution.py:385
  71.2 15.4 %collective-permute-start = (bf16[8,64,256]{2,1,0:T(8,128)(2,1)S(1)}, bf16[8,64,256]{2,1,0:T(8,128)(2,1)}, u32[]{:S(2)}, u32[]{:S(2)}) collective-permute-start(bf16[8,64,256]{2,1,0:T(8,128)(2,1)S(1)} %slice.117), channel_id=1, source_target_pairs={{0,1},{1,0},{2,3},{3,2},{4,5},{5,4},{6,7},{7,6},{8,9},{9,8},{10,11... | collective-permute-start | bytes 786440 | tf_op jit(solution)/shard_map/ppermute | solution.py:349
  73.3 2.7 %copy-start.5 = (bf16[4,4,48,256]{3,2,1,0:T(8,128)(2,1)}, bf16[4,4,48,256]{3,2,1,0:T(8,128)(2,1)S(1)}, u32[]{:S(2)}) copy-start(bf16[4,4,48,256]{3,2,1,0:T(8,128)(2,1)S(1)} %collective-permute-done.5.refs_7_.refs_2_) | copy-start | bytes 1179652
  74.3 25.7 %collective-permute-start.7 = (bf16[8,4,48,256]{3,2,1,0:T(8,128)(2,1)}, bf16[8,4,48,256]{3,2,1,0:T(8,128)(2,1)}, u32[]{:S(2)}, u32[]{:S(2)}) collective-permute-start(bf16[8,4,48,256]{3,2,1,0:T(8,128)(2,1)} %pad_maximum_fusion), channel_id=1, source_target_pairs={{0,12},{1,5},{4,8},{5,1},{8,4},{9,13},{12,0},{13,9},{2,14},{3,7},{... | collective-permute-start | bytes 2359304 | tf_op jit(solution)/shard_map/ppermute | solution.py:339
  76.0 6.8 %copy-start.6 = (bf16[4,4,48,256]{3,2,1,0:T(8,128)(2,1)}, bf16[4,4,48,256]{3,2,1,0:T(8,128)(2,1)S(1)}, u32[]{:S(2)}) copy-start(bf16[4,4,48,256]{3,2,1,0:T(8,128)(2,1)S(1)} %collective-permute-done.6.refs_8_.refs_3_) | copy-start | bytes 1179652
  76.1 24.0 %collective-permute-start.8 = (bf16[8,4,48,256]{3,2,1,0:T(8,128)(2,1)S(1)}, bf16[8,4,48,256]{3,2,1,0:T(8,128)(2,1)S(1)}, u32[]{:S(2)}, u32[]{:S(2)}) collective-permute-start(bf16[8,4,48,256]{3,2,1,0:T(8,128)(2,1)S(1)} %pad_maximum_fusion.1), channel_id=1, source_target_pairs={{0,48},{1,17},{16,32},{17,1},{32,16},{33,49},{48,0},{49,33},{2,50}... | collective-permute-start | bytes 2359304 | tf_op jit(solution)/shard_map/ppermute | solution.py:339
  79.1 0.7 copy-start.7
  82.8 31.1 %all-to-all-start.4 = ((f32[16,88,128]{2,1,0:T(8,128)}), f32[16,88,128]{2,1,0:T(8,128)S(1)}, u32[]{:S(2)}, u32[]{:S(2)}) async-start(f32[16,88,128]{2,1,0:T(8,128)} %project.1), calls=%async_computation.4 | async-start | bytes 1441792 | tf_op jit(solution)/shard_map/all_to_all | solution.py:400
  100.0 0.9 copy-start.9
  112.0 18.2 %collective-permute-start.9 = (f32[1040,128]{1,0:T(8,128)}, f32[1040,128]{1,0:T(8,128)S(1)}, u32[]{:S(2)}, u32[]{:S(2)}) collective-permute-start(f32[1040,128]{1,0:T(8,128)} %get-tuple-element.20), channel_id=1, source_target_pairs={{0,1},{1,0},{2,3},{3,2},{4,5},{5,4},{6,7},{7,6},{8,9},{9,8},{10,11... | collective-permute-start | bytes 1597448 | tf_op jit(solution)/shard_map/ppermute | solution.py:428
  113.8 0.9 copy-start
  116.5 4.2 %collective-permute-start.11 = (f32[88,128]{1,0:T(8,128)}, f32[88,128]{1,0:T(8,128)S(1)}, u32[]{:S(2)}, u32[]{:S(2)}) collective-permute-start(f32[88,128]{1,0:T(8,128)} %sum.1), channel_id=1, source_target_pairs={{0,1},{1,65},{2,3},{3,67},{16,0},{17,64},{18,2},{19,66},{32,129},{... | collective-permute-start | bytes 135176 | tf_op jit(solution)/shard_map/ppermute | solution.py:408
  118.7 5.6 %collective-permute-start.10 = (f32[88,128]{1,0:T(8,128)}, f32[88,128]{1,0:T(8,128)S(1)}, u32[]{:S(2)}, u32[]{:S(2)}) collective-permute-start(f32[88,128]{1,0:T(8,128)} %sum.1), channel_id=1, source_target_pairs={{0,0},{1,64},{2,2},{3,66},{16,1},{17,65},{18,3},{19,67},{32,128},{... | collective-permute-start | bytes 135176 | tf_op jit(solution)/shard_map/ppermute | solution.py:408
  120.7 3.6 %copy-start.16 = (f32[88,128]{1,0:T(8,128)}, f32[88,128]{1,0:T(8,128)S(1)}, u32[]{:S(2)}) copy-start(f32[88,128]{1,0:T(8,128)S(1)} %collective-permute-done.11.theirs) | copy-start | bytes 135172
  124.3 0.6 copy-start.17
  128.8 1.5 collective-permute-start.12
  130.3 0.6 copy-start.15
  130.3 0.8 copy-start.10
  133.7 15.7 %collective-permute-start.13 = (bf16[32,1152]{1,0:T(8,128)(2,1)}, bf16[32,1152]{1,0:T(8,128)(2,1)S(1)}, u32[]{:S(2)}, u32[]{:S(2)}) collective-permute-start(bf16[32,1152]{1,0:T(8,128)(2,1)} %get-tuple-element.22), channel_id=1, source_target_pairs={{0,0},{1,64},{2,2},{3,66},{64,1},{65,65},{66,3},{67,67},{128,128},... | collective-permute-start | bytes 221192 | tf_op jit(solution)/shard_map/ppermute | solution.py:457
  137.7 11.8 %collective-permute-start.14 = (bf16[32,1152]{1,0:T(8,128)(2,1)}, bf16[32,1152]{1,0:T(8,128)(2,1)S(1)}, u32[]{:S(2)}, u32[]{:S(2)}) collective-permute-start(bf16[32,1152]{1,0:T(8,128)(2,1)} %get-tuple-element.23), channel_id=1, source_target_pairs={{0,64},{1,128},{2,66},{3,130},{64,65},{65,129},{66,67},{67,131},{1... | collective-permute-start | bytes 221192 | tf_op jit(solution)/shard_map/ppermute | solution.py:457
  145.9 8.1 %collective-permute-start.15 = (bf16[32,1152]{1,0:T(8,128)(2,1)}, bf16[32,1152]{1,0:T(8,128)(2,1)S(1)}, u32[]{:S(2)}, u32[]{:S(2)}) collective-permute-start(bf16[32,1152]{1,0:T(8,128)(2,1)} %get-tuple-element.24), channel_id=1, source_target_pairs={{0,128},{1,192},{2,130},{3,194},{64,129},{65,193},{66,131},{67,195... | collective-permute-start | bytes 221192 | tf_op jit(solution)/shard_map/ppermute | solution.py:457
  146.8 7.2 %collective-permute-start.16 = (bf16[32,1152]{1,0:T(8,128)(2,1)}, bf16[32,1152]{1,0:T(8,128)(2,1)S(1)}, u32[]{:S(2)}, u32[]{:S(2)}) collective-permute-start(bf16[32,1152]{1,0:T(8,128)(2,1)} %get-tuple-element.25), channel_id=1, source_target_pairs={{0,192},{1,0},{2,194},{3,2},{64,193},{65,1},{66,195},{67,3},{128,6... | collective-permute-start | bytes 221192 | tf_op jit(solution)/shard_map/ppermute | solution.py:457
  149.5 4.6 %copy-start.11 = (bf16[32,1152]{1,0:T(8,128)(2,1)}, bf16[32,1152]{1,0:T(8,128)(2,1)S(1)}, u32[]{:S(2)}) copy-start(bf16[32,1152]{1,0:T(8,128)(2,1)S(1)} %collective-permute-done.13.refs_0_) | copy-start | bytes 221188
  149.5 4.6 %copy-start.12 = (bf16[32,1152]{1,0:T(8,128)(2,1)}, bf16[32,1152]{1,0:T(8,128)(2,1)S(1)}, u32[]{:S(2)}) copy-start(bf16[32,1152]{1,0:T(8,128)(2,1)S(1)} %collective-permute-done.14.refs_1_) | copy-start | bytes 221188
  154.0 0.6 copy-start.13
  154.7 0.6 copy-start.14
